TPU v7x, 32 devices: a whole 2x2x4 slice. The times are simulated.
32 devices in a mesh: seq: 4 (over y, core), batch: 8 (over z, x).
Axes of the slice: x: 2, y: 2, z: 4, core: 2. Of those that a mesh axis runs over, the one named last changes fastest.
Arguments:
- inputs: bfloat16 [24, 512, 768], P('batch', 'seq'), may hold values from -6 to 6
- cotangent: bfloat16 [24, 512, 768], P('batch', 'seq'), may hold values from -6 to 6
- segment_ids: int32 [24, 512], P('batch', 'seq'), may hold values from 0 to 2, as said below
- bucket_table: int32 [1023], replicated, may hold values from 0 to 31
- position_bias: float32 [32, 12], replicated, may hold values from -4 to 4
- query_weight: bfloat16 [768, 768], replicated, may hold values from -0.109375 to 0.109375
- key_weight: bfloat16 [768, 768], replicated, may hold values from -0.109375 to 0.109375
- value_weight: bfloat16 [768, 768], replicated, may hold values from -0.21875 to 0.21875
- out_weight: bfloat16 [768, 768], replicated, may hold values from -0.875 to 0.875
- hidden_in: bfloat16 [768, 3072], replicated, may hold values from -0.21875 to 0.21875
- hidden_out: bfloat16 [3072, 768], replicated, may hold values from -0.109375 to 0.109375
- gain_first: float32 [768], replicated, may hold values from 0.1 to 1.9
- gain_second: float32 [768], replicated, may hold values from 0.1 to 1.9
- shared: float32 [4, 4, 4], replicated, may hold values from -4 to 4
- down_left: float32 [4, 192], replicated, may hold values from -0.4 to 0.4
- down_right: float32 [4, 12], replicated, may hold values from -2.5 to 2.5
- up_left_vectors: float32 [4, 12], replicated, may hold values from -1.5 to 1.5
- up_right: float32 [4, 192], replicated, may hold values from -0.8 to 0.8
- bias_down: float32 [48], replicated, may hold values from -2.5 to 2.5
- bias_up: float32 [768], replicated, may hold values from -2.5 to 2.5
Outputs:
- output: bfloat16 [24, 512, 768], P('batch', 'seq')
- grad_input: bfloat16 [24, 512, 768], P('batch', 'seq')
- grad_gain_first: float32 [768], replicated
- grad_gain_second: float32 [768], replicated
- grad_shared: float32 [4, 4, 4], replicated
- grad_down_left: float32 [4, 192], replicated
- grad_down_right: float32 [4, 12], replicated
- grad_up_left: float32 [4, 12], replicated
- up_right_gradient: float32 [4, 192], replicated
- grad_bias_down: float32 [48], replicated
- grad_bias_up: float32 [768], replicated
Inputs may be any that keep to these rules, and one draw needn't show every extreme that they name: `segment_ids`: in each row the ids never fall; id 1 runs from a position under 512 // 8 past position 448, ids 0 and 2 fill the two ends, both present.
All inputs are finite; a program needn't handle non-finite values.
Results may differ from a plain program's by a relative error of at most 0.04.
Values may be sent and summed in bfloat16 or wider, within the bound.
No kernel may reach another device: no remote copies, remote signals or barrier semaphores. Data moves between devices by JAX's collectives and lax.ppermute only.
A program may use at most 128 MiB of HBM per device.

v0:
```python
import jax
import jax.numpy as jnp
from jax import lax
from jax.sharding import PartitionSpec as P

epsilon = 1e-06
masked_score = -1e30
highest_precision = lax.Precision.HIGHEST


def passed_along(value, axis, steps):
    count = lax.axis_size(axis)
    pairs = [(source, (source + steps) % count) for source in range(count)]
    return lax.ppermute(value, axis, pairs)


def rms_scale(values, gain):
    return values * lax.rsqrt(jnp.mean(values * values, -1, keepdims=True) + epsilon) * gain


def adapter(branch, shared, down_left, down_right, up_left_vectors, up_right, bias_down, bias_up):
    count_rows = branch.shape[0]
    factors = shared.shape[0]
    blocks = branch.reshape(count_rows, factors, down_left.shape[1])
    projected = jnp.einsum("tab,ib->tia", blocks, down_left, precision=highest_precision)
    mixed = jnp.einsum("tia,iac->tic", projected, shared, precision=highest_precision)
    lowered = jnp.einsum("tic,ij->tcj", mixed, down_right, precision=highest_precision)
    bottleneck = jax.nn.gelu(lowered.reshape(count_rows, -1) + bias_down)
    folded_together = bottleneck.reshape(count_rows, factors, up_left_vectors.shape[1])
    backward_projection = jnp.einsum(
        "orj,gj->ogr", folded_together, up_left_vectors, precision=highest_precision
    )
    remixed = jnp.einsum("tia,iab->tib", backward_projection, shared, precision=highest_precision)
    raised = jnp.einsum("tib,ij->tbj", remixed, up_right, precision=highest_precision)
    return raised.reshape(count_rows, -1) + bias_up


def project(left, right):
    return jnp.dot(left, right, preferred_element_type=jnp.float32)


def project_back(gradient, weight):
    return lax.dot_general(
        gradient, weight, (((1,), (1,)), ((), ())), preferred_element_type=jnp.float32
    )


def toeplitz_bias(offset_bias, first_query, shard_len, row_len):
    table_len = offset_bias.shape[0]
    by_head = jnp.transpose(offset_bias, (1, 0))
    doubled = jnp.concatenate([by_head, by_head], axis=1)
    start = row_len - 1 - first_query
    turned = lax.dynamic_slice_in_dim(doubled, start, table_len, 1)
    tiled = jnp.tile(turned, (1, shard_len))[:, : shard_len * (table_len - 1)]
    skewed = tiled.reshape(by_head.shape[0], shard_len, table_len - 1)
    return skewed[:, :, :row_len]


def score_block(query_heads, key_piece, query_segs, key_segs, first_key, bias_rows):
    row_count, key_count = (key_piece.shape[0], key_piece.shape[1])
    head_count = bias_rows.shape[0]
    key_heads = key_piece.reshape(row_count, key_count, head_count, -1)
    raw_scores = jnp.einsum(
        "rqhe,rkhe->rhqk", query_heads, key_heads, preferred_element_type=jnp.float32
    )
    bias_block = lax.dynamic_slice_in_dim(bias_rows, first_key, key_count, 2)
    same_doc = (query_segs[:, :, None] == key_segs[:, None, :])[:, None]
    return (jnp.where(same_doc, raw_scores + bias_block[None], masked_score), same_doc)


def shards(
    inputs,
    cotangent,
    segment_ids,
    bucket_table,
    position_bias,
    query_weight,
    key_weight,
    value_weight,
    out_weight,
    hidden_in,
    hidden_out,
    gain_first,
    gain_second,
    shared,
    down_left,
    down_right,
    up_left_vectors,
    up_right,
    bias_down,
    bias_up,
):
    row_count, shard_len, model_dim = inputs.shape
    bucket_count, head_count = position_bias.shape
    head_size = model_dim // head_count
    seq_parts = lax.axis_size("seq")
    row_len = shard_len * seq_parts
    seq_place = lax.axis_index("seq")
    bucket_hits = (
        bucket_table[:, None] == jnp.arange(bucket_count, dtype=jnp.int32)[None, :]
    ).astype(jnp.float32)
    offset_bias = jnp.dot(bucket_hits, position_bias, precision=highest_precision)
    bias_rows = toeplitz_bias(offset_bias, seq_place * shard_len, shard_len, row_len)
    flat_rows = inputs.astype(jnp.float32).reshape(row_count * shard_len, model_dim)
    normed_one, norm_one_back = jax.vjp(rms_scale, flat_rows, gain_first)
    normed_low = normed_one.astype(jnp.bfloat16)
    query_low = project(normed_low, query_weight).astype(jnp.bfloat16)
    key_rows = (
        project(normed_low, key_weight)
        .astype(jnp.bfloat16)
        .reshape(row_count, shard_len, model_dim)
    )
    value_rows = (
        project(normed_low, value_weight)
        .astype(jnp.bfloat16)
        .reshape(row_count, shard_len, model_dim)
    )
    query_heads = query_low.reshape(row_count, shard_len, head_count, head_size)
    running_max = jnp.full((row_count, head_count, shard_len), masked_score, jnp.float32)
    key_piece = lax.all_gather(key_rows, "seq", axis=1, tiled=True)
    value_piece = lax.all_gather(value_rows, "seq", axis=1, tiled=True)
    seg_piece = lax.all_gather(segment_ids, "seq", axis=1, tiled=True)
    key_count = key_piece.shape[1]
    scores, same_doc = score_block(
        query_heads, key_piece, segment_ids, seg_piece, jnp.int32(0), bias_rows
    )
    new_max = jnp.maximum(running_max, jnp.max(scores, -1))
    probs = jnp.where(same_doc, jnp.exp(scores - new_max[..., None]), 0.0)
    running_sum = jnp.sum(probs, -1)
    value_heads = value_piece.reshape(row_count, key_count, head_count, head_size)
    mixed = jnp.einsum(
        "rhqk,rkhe->rqhe",
        probs.astype(jnp.bfloat16),
        value_heads,
        preferred_element_type=jnp.float32,
    )
    context_sum = mixed
    running_max, running_sum, context_sum = (new_max, running_sum, context_sum)
    log_total = running_max + jnp.log(running_sum)
    context = context_sum / jnp.transpose(running_sum, (0, 2, 1))[..., None]
    context_low = context.astype(jnp.bfloat16).reshape(row_count * shard_len, model_dim)
    hidden_state = flat_rows + project(context_low, out_weight)
    normed_two, norm_two_back = jax.vjp(rms_scale, hidden_state, gain_second)
    pre_gelu = project(normed_two.astype(jnp.bfloat16), hidden_in)
    activated, gelu_back = jax.vjp(jax.nn.gelu, pre_gelu)
    branch = project(activated.astype(jnp.bfloat16), hidden_out)
    adapted, adapter_back = jax.vjp(
        adapter,
        branch,
        shared,
        down_left,
        down_right,
        up_left_vectors,
        up_right,
        bias_down,
        bias_up,
    )
    output = (
        (hidden_state + branch + adapted)
        .astype(jnp.bfloat16)
        .reshape(row_count, shard_len, model_dim)
    )
    upstream = cotangent.astype(jnp.float32).reshape(row_count * shard_len, model_dim)
    pulled = adapter_back(upstream)
    adapter_gradient_tree = pulled[1:]
    adapter_gradient_tree = lax.psum(
        (
            adapter_gradient_tree[0],
            adapter_gradient_tree[1],
            adapter_gradient_tree[2],
            adapter_gradient_tree[3],
            adapter_gradient_tree[4],
            adapter_gradient_tree[5],
            adapter_gradient_tree[6],
        ),
        ("seq", "batch"),
    )
    branch_grad = (upstream + pulled[0]).astype(jnp.bfloat16)
    activated_grad = project_back(branch_grad, hidden_out)
    pre_grad = gelu_back(activated_grad)[0].astype(jnp.bfloat16)
    normed_two_grad = project_back(pre_grad, hidden_in)
    hidden_norm_grad, gain_two_grad = norm_two_back(normed_two_grad)
    gain_two_grad = lax.psum(gain_two_grad, ("seq", "batch"))
    hidden_grad = upstream + hidden_norm_grad
    attention_grad = hidden_grad.astype(jnp.bfloat16)
    context_grad = (
        project_back(attention_grad, out_weight)
        .astype(jnp.bfloat16)
        .reshape(row_count, shard_len, head_count, head_size)
    )
    row_delta = jnp.transpose(jnp.sum(context_grad.astype(jnp.float32) * context, -1), (0, 2, 1))
    query_sum = jnp.zeros((row_count, shard_len, head_count, head_size), jnp.float32)
    key_sum = jnp.zeros((row_count, shard_len, model_dim), jnp.float32)
    value_sum = jnp.zeros((row_count, shard_len, model_dim), jnp.float32)
    carried = (key_rows, value_rows, segment_ids)
    for turn_index in range(seq_parts):
        source_index = (seq_place - turn_index) % seq_parts
        grad_key_piece, grad_value_piece, grad_seg_piece = carried
        grad_key_count = grad_key_piece.shape[1]
        grad_scores, grad_same_doc = score_block(
            query_heads,
            grad_key_piece,
            segment_ids,
            grad_seg_piece,
            source_index * shard_len,
            bias_rows,
        )
        grad_probs = jnp.where(grad_same_doc, jnp.exp(grad_scores - log_total[..., None]), 0.0)
        key_heads = grad_key_piece.reshape(row_count, grad_key_count, head_count, head_size)
        grad_value_heads = grad_value_piece.reshape(
            row_count, grad_key_count, head_count, head_size
        )
        prob_grad = jnp.einsum(
            "rqhe,rkhe->rhqk", context_grad, grad_value_heads, preferred_element_type=jnp.float32
        )
        score_grad = (grad_probs * (prob_grad - row_delta[..., None])).astype(jnp.bfloat16)
        query_part = jnp.einsum(
            "rhqk,rkhe->rqhe", score_grad, key_heads, preferred_element_type=jnp.float32
        )
        key_part = jnp.einsum(
            "rhqk,rqhe->rkhe", score_grad, query_heads, preferred_element_type=jnp.float32
        )
        value_part = jnp.einsum(
            "rhqk,rqhe->rkhe",
            grad_probs.astype(jnp.bfloat16),
            context_grad,
            preferred_element_type=jnp.float32,
        )
        query_part, key_part, value_part = (
            query_part,
            key_part.reshape(row_count, grad_key_count, model_dim),
            value_part.reshape(row_count, grad_key_count, model_dim),
        )
        query_sum = query_sum + query_part
        key_sum = key_sum + key_part
        value_sum = value_sum + value_part
        if turn_index + 1 < seq_parts:
            carried = passed_along((carried[0], carried[1], carried[2]), "seq", 1)
        key_sum, value_sum = (
            passed_along(key_sum.astype(jnp.bfloat16), "seq", 1).astype(key_sum.dtype),
            passed_along(value_sum.astype(jnp.bfloat16), "seq", 1).astype(value_sum.dtype),
        )
    query_grad = query_sum.astype(jnp.bfloat16).reshape(row_count * shard_len, model_dim)
    key_grad = key_sum.astype(jnp.bfloat16).reshape(row_count * shard_len, model_dim)
    value_grad = value_sum.astype(jnp.bfloat16).reshape(row_count * shard_len, model_dim)
    normed_one_grad = (
        project_back(query_grad, query_weight)
        + project_back(key_grad, key_weight)
        + project_back(value_grad, value_weight)
    )
    input_norm_grad, gain_one_grad = norm_one_back(normed_one_grad)
    input_grad = (
        (hidden_grad + input_norm_grad)
        .astype(jnp.bfloat16)
        .reshape(row_count, shard_len, model_dim)
    )
    gain_one_grad = lax.psum(gain_one_grad, ("seq", "batch"))
    return (
        output,
        input_grad,
        gain_one_grad,
        gain_two_grad,
        adapter_gradient_tree[0],
        adapter_gradient_tree[1],
        adapter_gradient_tree[2],
        adapter_gradient_tree[3],
        adapter_gradient_tree[4],
        adapter_gradient_tree[5],
        adapter_gradient_tree[6],
    )


def solution(mesh):
    in_specs = (
        P("batch", "seq", None),
        P("batch", "seq", None),
        P("batch", "seq"),
        P(),
        P(),
        P(),
        P(),
        P(),
        P(),
        P(),
        P(),
        P(),
        P(),
        P(),
        P(),
        P(),
        P(),
        P(),
        P(),
        P(),
    )
    out_specs = (
        P("batch", "seq", None),
        P("batch", "seq", None),
        P(),
        P(),
        P(),
        P(),
        P(),
        P(),
        P(),
        P(),
        P(),
    )
    return jax.shard_map(shards, mesh=mesh, in_specs=in_specs, out_specs=out_specs, check_vma=False)
```

profile of v0, /device:TPU:0, one launch (start us, length us, event | category | flops | bytes accessed | tf_op | source)
XLA Modules:
  0.0 345.9 jit_solution(9261473480175663570)
XLA Ops:
  13.5 2.6 collective-permute-start.2
  20.1 16.5 %all_gather.10 = s32[3,512]{1,0:T(4,128)S(1)} all-gather(s32[3,128]{1,0:T(4,128)S(1)} %copy-done.71), channel_id=1, replica_groups=mesh['seq'=4,'batch'=8] {'seq'}, dimensions={1}, use_global_device_ids=true | all-gather | bytes 7680 | tf_op jit(solution)/shard_map/all_gather | solution.py:122
  39.7 2.9 collective-permute-start.3
  42.6 3.4 collective-permute-start.5
  46.2 3.4 tile.4
  49.6 8.7 %tile.10 = f32[12,130944]{1,0:T(8,128)} reshape(f32[12,128,1023]{2,1,0:T(8,128)} %tile.4) | data formatting | bytes 12570624 | tf_op jit(solution)/shard_map/tile | solution.py:54
  58.3 7.3 %slice.8 = f32[12,130816]{1,0:T(8,128)} slice(f32[12,130944]{1,0:T(8,128)} %tile.10), slice={[0:12], [0:130816]} | slice | bytes 12558336 | tf_op jit(solution)/shard_map/slice | solution.py:54
  65.5 8.7 %reshape.232 = f32[12,128,1022]{2,1,0:T(8,128)} reshape(f32[12,130816]{1,0:T(8,128)} %slice.8) | data formatting | bytes 12558336 | tf_op jit(solution)/shard_map/reshape | solution.py:55
  74.2 4.0 %slice.9 = f32[12,128,512]{2,1,0:T(8,128)} slice(f32[12,128,1022]{2,1,0:T(8,128)} %reshape.232), slice={[0:12], [0:128], [0:512]} | slice | bytes 6291456 | tf_op jit(solution)/shard_map/slice | solution.py:56
  78.4 3.7 %constant_dynamic-slice_fusion = (f32[12,128,128]{2,1,0:T(8,128)}, f32[12,128,128]{2,1,0:T(8,128)}, f32[12,128,128]{2,1,0:T(8,128)}, f32[12,128,128]{2,1,0:T(8,128)}) fusion(f32[12,128,512]{2,1,0:T(8,128)} %slice.9, s32[]{:T(128)S(6)} %select_n.82, s32[]{:T(128)S(6)} %select_n.78, s32[]{:T(128)S(6)} %select_n.74, s32[]{:T(128)S(6)} %select_n.70), kind=kLoop, calls=%fused_computation.172 | loop fusion | bytes 6291472 | tf_op jit(solution)/shard_map/dynamic_slice | solution.py:66
  84.8 2.8 reshape.264
  89.5 2.2 copy.78
  92.3 2.6 copy.102
  97.1 2.3 copy.105
  99.5 2.3 collective-permute-start.8
  105.1 2.3 copy.109
  110.7 4.7 %collective-permute-done.8 = bf16[3,128,768]{2,1,0:T(8,128)(2,1)} collective-permute-done((bf16[3,128,768]{2,1,0:T(8,128)(2,1)}, bf16[3,128,768]{2,1,0:T(8,128)(2,1)}, u32[]{:S(2)}, u32[]{:S(2)}) %collective-permute-start.8) | collective-permute-done | bytes 589856 | tf_op jit(solution)/shard_map/ppermute | solution.py:14
  115.4 2.2 copy.113
  119.5 4.3 %copy.77 = bf16[3,512,768]{1,2,0:T(8,128)(2,1)} copy(bf16[3,512,768]{2,1,0:T(8,128)(2,1)} %all-gather.5.cloned.1.call-done) | data formatting | bytes 4718592 | tf_op jit(solution)/shard_map/all_gather | solution.py:120
  123.9 4.9 %fusion = (f32[3,12,128]{2,1,0:T(8,128)S(1)}, f32[3,12,128,512]{3,2,1,0:T(8,128)S(1)}) fusion(f32[12,128,512]{2,1,0:T(8,128)} %slice.9, pred[3,128,512]{2,1,0:T(8,128)(4,1)S(1)} %copy-done.37, bf16[3,128,12,64]{1,3,2,0:T(8,128)(2,1)S(1)} %copy.78, bf16[3,512,12,64]{1,3,2,0:T(8,128)(2,1)} %bitcast.201), kind=kOutput, calls=%fused_computation.2 | convolution fusion | flops 309063168 | bytes 15747072 | tf_op jit(solution)/shard_map/rqhe,rkhe->rhqk/dot_general | solution.py:63
  128.8 3.2 fusion.1
  133.1 4.3 %copy.75 = bf16[3,512,768]{1,2,0:T(8,128)(2,1)} copy(bf16[3,512,768]{2,1,0:T(8,128)(2,1)} %all-gather.3.cloned.1.call-done) | data formatting | bytes 4718592 | tf_op jit(solution)/shard_map/all_gather | solution.py:121
  137.4 9.1 %fusion.128 = (bf16[3,128,12,64]{1,3,2,0:T(8,128)(2,1)S(1)}, f32[3,128,12,64]{1,3,2,0:T(8,128)}) fusion(f32[3,128,12]{1,2,0:T(8,128)S(1)} %bitcast.236, bf16[3,512,12,64]{1,3,2,0:T(8,128)(2,1)} %bitcast.221, f32[3,12,128,512]{3,2,1,0:T(8,128)} %copy-done.2, f32[3,12,128]{2,1,0:T(8,128)S(1)} %broadcast_maximum_fusion, f32[12,128,512]{2,1,0:T(8,128)} %slice.9, ...), kind=kOutput, calls=%fused_computation.202 | convolution fusion | flops 314376192 | bytes 16945152 | tf_op jit(solution)/shard_map/rhqk,rkhe->rqhe/dot_general | solution.py:131
  148.4 4.8 %fusion.55 = f32[384,3072]{1,0:T(8,128)S(1)} fusion(bf16[768,3072]{1,0:T(8,128)(2,1)} %param.29, f32[384,768]{1,0:T(8,128)S(1)} %get-tuple-element.39, f32[768]{0:T(1024)S(1)} %copy-done.87, f32[384]{0:T(512)S(1)} %fusion.101), kind=kOutput, calls=%fused_computation.106 | convolution fusion | flops 1812824064 | bytes 10621440 | tf_op jit(solution)/shard_map/dot_general | solution.py:39
  153.3 2.2 copy-done.94
  155.5 3.9 %fusion.13 = f32[384,768]{1,0:T(8,128)} fusion(bf16[3072,768]{1,0:T(8,128)(2,1)S(1)} %bitcast.238, f32[384,3072]{1,0:T(8,128)S(1)} %fusion.55), kind=kOutput, calls=%fused_computation.25 | convolution fusion | flops 1822556160 | bytes 10616832 | tf_op jit(solution)/shard_map/dot_general | solution.py:39
  167.5 2.1 fusion.73
  169.6 2.8 copy.93
  172.4 2.2 fusion.34
  174.6 12.5 %multiply_reduce_fusion = (f32[768]{0:T(1024)}, f32[384]{0:T(512)}, f32[384,768]{1,0:T(8,128)}) fusion(f32[384,768]{1,0:T(8,128)} %copy-done.43, f32[384]{0:T(512)} %copy-done.85, f32[768]{0:T(1024)} %param.32, bf16[768,3072]{1,0:T(8,128)(2,1)} %param.29, f32[384,3072]{1,0:T(8,128)} %copy-done.94, bf16[384,768]{1,0:T(8,128)(2,1)} %fusion.34, ...), kind=kOutput, calls=%fused_computation.61 | convolution fusion | flops 3649240064 | bytes 17114112 | tf_op jit(solution)/shard_map/dot_general | solution.py:43
  190.0 2.8 fusion.85
  192.8 2.8 copy.87
  195.6 3.7 %fusion.30 = (f32[384,768]{1,0:T(8,128)S(1)}, bf16[384,768]{1,0:T(8,128)(2,1)}) fusion(bf16[3,128,768]{2,1,0:T(8,128)(2,1)S(1)} %copy-done.10, f32[384,768]{1,0:T(8,128)} %copy-done.43, f32[384,768]{1,0:T(8,128)} %get-tuple-element.40, f32[384]{0:T(512)S(1)} %copy-done.84, f32[768]{0:T(1024)} %param.32, f32[384]{0:T(512)S(1)} %copy-done.86, ...), kind=kLoop, calls=%fused_computation.50 | loop fusion | flops 3244032 | bytes 7087104 | tf_op jit(solution)/shard_map/add | solution.py:184
  202.9 2.2 copy.99
  205.1 2.4 exponential_select_fusion.4
  214.8 2.1 copy.125
  217.0 4.0 %fusion.28 = f32[3,12,64,128]{3,2,1,0:T(8,128)} fusion(bf16[3,128,12,64]{1,3,2,0:T(8,128)(2,1)S(1)} %copy.99, f32[3,12,128,128]{3,2,1,0:T(8,128)} %fusion.133, f32[12,128,128]{2,1,0:T(8,128)} %get-tuple-element.26, f32[3,12,128]{2,1,0:T(8,128)} %log_add_fusion, pred[3,128,128]{2,1,0:T(8,128)(4,1)} %get-tuple-element.32), kind=kOutput, calls=%fused_computation.49 | convolution fusion | flops 78446592 | bytes 4982784 | tf_op jit(solution)/shard_map/rhqk,rqhe->rkhe/dot_general | solution.py:223
  224.6 2.1 copy.117
  228.8 4.0 %fusion.26 = f32[3,12,64,128]{3,2,1,0:T(8,128)} fusion(bf16[3,128,12,64]{1,3,2,0:T(8,128)(2,1)S(1)} %copy.99, f32[3,12,128,128]{3,2,1,0:T(8,128)} %fusion.134, f32[12,128,128]{2,1,0:T(8,128)} %get-tuple-element.25, f32[3,12,128]{2,1,0:T(8,128)} %log_add_fusion, pred[3,128,128]{2,1,0:T(8,128)(4,1)} %get-tuple-element.31), kind=kOutput, calls=%fused_computation.48 | convolution fusion | flops 78446592 | bytes 4982784 | tf_op jit(solution)/shard_map/rhqk,rqhe->rkhe/dot_general | solution.py:223
  245.3 2.7 copy.127
  249.6 2.7 fusion.137
  258.8 2.8 copy.121
  263.1 2.1 add_convert_fusion.4
  265.3 4.2 %collective-permute-done.14 = bf16[3,128,768]{2,1,0:T(8,128)(2,1)} collective-permute-done((bf16[3,128,768]{2,1,0:T(8,128)(2,1)}, bf16[3,128,768]{2,1,0:T(8,128)(2,1)}, u32[]{:S(2)}, u32[]{:S(2)}) %collective-permute-start.14) | collective-permute-done | bytes 589856 | tf_op jit(solution)/shard_map/ppermute | solution.py:14
  286.3 3.0 collective-permute-done.12
  289.3 2.2 convolution_add_fusion.1
  291.5 4.0 %collective-permute-done.16 = bf16[3,128,768]{2,1,0:T(8,128)(2,1)S(1)} collective-permute-done((bf16[3,128,768]{2,1,0:T(8,128)(2,1)}, bf16[3,128,768]{2,1,0:T(8,128)(2,1)S(1)}, u32[]{:S(2)}, u32[]{:S(2)}) %collective-permute-start.16) | collective-permute-done | bytes 589856 | tf_op jit(solution)/shard_map/ppermute | solution.py:14
  298.0 40.8 %all-reduce = (f32[768]{0:T(1024)}, f32[768]{0:T(1024)}, f32[4,4,4]{2,1,0:T(4,128)}, f32[4,192]{1,0:T(4,128)}, f32[4,12]{1,0:T(4,128)}, /*index=5*/f32[4,12]{1,0...) all-reduce(f32[768]{0:T(1024)S(1)} %get-tuple-element.13, ...), channel_id=1, replica_groups=mesh['seq'=4,'batch'=8] {'seq','batch'}, use_global_device_ids=true, to_apply=%region_8.9 | all-reduce | flops 4048 | bytes 32384 | tf_op jit(solution)/shard_map/psum | solution.py:257
  (302 shorter events, 101.1 us)
Async XLA Ops:
  7.2 4.8 %copy-start = (bf16[768,768]{1,0:T(8,128)(2,1)S(1)}, bf16[768,768]{1,0:T(8,128)(2,1)}, u32[]{:S(2)}) copy-start(bf16[768,768]{1,0:T(8,128)(2,1)} %param.27) | copy-start | bytes 3538948
  7.2 112.3 %all-gather.5.cloned.1.call-start = ((), (), s32[]{:S(2)}) async-start(), calls=%async_computation.1 | async-start | bytes 2949120 | tf_op jit(solution)/shard_map/all_gather | solution.py:120
  11.4 4.7 %copy-start.71 = (s32[3,128]{1,0:T(4,128)S(1)}, s32[3,128]{1,0:T(4,128)}, u32[]{:S(2)}) copy-start(s32[3,128]{1,0:T(4,128)} %param.22) | copy-start | bytes 4612
  11.5 4.8 %copy-start.10 = (bf16[3,128,768]{2,1,0:T(8,128)(2,1)S(1)}, bf16[3,128,768]{2,1,0:T(8,128)(2,1)}, u32[]{:S(2)}) copy-start(bf16[3,128,768]{2,1,0:T(8,128)(2,1)} %param.21) | copy-start | bytes 1769476
  11.5 121.6 %all-gather.3.cloned.1.call-start = ((), (), s32[]{:S(2)}) async-start(), calls=%async_computation | async-start | bytes 2949120 | tf_op jit(solution)/shard_map/all_gather | solution.py:121
  11.5 28.1 %collective-permute-start = (bf16[3,128,768]{2,1,0:T(8,128)(2,1)}, bf16[3,128,768]{2,1,0:T(8,128)(2,1)}, u32[]{:S(2)}, u32[]{:S(2)}) collective-permute-start(bf16[3,128,768]{2,1,0:T(8,128)(2,1)} %bitcast.223), channel_id=1, source_target_pairs={{0,8},{8,16},{16,24},{24,0},{1,9},{9,17},{17,25},{25,1},{2,10},{10... | collective-permute-start | bytes 1769480 | tf_op jit(solution)/shard_map/ppermute | solution.py:14
  13.5 29.1 %collective-permute-start.2 = (bf16[3,128,768]{2,1,0:T(8,128)(2,1)}, bf16[3,128,768]{2,1,0:T(8,128)(2,1)}, u32[]{:S(2)}, u32[]{:S(2)}) collective-permute-start(bf16[3,128,768]{2,1,0:T(8,128)(2,1)} %bitcast.2), channel_id=1, source_target_pairs={{0,8},{8,16},{16,24},{24,0},{1,9},{9,17},{17,25},{25,1},{2,10},{10... | collective-permute-start | bytes 1769480 | tf_op jit(solution)/shard_map/ppermute | solution.py:14
  16.2 62.0 %collective-permute-start.1 = (s32[3,128]{1,0:T(4,128)S(1)}, s32[3,128]{1,0:T(4,128)S(1)}, u32[]{:S(2)}, u32[]{:S(2)}) collective-permute-start(s32[3,128]{1,0:T(4,128)S(1)} %copy-done.71), channel_id=1, source_target_pairs={{0,8},{8,16},{16,24},{24,0},{1,9},{9,17},{17,25},{25,1},{2,10},{10... | collective-permute-start | bytes 4616 | tf_op jit(solution)/shard_map/ppermute | solution.py:14
  17.9 21.7 %copy-start.17 = (bf16[384,4,192]{0,2,1:T(8,128)(2,1)}, bf16[384,4,192]{0,2,1:T(8,128)(2,1)S(1)}, u32[]{:S(2)}) copy-start(bf16[384,4,192]{0,2,1:T(8,128)(2,1)S(1)} %copy.88) | copy-start | bytes 1769476
  39.7 59.8 %collective-permute-start.3 = (bf16[3,128,768]{2,1,0:T(8,128)(2,1)}, bf16[3,128,768]{2,1,0:T(8,128)(2,1)}, u32[]{:S(2)}, u32[]{:S(2)}) collective-permute-start(bf16[3,128,768]{2,1,0:T(8,128)(2,1)} %collective-permute-done), channel_id=1, source_target_pairs={{0,8},{8,16},{16,24},{24,0},{1,9},{9,17},{17,25},{25,1},{2,10},{10... | collective-permute-start | bytes 1769480 | tf_op jit(solution)/shard_map/ppermute | solution.py:14
  42.6 56.9 %collective-permute-start.5 = (bf16[3,128,768]{2,1,0:T(8,128)(2,1)}, bf16[3,128,768]{2,1,0:T(8,128)(2,1)}, u32[]{:S(2)}, u32[]{:S(2)}) collective-permute-start(bf16[3,128,768]{2,1,0:T(8,128)(2,1)} %collective-permute-done.2), channel_id=1, source_target_pairs={{0,8},{8,16},{16,24},{24,0},{1,9},{9,17},{17,25},{25,1},{2,10},{10... | collective-permute-start | bytes 1769480 | tf_op jit(solution)/shard_map/ppermute | solution.py:14
  78.2 4.7 %copy-start.35 = (bf16[384,768]{1,0:T(8,128)(2,1)S(1)}, bf16[384,768]{1,0:T(8,128)(2,1)}, u32[]{:S(2)}) copy-start(bf16[384,768]{1,0:T(8,128)(2,1)} %convolution_convert_fusion.3) | copy-start | bytes 1769476
  78.2 3.9 %collective-permute-start.4 = (s32[3,128]{1,0:T(4,128)S(1)}, s32[3,128]{1,0:T(4,128)S(1)}, u32[]{:S(2)}, u32[]{:S(2)}) collective-permute-start(s32[3,128]{1,0:T(4,128)S(1)} %collective-permute-done.1), channel_id=1, source_target_pairs={{0,8},{8,16},{16,24},{24,0},{1,9},{9,17},{17,25},{25,1},{2,10},{10... | collective-permute-start | bytes 4616 | tf_op jit(solution)/shard_map/ppermute | solution.py:14
  82.0 12.8 %collective-permute-start.7 = (s32[3,128]{1,0:T(4,128)S(1)}, s32[3,128]{1,0:T(4,128)S(1)}, u32[]{:S(2)}, u32[]{:S(2)}) collective-permute-start(s32[3,128]{1,0:T(4,128)S(1)} %collective-permute-done.4), channel_id=1, source_target_pairs={{0,8},{8,16},{16,24},{24,0},{1,9},{9,17},{17,25},{25,1},{2,10},{10... | collective-permute-start | bytes 4616 | tf_op jit(solution)/shard_map/ppermute | solution.py:14
  97.1 6.6 %copy-start.13 = (bf16[3,128,768]{1,2,0:T(8,128)(2,1)}, bf16[3,128,768]{1,2,0:T(8,128)(2,1)S(1)}, u32[]{:S(2)}) copy-start(bf16[3,128,768]{1,2,0:T(8,128)(2,1)S(1)} %copy.103) | copy-start | bytes 1769476
  99.5 9.9 %collective-permute-start.6 = (bf16[3,128,768]{2,1,0:T(8,128)(2,1)}, bf16[3,128,768]{2,1,0:T(8,128)(2,1)}, u32[]{:S(2)}, u32[]{:S(2)}) collective-permute-start(bf16[3,128,768]{2,1,0:T(8,128)(2,1)} %collective-permute-done.3), channel_id=1, source_target_pairs={{0,8},{8,16},{16,24},{24,0},{1,9},{9,17},{17,25},{25,1},{2,10},{10... | collective-permute-start | bytes 1769480 | tf_op jit(solution)/shard_map/ppermute | solution.py:14
  99.5 15.9 %collective-permute-start.8 = (bf16[3,128,768]{2,1,0:T(8,128)(2,1)}, bf16[3,128,768]{2,1,0:T(8,128)(2,1)}, u32[]{:S(2)}, u32[]{:S(2)}) collective-permute-start(bf16[3,128,768]{2,1,0:T(8,128)(2,1)} %collective-permute-done.5), channel_id=1, source_target_pairs={{0,8},{8,16},{16,24},{24,0},{1,9},{9,17},{17,25},{25,1},{2,10},{10... | collective-permute-start | bytes 1769480 | tf_op jit(solution)/shard_map/ppermute | solution.py:14
  105.1 4.3 %copy-start.15 = (bf16[3,128,768]{1,2,0:T(8,128)(2,1)}, bf16[3,128,768]{1,2,0:T(8,128)(2,1)S(1)}, u32[]{:S(2)}) copy-start(bf16[3,128,768]{1,2,0:T(8,128)(2,1)S(1)} %copy.107) | copy-start | bytes 1769476
  110.7 8.8 %copy-start.11 = (bf16[3,128,768]{1,2,0:T(8,128)(2,1)}, bf16[3,128,768]{1,2,0:T(8,128)(2,1)S(1)}, u32[]{:S(2)}) copy-start(bf16[3,128,768]{1,2,0:T(8,128)(2,1)S(1)} %copy.111) | copy-start | bytes 1769476
  119.5 4.3 %copy-start.37 = (pred[3,128,512]{2,1,0:T(8,128)(4,1)S(1)}, pred[3,128,512]{2,1,0:T(8,128)(4,1)}, u32[]{:S(2)}) copy-start(pred[3,128,512]{2,1,0:T(8,128)(4,1)} %broadcast_compare_fusion) | copy-start | bytes 589828
  123.9 4.9 %copy-start.1 = (f32[12,128,512]{2,1,0:T(8,128)S(1)}, f32[12,128,512]{2,1,0:T(8,128)}, u32[]{:S(2)}) copy-start(f32[12,128,512]{2,1,0:T(8,128)} %slice.9) | copy-start | bytes 9437188
  137.4 9.6 %copy-start.39 = (bf16[768,768]{1,0:T(8,128)(2,1)S(1)}, bf16[768,768]{1,0:T(8,128)(2,1)}, u32[]{:S(2)}) copy-start(bf16[768,768]{1,0:T(8,128)(2,1)} %param.28) | copy-start | bytes 3538948
  147.6 7.9 %slice-start = ((s8[4718592]{0:T(1024)(128)(4,1)}), s8[524288]{0:T(1024)(128)(4,1)S(1)}, s32[]{:S(2)}) async-start(s8[4718592]{0:T(1024)(128)(4,1)} %bitcast.237), calls=%async_computation.2 | async-start | bytes 1048576
  148.3 4.9 %copy-start.43 = (f32[384,768]{1,0:T(8,128)}, f32[384,768]{1,0:T(8,128)S(1)}, u32[]{:S(2)}) copy-start(f32[384,768]{1,0:T(8,128)S(1)} %get-tuple-element.39) | copy-start | bytes 3538948
  148.3 4.9 %copy-start.83 = (f32[384]{0:T(512)}, f32[384]{0:T(512)S(1)}, u32[]{:S(2)}) copy-start(f32[384]{0:T(512)S(1)} %get-tuple-element.38) | copy-start | bytes 4612
  148.4 4.9 %copy-start.85 = (f32[384]{0:T(512)}, f32[384]{0:T(512)S(1)}, u32[]{:S(2)}) copy-start(f32[384]{0:T(512)S(1)} %fusion.101) | copy-start | bytes 4612
  148.4 7.1 %slice-start.1 = ((s8[4718592]{0:T(1024)(128)(4,1)}), s8[4194304]{0:T(1024)(128)(4,1)S(1)}, s32[]{:S(2)}) async-start(s8[4718592]{0:T(1024)(128)(4,1)} %bitcast.237), calls=%async_computation.3 | async-start | bytes 8388608
  161.0 6.4 %copy-start.76 = (f32[4,192]{1,0:T(4,128)S(1)}, f32[4,192]{1,0:T(4,128)}, u32[]{:S(2)}) copy-start(f32[4,192]{1,0:T(4,128)} %param.34) | copy-start | bytes 9220
  162.5 7.1 %copy-start.69 = (f32[384,4,4]{0,1,2:T(4,128)}, f32[384,4,4]{0,1,2:T(4,128)S(1)}, u32[]{:S(2)}) copy-start(f32[384,4,4]{0,1,2:T(4,128)S(1)} %convolution_bitcast_fusion.5) | copy-start | bytes 73732
  195.6 4.7 %copy-start.40 = (bf16[768,768]{1,0:T(8,128)(2,1)S(1)}, bf16[768,768]{1,0:T(8,128)(2,1)}, u32[]{:S(2)}) copy-start(bf16[768,768]{1,0:T(8,128)(2,1)} %param.28) | copy-start | bytes 3538948
  216.9 36.9 %collective-permute-start.13 = (bf16[3,128,768]{2,1,0:T(8,128)(2,1)}, bf16[3,128,768]{2,1,0:T(8,128)(2,1)}, u32[]{:S(2)}, u32[]{:S(2)}) collective-permute-start(bf16[3,128,768]{2,1,0:T(8,128)(2,1)} %copy.125), channel_id=1, source_target_pairs={{0,8},{8,16},{16,24},{24,0},{1,9},{9,17},{17,25},{25,1},{2,10},{10... | collective-permute-start | bytes 1769480 | tf_op jit(solution)/shard_map/ppermute | solution.py:14
  226.7 25.7 %collective-permute-start.9 = (bf16[3,128,768]{2,1,0:T(8,128)(2,1)}, bf16[3,128,768]{2,1,0:T(8,128)(2,1)}, u32[]{:S(2)}, u32[]{:S(2)}) collective-permute-start(bf16[3,128,768]{2,1,0:T(8,128)(2,1)} %copy.117), channel_id=1, source_target_pairs={{0,8},{8,16},{16,24},{24,0},{1,9},{9,17},{17,25},{25,1},{2,10},{10... | collective-permute-start | bytes 1769480 | tf_op jit(solution)/shard_map/ppermute | solution.py:14
  234.9 5.1 %copy-start.29 = (bf16[3,12,128,128]{3,2,1,0:T(8,128)(2,1)}, bf16[3,12,128,128]{3,2,1,0:T(8,128)(2,1)S(1)}, u32[]{:S(2)}) copy-start(bf16[3,12,128,128]{3,2,1,0:T(8,128)(2,1)S(1)} %multiply_convert_fusion.2) | copy-start | bytes 3538948
  253.7 9.5 %collective-permute-start.10 = (bf16[3,128,768]{2,1,0:T(8,128)(2,1)S(1)}, bf16[3,128,768]{2,1,0:T(8,128)(2,1)}, u32[]{:S(2)}, u32[]{:S(2)}) collective-permute-start(bf16[3,128,768]{2,1,0:T(8,128)(2,1)S(1)} %add_convert_fusion.5), channel_id=1, source_target_pairs={{0,8},{8,16},{16,24},{24,0},{1,9},{9,17},{17,25},{25,1},{2,10},{10... | collective-permute-start | bytes 1769480 | tf_op jit(solution)/shard_map/ppermute | solution.py:14
  255.9 13.6 %collective-permute-start.14 = (bf16[3,128,768]{2,1,0:T(8,128)(2,1)}, bf16[3,128,768]{2,1,0:T(8,128)(2,1)}, u32[]{:S(2)}, u32[]{:S(2)}) collective-permute-start(bf16[3,128,768]{2,1,0:T(8,128)(2,1)} %add_convert_fusion.2), channel_id=1, source_target_pairs={{0,8},{8,16},{16,24},{24,0},{1,9},{9,17},{17,25},{25,1},{2,10},{10... | collective-permute-start | bytes 1769480 | tf_op jit(solution)/shard_map/ppermute | solution.py:14
  263.1 6.4 %copy-start.24 = (f32[3,128,768]{2,1,0:T(8,128)S(1)}, f32[3,128,768]{2,1,0:T(8,128)}, u32[]{:S(2)}) copy-start(f32[3,128,768]{2,1,0:T(8,128)} %copy.129) | copy-start | bytes 3538948
  265.2 6.2 %copy-start.66 = (f32[384,4,12]{0,2,1:T(8,128)S(1)}, f32[384,4,12]{0,2,1:T(8,128)}, u32[]{:S(2)}) copy-start(f32[384,4,12]{0,2,1:T(8,128)} %copy-done.65) | copy-start | bytes 221188
  265.2 6.2 %copy-start.74 = (f32[4,384,4]{1,2,0:T(4,128)S(1)}, f32[4,384,4]{1,2,0:T(4,128)}, u32[]{:S(2)}) copy-start(f32[4,384,4]{1,2,0:T(4,128)} %fusion.82) | copy-start | bytes 73732
  265.2 7.1 %copy-start.20 = (f32[3,12,64,128]{3,2,1,0:T(8,128)S(1)}, f32[3,12,64,128]{3,2,1,0:T(8,128)}, u32[]{:S(2)}) copy-start(f32[3,12,64,128]{3,2,1,0:T(8,128)} %fusion.24) | copy-start | bytes 3538948
  265.2 12.5 %collective-permute-start.11 = (bf16[3,128,768]{2,1,0:T(8,128)(2,1)}, bf16[3,128,768]{2,1,0:T(8,128)(2,1)}, u32[]{:S(2)}, u32[]{:S(2)}) collective-permute-start(bf16[3,128,768]{2,1,0:T(8,128)(2,1)} %add_convert_fusion.4), channel_id=1, source_target_pairs={{0,8},{8,16},{16,24},{24,0},{1,9},{9,17},{17,25},{25,1},{2,10},{10... | collective-permute-start | bytes 1769480 | tf_op jit(solution)/shard_map/ppermute | solution.py:14
  271.4 10.6 %collective-permute-start.15 = (bf16[3,128,768]{2,1,0:T(8,128)(2,1)}, bf16[3,128,768]{2,1,0:T(8,128)(2,1)}, u32[]{:S(2)}, u32[]{:S(2)}) collective-permute-start(bf16[3,128,768]{2,1,0:T(8,128)(2,1)} %add_convert_fusion.1), channel_id=1, source_target_pairs={{0,8},{8,16},{16,24},{24,0},{1,9},{9,17},{17,25},{25,1},{2,10},{10... | collective-permute-start | bytes 1769480 | tf_op jit(solution)/shard_map/ppermute | solution.py:14
  279.7 4.7 %copy-start.51 = (f32[384,4,12]{0,2,1:T(8,128)S(1)}, f32[384,4,12]{0,2,1:T(8,128)}, u32[]{:S(2)}) copy-start(f32[384,4,12]{0,2,1:T(8,128)} %copy-done.50) | copy-start | bytes 221188
  279.7 4.7 %copy-start.68 = (f32[384,4,4]{0,2,1:T(4,128)S(1)}, f32[384,4,4]{0,2,1:T(4,128)}, u32[]{:S(2)}) copy-start(f32[384,4,4]{0,2,1:T(4,128)} %copy-done.67) | copy-start | bytes 73732
  279.7 9.6 %copy-start.28 = (f32[384,768]{1,0:T(8,128)S(1)}, f32[384,768]{1,0:T(8,128)}, u32[]{:S(2)}) copy-start(f32[384,768]{1,0:T(8,128)} %fusion.56) | copy-start | bytes 3538948
  279.7 9.6 %collective-permute-start.12 = (bf16[3,128,768]{2,1,0:T(8,128)(2,1)}, bf16[3,128,768]{2,1,0:T(8,128)(2,1)}, u32[]{:S(2)}, u32[]{:S(2)}) collective-permute-start(bf16[3,128,768]{2,1,0:T(8,128)(2,1)} %add_convert_fusion.3), channel_id=1, source_target_pairs={{0,8},{8,16},{16,24},{24,0},{1,9},{9,17},{17,25},{25,1},{2,10},{10... | collective-permute-start | bytes 1769480 | tf_op jit(solution)/shard_map/ppermute | solution.py:14
  284.1 11.4 %collective-permute-start.16 = (bf16[3,128,768]{2,1,0:T(8,128)(2,1)}, bf16[3,128,768]{2,1,0:T(8,128)(2,1)S(1)}, u32[]{:S(2)}, u32[]{:S(2)}) collective-permute-start(bf16[3,128,768]{2,1,0:T(8,128)(2,1)} %add_convert_fusion), channel_id=1, source_target_pairs={{0,8},{8,16},{16,24},{24,0},{1,9},{9,17},{17,25},{25,1},{2,10},{10... | collective-permute-start | bytes 1769480 | tf_op jit(solution)/shard_map/ppermute | solution.py:14
  289.3 6.2 %copy-start.9 = (bf16[3,128,768]{2,1,0:T(8,128)(2,1)S(1)}, bf16[3,128,768]{2,1,0:T(8,128)(2,1)}, u32[]{:S(2)}) copy-start(bf16[3,128,768]{2,1,0:T(8,128)(2,1)} %param.20) | copy-start | bytes 1769476
  289.3 6.2 %copy-start.70 = (f32[768]{0:T(1024)S(1)}, f32[768]{0:T(1024)}, u32[]{:S(2)}) copy-start(f32[768]{0:T(1024)} %param.31) | copy-start | bytes 9220
  (68 other events, 149.3 us)
Sparse Core Ops, SparseCore 0:
  11.6 30.7 all-gather.4
  43.9 29.8 all-gather.2
where the time goes:
time: 352 us; the launch traced here: 346 us
  local copies, waits for them, and re-layouts  108 us (31%)
  matrix products  103 us (29%)
  blocking collectives  57.3 us (16%)
  other arithmetic  29.1 us (8%)
  waiting for transfers between devices  18 us (5%)
  between operations  15.5 us (4%)
  starting transfers between devices  15.4 us (4%)
    psum x1, blocking collectives, shards(): gain_one_grad = lax.psum(gain_one_grad, ('seq', 'batch'))  40.8 us
    ppermute x17, waiting for transfers between devices, passed_along(): return lax.ppermute(value, axis, pairs)  18 us
    dot_general x5, matrix products, project_back(): lax.dot_general(gradient, weight, (((1,), (1,)), ((), ())), preferred_ele...  18 us
    all_gather x1, blocking collectives, shards(): seg_piece = lax.all_gather(segment_ids, 'seq', axis=1, tiled=True)  16.5 us
    ppermute x17, starting transfers between devices, passed_along(): return lax.ppermute(value, axis, pairs)  15.3 us
    dot_general x6, matrix products, project(): return jnp.dot(left, right, preferred_element_type=jnp.float32)  14.5 us
    dot_general x5, matrix products, score_block(): jnp.einsum('rqhe,rkhe->rhqk', query_heads, key_heads, preferred_element_t...  13 us
    another operation x2, local copies, waits for them, and re-layouts, toeplitz_bias(): tiled = jnp.tile(turned, (1, shard_len))[:, :shard_len * (table_len - 1)]  12.1 us
  transfers between devices with their start and end apart: 19, of which 6 were waited for; matrix products, arithmetic and copies ran while one was open for 43% of the time, Pallas kernels for 0%

commit v1 on v0

v1 whole, which is shorter than its diff:
```python
import functools

import jax
import jax.numpy as jnp
from jax import lax
from jax.experimental import pallas as pl
from jax.experimental.pallas import tpu as pltpu
from jax.sharding import PartitionSpec as P

F32 = jnp.float32
BF16 = jnp.bfloat16
epsilon = 1e-06
masked = -1e30
gelu_a = 0.7978845608028654
gelu_b = 0.044715
MIB = 1024 * 1024


def dot(a, b, precision=None):
    return lax.dot_general(a, b, (((1,), (0,)), ((), ())), precision=precision, preferred_element_type=F32)


def dot_nt(a, b, precision=None):
    return lax.dot_general(a, b, (((1,), (1,)), ((), ())), precision=precision, preferred_element_type=F32)


def dot_tn(a, b, precision=None):
    return lax.dot_general(a, b, (((0,), (0,)), ((), ())), precision=precision, preferred_element_type=F32)


HI = lax.Precision.HIGHEST


def iota(shape, axis):
    return lax.broadcasted_iota(jnp.int32, shape, axis)


def block_of(index, size, count):
    total = jnp.zeros_like(index)
    for k in range(1, count):
        total = total + (index >= k * size).astype(jnp.int32)
    return total


def gelu_pair(v):
    square = v * v
    h = 0.5 + 0.5 * jnp.tanh(v * (gelu_a + gelu_a * gelu_b * square))
    g = v * h
    slope = h + (g - g * h) * (2.0 * gelu_a + 6.0 * gelu_a * gelu_b * square)
    return g, slope


def inverse_rms(x):
    return lax.rsqrt(jnp.mean(x * x, -1, keepdims=True) + epsilon)


def main_kernel(dims, *refs):
    rows, shard, width, heads, hidden, parts, ranks, mid = dims
    names = (
        "own", "sib", "rown", "rsib", "cot", "seg_own", "seg_sib", "seg_rown", "seg_rsib", "table", "bias", "wq",
        "wk", "wv", "wo", "win", "wout", "gain1", "gain2", "shared", "dl", "dr", "ul", "ur", "bd", "bu", "out",
        "own_part", "sib_part", "rsib_part", "rown_part", "hidden_grad", "pack", "xs", "xn", "ks", "vs", "kf", "q", "qt", "e",
        "bias_rows", "ctx", "ctx_low", "rinv", "hid", "hid_low", "gslope", "dctx", "dq", "dkt", "dvt", "cots", "wqv",
        "wkv", "wvv", "wov", "winv", "woutv", "tab", "sh16", "sh16t", "work", "act", "sems",
    )
    n = dict(zip(names, refs, strict=True))
    (own, sib, rown, rsib, cot) = (n[k] for k in ("own", "sib", "rown", "rsib", "cot"))
    xs, xn, ks, vs, kf, q, qt, e = (n[k] for k in ("xs", "xn", "ks", "vs", "kf", "q", "qt", "e"))
    bias_rows, ctx, ctx_low, rinv = (n[k] for k in ("bias_rows", "ctx", "ctx_low", "rinv"))
    hid, hid_low, gslope, dctx, dq, dkt, dvt = (n[k] for k in ("hid", "hid_low", "gslope", "dctx", "dq", "dkt", "dvt"))
    sems, pack, act = n["sems"], n["pack"], n["act"]
    pairs = heads // 2
    lanes = width // pairs
    half = lanes // 2
    keys = shard * parts
    tokens = rows * shard
    place = lax.axis_index("seq")

    copies = []

    def fetch(source, target):
        c = pltpu.make_async_copy(source, target, sems.at[len(copies)])
        c.start()
        copies.append(c)
        return c

    x_copies = [
        fetch(block, xs.at[:, pl.ds(k * shard, shard), :]) for k, block in enumerate((own, sib, rown, rsib))
    ]
    w_copies = {
        k: fetch(n[k], n[k + "v"]) for k in ("wq", "wk", "wv", "wo", "win", "wout")
    }
    cot_copy = fetch(cot, n["cots"])

    hits = (n["table"][...][None, :] == iota((n["bias"].shape[0], n["table"].shape[0]), 0)).astype(F32)
    n["tab"][0:heads, 0 : n["table"].shape[0]] = dot_tn(n["bias"][...], hits, HI)
    for k in range(parts):
        other = jnp.bitwise_xor(place, k)
        start = pl.multiple_of((other - place + parts - 1) * shard, shard)
        for h in range(heads):
            line = n["tab"][h : h + 1, pl.ds(start, 2 * shard)]
            turned = pltpu.roll(
                jnp.broadcast_to(line, (shard, 2 * shard)), shard + 1, 1, stride=1, stride_axis=0
            )
            bias_rows[h // 2, (h % 2) * shard : (h % 2 + 1) * shard, k * shard : (k + 1) * shard] = turned[:, :shard]

    lane = iota((shard, lanes), 1)
    query_feature = []
    for r in range(rows):
        for k, ids in enumerate((n["seg_own"], n["seg_sib"], n["seg_rown"], n["seg_rsib"])):
            line = jnp.broadcast_to(ids[r : r + 1, :].astype(F32), (lanes, shard))
            seg = jnp.transpose(line)
            same = lane.astype(F32) == seg
            kf[r, k * shard : (k + 1) * shard, :] = same.astype(F32).astype(BF16)
            if k == 0:
                n["work"][r, :, :] = jnp.where((lane < 3) & jnp.logical_not(same), masked, 0.0).astype(BF16)

    mixes = adapter_setup(n, ranks, mid, width)

    for k, c in enumerate(x_copies):
        c.wait()
        for r in range(rows):
            x = xs[r, k * shard : (k + 1) * shard, :].astype(F32)
            xn[r, k * shard : (k + 1) * shard, :] = (x * inverse_rms(x) * n["gain1"][...][None, :]).astype(BF16)

    step = 2 * lanes
    for key in ("wq", "wk", "wv"):
        w_copies[key].wait()

    for t in range(width // step):
        cols = slice(t * step, (t + 1) * step)
        for r in range(rows):
            block = xn[r]
            kk = dot(block, n["wkv"][:, cols]).astype(BF16)
            vv = dot(block, n["wvv"][:, cols]).astype(BF16)
            qq = dot(block[:shard], n["wqv"][:, cols]).astype(BF16)
            for s in range(2):
                part = slice(s * lanes, (s + 1) * lanes)
                ks[2 * t + s, r] = kk[:, part]
                vs[2 * t + s, r] = vv[:, part]
                q[2 * t + s, r] = qq[:, part]
                qt[2 * t + s, r] = jnp.transpose(qq[:, part])

    low_half = iota((1, lanes), 1) < half
    low_lane = low_half.astype(F32).astype(BF16)
    high_lane = 1.0 - low_lane
    low_row = (iota((lanes, 1), 0) < half).astype(F32).astype(BF16)
    high_row = 1.0 - low_row
    ones = jnp.ones((keys, lanes), BF16)

    def forward(index):
        r, p = index // pairs, index % pairs
        qq = q[p, r]
        feature = n["work"][r]
        left = jnp.concatenate(
            [
                jnp.concatenate([qq * low_lane, feature], 1),
                jnp.concatenate([qq * high_lane, feature], 1),
            ],
            0,
        )
        right = jnp.concatenate([ks[p, r], kf[r]], 1)
        scores = dot_nt(left, right) + bias_rows[p]
        peak = jnp.max(scores, 1, keepdims=True)
        weights = jnp.exp(scores - peak).astype(BF16)
        e[index] = weights
        both = dot(weights, jnp.concatenate([vs[p, r], ones], 1))
        scale = 1.0 / both[:, lanes:]
        mixed = both[:, :lanes] * scale
        kept = jnp.where(low_half, mixed[:shard], mixed[shard:])
        ctx[p, r] = kept
        ctx_low[p, r] = kept.astype(BF16)
        rinv[p, r] = jnp.where(low_half, scale[:shard], scale[shard:])

    for index in range(rows * pairs):
        forward(index)

    w_copies["wo"].wait()
    for r in range(rows):
        context = jnp.concatenate([ctx_low[p, r] for p in range(pairs)], 1)
        hid[r * shard : (r + 1) * shard, :] = xs[r, :shard, :].astype(F32) + dot(context, n["wov"][...])
    state = hid[...]
    inv2 = inverse_rms(state)
    hat2 = state * inv2
    hid_low[...] = (hat2 * n["gain2"][...][None, :]).astype(BF16)

    w_copies["win"].wait()
    w_copies["wout"].wait()
    chunk = 2 * lanes
    for j in range(hidden // chunk):
        cols = slice(j * chunk, (j + 1) * chunk)
        g, slope = gelu_pair(dot(hid_low[...], n["winv"][:, cols]))
        gslope[:, cols] = slope.astype(BF16)
        act[:, cols] = g.astype(BF16)

    cot_copy.wait()
    branch = dot(act[...], n["woutv"][...])
    branch_low = branch.astype(BF16)
    down_t, up = mixes["down_t"], mixes["up"]
    g, slope = gelu_pair(dot_nt(branch_low, down_t) + n["bd"][...][None, :])
    g_low = g.astype(BF16)
    adapted = dot(g_low, up) + n["bu"][...][None, :]
    result = hid[...] + branch + adapted
    for r in range(rows):
        n["out"][r] = result[r * shard : (r + 1) * shard].astype(BF16)
    up_low = jnp.concatenate([n["cots"][r] for r in range(rows)], 0)
    upstream = up_low.astype(F32)
    gb = dot_nt(up_low, up) * slope
    gb_low = gb.astype(BF16)
    branch_grad = (upstream + dot(gb_low, down_t)).astype(BF16)
    grad_up = dot_tn(g_low, up_low)
    grad_down_t = dot_tn(gb_low, branch_low)
    adapter_grads(n, mixes, grad_up, grad_down_t, ranks, mid, width)
    pack[2:3, :] = jnp.sum(upstream, 0, keepdims=True)
    pack[7:8, 0 : gb.shape[1]] = jnp.sum(gb, 0, keepdims=True)

    n["hid_low"][...] = branch_grad
    for j in range(hidden // chunk):
        cols = slice(j * chunk, (j + 1) * chunk)
        act[:, cols] = (dot_nt(hid_low[...], n["woutv"][cols, :]) * gslope[:, cols].astype(F32)).astype(BF16)
    grad2 = dot_nt(act[...], n["winv"][...])
    state = hid[...]
    inv2 = inverse_rms(state)
    hat2 = state * inv2
    pack[1:2, :] = jnp.sum(grad2 * hat2, 0, keepdims=True)
    c = grad2 * n["gain2"][...][None, :]
    hidden_grad = upstream + inv2 * (c - hat2 * jnp.mean(hat2 * c, -1, keepdims=True))
    n["hidden_grad"][...] = hidden_grad
    hid_low[...] = hidden_grad.astype(BF16)

    for t in range(width // step):
        part = dot_nt(hid_low[...], n["wov"][t * step : (t + 1) * step, :]).astype(BF16)
        for r in range(rows):
            for s in range(2):
                dctx[2 * t + s, r] = part[r * shard : (r + 1) * shard, s * lanes : (s + 1) * lanes]

    def backward(index):
        r, p = index // pairs, index % pairs
        scale = rinv[p, r]
        slope_in = dctx[p, r].astype(F32) * scale
        product = slope_in * ctx[p, r]
        first = jnp.sum(jnp.where(low_half, product, 0.0), 1, keepdims=True)
        second = jnp.sum(jnp.where(low_half, 0.0, product), 1, keepdims=True)
        delta = jnp.concatenate([first, second], 0)
        slope_low = slope_in.astype(BF16)
        slope_t = jnp.transpose(slope_low)
        left = jnp.concatenate([slope_low * low_lane, slope_low * high_lane], 0)
        weights = e[index]
        steep = weights * (dot_nt(left, vs[p, r]) - delta).astype(BF16)
        grad_q = dot(steep, ks[p, r])
        dq[r, p] = jnp.where(low_half, grad_q[:shard], grad_q[shard:]).astype(BF16)
        qq_t = qt[p, r]
        turned_q = jnp.concatenate([qq_t * low_row, qq_t * high_row], 1)
        turned_s = jnp.concatenate([slope_t * low_row, slope_t * high_row], 1)
        dkt[r, p] = dot(turned_q, steep).astype(BF16)
        dvt[r, p] = dot(turned_s, weights).astype(BF16)

    for index in range(rows * pairs):
        backward(index)

    gain_total = jnp.zeros((1, width), F32)
    for r in range(rows):
        key_t = dkt[r].reshape(width, keys)
        value_t = dvt[r].reshape(width, keys)
        part = jnp.transpose(dot(n["wkv"][...], key_t) + dot(n["wvv"][...], value_t))
        grad_q = jnp.concatenate([dq[r, p] for p in range(pairs)], 1)
        own_grad = part[:shard] + dot_nt(grad_q, n["wqv"][...])
        x = xs[r].astype(F32)
        hat = x * inverse_rms(x)
        gain_total = gain_total + jnp.sum(own_grad * hat[:shard], 0, keepdims=True)
        gain_total = gain_total + jnp.sum(part[shard:] * hat[shard:], 0, keepdims=True)
        n["own_part"][r * shard : (r + 1) * shard, :] = own_grad
        n["sib_part"][r] = part[shard : 2 * shard].astype(BF16)
        n["rown_part"][r] = part[2 * shard : 3 * shard].astype(BF16)
        n["rsib_part"][r] = part[3 * shard :].astype(BF16)
    pack[0:1, :] = gain_total


def adapter_setup(n, ranks, mid, width):
    inner, outer = mid // ranks, width // ranks
    square = ranks * ranks
    for i in range(ranks):
        block = n["shared"][i]
        n["sh16"][i * ranks : (i + 1) * ranks, :] = block
        eye = (iota((ranks, ranks), 0) == iota((ranks, ranks), 1)).astype(F32)
        n["sh16t"][i * ranks : (i + 1) * ranks, :] = dot_tn(block, eye, HI)
    spread = (block_of(iota((square, ranks), 0), ranks, ranks) == iota((square, ranks), 1)).astype(F32)
    by_c = (block_of(iota((ranks, mid), 1), inner, ranks) == iota((ranks, mid), 0)).astype(F32)
    column = iota((inner, mid), 1)
    by_j = (column - inner * block_of(column, inner, ranks) == iota((inner, mid), 0)).astype(F32)
    column = iota((outer, width), 1)
    by_b = (column - outer * block_of(column, outer, ranks) == iota((outer, width), 0)).astype(F32)
    line = iota((square, width), 0)
    own_block = (
        line - ranks * block_of(line, ranks, ranks) == block_of(iota((square, width), 1), outer, ranks)
    ).astype(F32)
    shx = dot(n["sh16"][...], by_c, HI)
    shtx = dot(n["sh16t"][...], by_c, HI)
    drx = dot(dot(spread, n["dr"][...], HI), by_j, HI)
    ulx = dot(dot(spread, n["ul"][...], HI), by_j, HI)
    dlx = dot(dot(spread, n["dl"][...], HI), by_b, HI) * own_block
    urx = dot(dot(spread, n["ur"][...], HI), by_b, HI) * own_block
    mx = shx * drx
    nx = shtx * ulx
    return dict(
        spread=spread, by_c=by_c, by_j=by_j, by_b=by_b, own_block=own_block, shx=shx, shtx=shtx, drx=drx, ulx=ulx,
        dlx=dlx, urx=urx, mx=mx, nx=nx,
        down_t=dot_tn(mx, dlx, HI).astype(BF16), up=dot_tn(nx, urx, HI).astype(BF16),
    )


def adapter_grads(n, m, grad_up, grad_down_t, ranks, mid, width):
    inner, outer = mid // ranks, width // ranks
    square = ranks * ranks
    pack = n["pack"]
    pack[3:16, :] = jnp.zeros((13, width), F32)
    p_down = dot_nt(m["dlx"], grad_down_t, HI)
    p_up = dot_nt(m["urx"], grad_up, HI)
    pack[3 : 3 + ranks, 0:outer] = dot_nt(
        dot_tn(m["spread"], dot(m["mx"], grad_down_t, HI) * m["own_block"], HI), m["by_b"], HI
    )
    pack[3 : 3 + ranks, 256 : 256 + outer] = dot_nt(
        dot_tn(m["spread"], dot(m["nx"], grad_up, HI) * m["own_block"], HI), m["by_b"], HI
    )
    pack[3 : 3 + ranks, 512 : 512 + inner] = dot_nt(dot_tn(m["spread"], p_down * m["shx"], HI), m["by_j"], HI)
    pack[3 : 3 + ranks, 640 : 640 + inner] = dot_nt(dot_tn(m["spread"], p_up * m["shtx"], HI), m["by_j"], HI)
    shared_down = dot_nt(p_down * m["drx"], m["by_c"], HI)
    shared_up = dot_nt(p_up * m["ulx"], m["by_c"], HI)
    for i in range(ranks):
        rows = slice(i * ranks, (i + 1) * ranks)
        eye = (iota((ranks, ranks), 0) == iota((ranks, ranks), 1)).astype(F32)
        total = shared_down[rows] + dot_tn(shared_up[rows], eye, HI)
        pack[8 : 8 + ranks, i * 128 : i * 128 + ranks] = total


def last_kernel(dims, own, sib, far, x_ref, gain1, hidden_grad, grad_input):
    rows, shard = dims[0], dims[1]
    for r in range(rows):
        lines = slice(r * shard, (r + 1) * shard)
        grad = own[lines, :] + sib[r].astype(F32) + far[r].astype(F32)
        x = x_ref[r].astype(F32)
        inv = inverse_rms(x)
        hat = x * inv
        c = grad * gain1[...][None, :]
        total = hidden_grad[lines, :] + inv * (c - hat * jnp.mean(hat * c, -1, keepdims=True))
        grad_input[r] = total.astype(BF16)


def unpack_kernel(dims, pack, g1, g2, shared, dl, dr, ul, ur, bd, bu):
    rows, shard, width, heads, hidden, parts, ranks, mid = dims
    inner, outer = mid // ranks, width // ranks
    g1[...] = pack[0]
    g2[...] = pack[1]
    bu[...] = pack[2]
    bd[...] = pack[7, 0:mid]
    dl[...] = pack[3 : 3 + ranks, 0:outer]
    ur[...] = pack[3 : 3 + ranks, 256 : 256 + outer]
    dr[...] = pack[3 : 3 + ranks, 512 : 512 + inner]
    ul[...] = pack[3 : 3 + ranks, 640 : 640 + inner]
    for i in range(ranks):
        shared[i] = pack[8 : 8 + ranks, i * 128 : i * 128 + ranks]


def exchange(value, axis, bit):
    count = lax.axis_size(axis)
    return lax.ppermute(value, axis, [(k, k ^ bit) for k in range(count)])


def shards(
    inputs, cotangent, segment_ids, bucket_table, position_bias, query_weight, key_weight, value_weight, out_weight,
    hidden_in, hidden_out, gain_first, gain_second, shared, down_left, down_right, up_left_vectors, up_right,
    bias_down, bias_up,
):
    rows, shard, width = inputs.shape
    heads = position_bias.shape[1]
    hidden = hidden_in.shape[1]
    parts = lax.axis_size("seq")
    ranks, mid = shared.shape[0], bias_down.shape[0]
    dims = (rows, shard, width, heads, hidden, parts, ranks, mid)
    pairs, tokens, keys = heads // 2, rows * shard, shard * parts
    lanes = width // pairs

    x_far = exchange(inputs, "seq", 2)
    seg_far = exchange(segment_ids, "seq", 2)
    x_sib = exchange(inputs, "seq", 1)
    seg_sib = exchange(segment_ids, "seq", 1)
    x_farsib = exchange(x_far, "seq", 1)
    seg_farsib = exchange(seg_far, "seq", 1)

    any_spec = pl.BlockSpec(memory_space=pl.ANY)
    vmem = pl.BlockSpec(memory_space=pltpu.VMEM)
    scratch = [
        pltpu.VMEM((rows, keys, width), BF16),
        pltpu.VMEM((rows, keys, width), BF16),
        pltpu.VMEM((pairs, rows, keys, lanes), BF16),
        pltpu.VMEM((pairs, rows, keys, lanes), BF16),
        pltpu.VMEM((rows, keys, lanes), BF16),
        pltpu.VMEM((pairs, rows, shard, lanes), BF16),
        pltpu.VMEM((pairs, rows, lanes, shard), BF16),
        pltpu.VMEM((rows * pairs, 2 * shard, keys), BF16),
        pltpu.VMEM((pairs, 2 * shard, keys), F32),
        pltpu.VMEM((pairs, rows, shard, lanes), F32),
        pltpu.VMEM((pairs, rows, shard, lanes), BF16),
        pltpu.VMEM((pairs, rows, shard, lanes), F32),
        pltpu.VMEM((tokens, width), F32),
        pltpu.VMEM((tokens, width), BF16),
        pltpu.VMEM((tokens, hidden), BF16),
        pltpu.VMEM((pairs, rows, shard, lanes), BF16),
        pltpu.VMEM((rows, pairs, shard, lanes), BF16),
        pltpu.VMEM((rows, pairs, lanes, keys), BF16),
        pltpu.VMEM((rows, pairs, lanes, keys), BF16),
        pltpu.VMEM((rows, shard, width), BF16),
        pltpu.VMEM((width, width), BF16),
        pltpu.VMEM((width, width), BF16),
        pltpu.VMEM((width, width), BF16),
        pltpu.VMEM((width, width), BF16),
        pltpu.VMEM((width, hidden), BF16),
        pltpu.VMEM((hidden, width), BF16),
        pltpu.VMEM((16, 2 * keys), F32),
        pltpu.VMEM((ranks * ranks, ranks), F32),
        pltpu.VMEM((ranks * ranks, ranks), F32),
        pltpu.VMEM((rows, shard, lanes), BF16),
        pltpu.VMEM((tokens, hidden), BF16),
        pltpu.SemaphoreType.DMA((11,)),
    ]
    out, own_part, sib_part, rsib_part, rown_part, hidden_grad, pack = pl.pallas_call(
        functools.partial(main_kernel, dims),
        out_shape=[
            jax.ShapeDtypeStruct((rows, shard, width), BF16),
            jax.ShapeDtypeStruct((tokens, width), F32),
            jax.ShapeDtypeStruct((rows, shard, width), BF16),
            jax.ShapeDtypeStruct((rows, shard, width), BF16),
            jax.ShapeDtypeStruct((rows, shard, width), BF16),
            jax.ShapeDtypeStruct((tokens, width), F32),
            jax.ShapeDtypeStruct((16, width), F32),
        ],
        in_specs=[any_spec] * 5 + [vmem] * 6 + [any_spec] * 6 + [vmem] * 9,
        out_specs=[vmem] * 7,
        scratch_shapes=scratch,
        compiler_params=pltpu.CompilerParams(vmem_limit_bytes=60 * MIB),
    )(
        inputs, x_sib, x_far, x_farsib, cotangent, segment_ids, seg_sib, seg_far, seg_farsib,
        bucket_table, position_bias,
        query_weight, key_weight, value_weight, out_weight, hidden_in, hidden_out,
        gain_first, gain_second, shared, down_left, down_right, up_left_vectors, up_right,
        bias_down, bias_up,
    )

    far = exchange(rown_part + exchange(rsib_part, "seq", 1), "seq", 2)
    from_sib = exchange(sib_part, "seq", 1)
    for axis in ("seq", "batch"):
        bit = 1
        while bit < lax.axis_size(axis):
            pack = pack + exchange(pack, axis, bit)
            bit *= 2

    (grad_input,) = pl.pallas_call(
        functools.partial(last_kernel, dims),
        out_shape=[jax.ShapeDtypeStruct((rows, shard, width), BF16)],
        in_specs=[vmem] * 6,
        out_specs=[vmem],
        compiler_params=pltpu.CompilerParams(vmem_limit_bytes=30 * MIB),
    )(own_part, from_sib, far, inputs, gain_first, hidden_grad)

    inner, outer = mid // ranks, width // ranks
    grads = pl.pallas_call(
        functools.partial(unpack_kernel, dims),
        out_shape=[
            jax.ShapeDtypeStruct((width,), F32),
            jax.ShapeDtypeStruct((width,), F32),
            jax.ShapeDtypeStruct((ranks, ranks, ranks), F32),
            jax.ShapeDtypeStruct((ranks, outer), F32),
            jax.ShapeDtypeStruct((ranks, inner), F32),
            jax.ShapeDtypeStruct((ranks, inner), F32),
            jax.ShapeDtypeStruct((ranks, outer), F32),
            jax.ShapeDtypeStruct((mid,), F32),
            jax.ShapeDtypeStruct((width,), F32),
        ],
        in_specs=[vmem],
        out_specs=[vmem] * 9,
    )(pack)
    return (out, grad_input, *grads)


def solution(mesh):
    rows = P("batch", "seq", None)
    in_specs = (rows, rows, P("batch", "seq")) + (P(),) * 17
    out_specs = (rows, rows) + (P(),) * 9
    return jax.shard_map(shards, mesh=mesh, in_specs=in_specs, out_specs=out_specs, check_vma=False)
```

time: 352 us -> 105 us (0.30); the launches traced: 346 us -> 104 us
  local copies, waits for them, and re-layouts: 108 us -> 4.26 us
  matrix products: 103 us -> 0 us
  blocking collectives: 57.3 us -> 0 us
  Pallas kernels: 0 us -> 44.4 us
  other arithmetic: 29.1 us -> 1.98 us
  waiting for transfers between devices: 18 us -> 38.4 us
  between operations: 15.5 us -> 0.78 us
    dot_general x52 -> x0, matrix products: 103 us -> none  [the longest x5 18 us: project_back(): lax.dot_general(gradient, weight, (((1,), (1,)), ((), ())), preferred_ele...]
    pallas_call x0 -> x3, Pallas kernels: none -> 44.4 us  [the longest x1 41.5 us: shards(): pl.pallas_call(functools.partial(main_kernel, dims), out_shape=[jax.Shape...]
    psum x1 -> x0, blocking collectives: 40.8 us -> none  [shards(): gain_one_grad = lax.psum(gain_one_grad, ('seq', 'batch'))]
    reshape x13 -> x0, local copies, waits for them, and re-layouts: 32.8 us -> none  [the longest x1 8.67 us: toeplitz_bias(): skewed = tiled.reshape(by_head.shape[0], shard_len, table_len - 1)]
    another operation x7 -> x0, local copies, waits for them, and re-layouts: 21 us -> none  [the longest x2 12.1 us: toeplitz_bias(): tiled = jnp.tile(turned, (1, shard_len))[:, :shard_len * (table_len - 1)]]
    ppermute x17 -> x14, waiting for transfers between devices: 18 us -> 38.4 us  [exchange(): return lax.ppermute(value, axis, [(k, k ^ bit) for k in range(count)])]
    all_gather x1 -> x0, blocking collectives: 16.5 us -> none  [shards(): seg_piece = lax.all_gather(segment_ids, 'seq', axis=1, tiled=True)]
    convert_element_type x9 -> x0, other arithmetic: 16.1 us -> none  [the longest x3 6.1 us: shards(): value_sum.astype(jnp.bfloat16)]
  transfers between devices with their start and end apart: 19 -> 14, of which waited for: 6 -> 8; matrix products, arithmetic and copies ran while one was open for 43% -> 3% of each run, Pallas kernels for 0% -> 1%
where the time goes in v1:
time: 105 us; the launch traced here: 104 us
  Pallas kernels  44.4 us (42%)
  waiting for transfers between devices  38.4 us (37%)
  starting transfers between devices  14.7 us (14%)
  local copies, waits for them, and re-layouts  4.26 us (4%)
  other arithmetic  1.98 us (2%)
    pallas_call x1, Pallas kernels, shards(): pl.pallas_call(functools.partial(main_kernel, dims), out_shape=[jax.Shape...  41.5 us
    ppermute x14, waiting for transfers between devices, exchange(): return lax.ppermute(value, axis, [(k, k ^ bit) for k in range(count)])  38.4 us
    ppermute x14, starting transfers between devices, exchange(): return lax.ppermute(value, axis, [(k, k ^ bit) for k in range(count)])  14.7 us
    unnamed x23, local copies, waits for them, and re-layouts  4.26 us
  transfers between devices with their start and end apart: 14, of which 8 were waited for; matrix products, arithmetic and copies ran while one was open for 3% of the time, Pallas kernels for 1%

profile of v1, /device:TPU:0, one launch (start us, length us, event | category | flops | bytes accessed | tf_op | source)
XLA Modules:
  0.0 104.4 jit_solution(15978088298722493300)
XLA Ops:
  0.6 3.0 %collective-permute-start.1 = (bf16[3,128,768]{2,1,0:T(8,128)(2,1)}, bf16[3,128,768]{2,1,0:T(8,128)(2,1)S(1)}, u32[]{:S(2)}, u32[]{:S(2)}) collective-permute-start(bf16[3,128,768]{2,1,0:T(8,128)(2,1)} %x_ref.1), channel_id=1, source_target_pairs={{0,16},{8,24},{16,0},{24,8},{1,17},{9,25},{17,1},{25,9},{2,18},{10... | collective-permute-start | bytes 1769480 | tf_op jit(solution)/shard_map/ppermute | solution.py:366
  3.7 0.0 collective-permute-start
  3.7 13.5 %collective-permute-done.1.refs_2_ = bf16[3,128,768]{2,1,0:T(8,128)(2,1)S(1)} collective-permute-done((bf16[3,128,768]{2,1,0:T(8,128)(2,1)}, bf16[3,128,768]{2,1,0:T(8,128)(2,1)S(1)}, u32[]{:S(2)}, u32[]{:S(2)}) %collective-permute-start.1) | collective-permute-done | bytes 589856 | tf_op jit(solution)/shard_map/ppermute | solution.py:366
  17.2 0.0 collective-permute-start.2
  17.2 1.7 %collective-permute-start.4 = (s32[3,128]{1,0:T(4,128)}, s32[3,128]{1,0:T(4,128)S(1)}, u32[]{:S(2)}, u32[]{:S(2)}) collective-permute-start(s32[3,128]{1,0:T(4,128)} %refs_5_.1), channel_id=1, source_target_pairs={{0,16},{8,24},{16,0},{24,8},{1,17},{9,25},{17,1},{25,9},{2,18},{10... | collective-permute-start | bytes 4616 | tf_op jit(solution)/shard_map/ppermute | solution.py:366
  19.0 0.2 collective-permute-start.3
  19.2 1.8 %collective-permute-done.4.refs_7_ = s32[3,128]{1,0:T(4,128)S(1)} collective-permute-done((s32[3,128]{1,0:T(4,128)}, s32[3,128]{1,0:T(4,128)S(1)}, u32[]{:S(2)}, u32[]{:S(2)}) %collective-permute-start.4) | collective-permute-done | bytes 1568 | tf_op jit(solution)/shard_map/ppermute | solution.py:366
  21.0 0.0 collective-permute-start.5
  21.0 1.4 %copy.31.refs_10_ = f32[32,12]{1,0:T(8,128)} copy(f32[32,12]{0,1:T(8,128)} %param.24) | data formatting | bytes 3072 | tf_op args[4]
  22.4 0.0 collective-permute-done.3.refs_6_
  22.4 0.0 collective-permute-done.5.refs_8_
  22.4 0.0 copy-start.10
  22.4 0.0 collective-permute-done.refs_1_
  22.4 0.0 copy-start.5
  22.4 0.0 collective-permute-done.2.refs_3_
  22.5 0.0 copy-done.4
  22.5 0.0 copy-done.8
  22.5 0.5 copy-done.9
  23.0 0.0 copy-done.10
  23.0 0.3 copy-done.5
  23.2 0.8 copy-done.6
  24.1 41.5 %shard_map.275 = (bf16[3,128,768]{2,1,0:T(8,128)(2,1)}, f32[384,768]{1,0:T(8,128)}, bf16[3,128,768]{2,1,0:T(8,128)(2,1)}, bf16[3,128,768]{2,1,0:T(8,128)(2,1)}, ...) custom-call(bf16[3,128,768]{2,1,0:T(8,128)(2,1)} %x_ref.1, bf16[3,128,768]{2,1,0:T(8,128)(2,1)} %copy-done.5, ...), custom_call_target="tpu_custom_call" | custom-call | tf_op jit(solution)/shard_map/pallas_call | solution.py:426
  65.5 0.0 copy-start.7
  65.5 0.6 collective-permute-start.7
  66.2 0.1 collective-permute-start.6
  66.2 1.8 %collective-permute-done.7 = bf16[3,128,768]{2,1,0:T(8,128)(2,1)S(1)} collective-permute-done((bf16[3,128,768]{2,1,0:T(8,128)(2,1)}, bf16[3,128,768]{2,1,0:T(8,128)(2,1)S(1)}, u32[]{:S(2)}, u32[]{:S(2)}) %collective-permute-start.7) | collective-permute-done | bytes 589856 | tf_op jit(solution)/shard_map/ppermute | solution.py:366
  68.0 1.3 %add.18 = bf16[3,128,768]{2,1,0:T(8,128)(2,1)S(1)} add(bf16[3,128,768]{2,1,0:T(8,128)(2,1)} %get-tuple-element.30, bf16[3,128,768]{2,1,0:T(8,128)(2,1)S(1)} %collective-permute-done.7) | non-fusion elementwise | flops 294912 | bytes 1769472 | tf_op jit(solution)/shard_map/add | solution.py:449
  69.3 1.8 %collective-permute-start.8 = (bf16[3,128,768]{2,1,0:T(8,128)(2,1)S(1)}, bf16[3,128,768]{2,1,0:T(8,128)(2,1)S(1)}, u32[]{:S(2)}, u32[]{:S(2)}) collective-permute-start(bf16[3,128,768]{2,1,0:T(8,128)(2,1)S(1)} %add.18), channel_id=1, source_target_pairs={{0,16},{8,24},{16,0},{24,8},{1,17},{9,25},{17,1},{25,9},{2,18},{10... | collective-permute-start | bytes 1769480 | tf_op jit(solution)/shard_map/ppermute | solution.py:366
  71.1 0.0 copy-done.7
  71.1 0.1 collective-permute-start.9
  71.2 1.2 %collective-permute-done.9 = f32[16,768]{1,0:T(8,128)S(1)} collective-permute-done((f32[16,768]{1,0:T(8,128)S(1)}, f32[16,768]{1,0:T(8,128)S(1)}, u32[]{:S(2)}, u32[]{:S(2)}) %collective-permute-start.9) | collective-permute-done | bytes 49184 | tf_op jit(solution)/shard_map/ppermute | solution.py:366
  72.4 0.4 collective-permute-start.10
  72.7 13.3 %collective-permute-done.10 = f32[16,768]{1,0:T(8,128)S(1)} collective-permute-done((f32[16,768]{1,0:T(8,128)S(1)}, f32[16,768]{1,0:T(8,128)S(1)}, u32[]{:S(2)}, u32[]{:S(2)}) %collective-permute-start.10) | collective-permute-done | bytes 49184 | tf_op jit(solution)/shard_map/ppermute | solution.py:366
  86.1 1.8 %collective-permute-start.11 = (f32[16,768]{1,0:T(8,128)S(1)}, f32[16,768]{1,0:T(8,128)S(1)}, u32[]{:S(2)}, u32[]{:S(2)}) collective-permute-start(f32[16,768]{1,0:T(8,128)S(1)} %add.20), channel_id=1, source_target_pairs={{0,1},{1,0},{2,3},{3,2},{4,5},{5,4},{6,7},{7,6},{8,9},{9,8},{10,11... | collective-permute-start | bytes 147464 | tf_op jit(solution)/shard_map/ppermute | solution.py:366
  87.8 2.4 %collective-permute-done.11 = f32[16,768]{1,0:T(8,128)S(1)} collective-permute-done((f32[16,768]{1,0:T(8,128)S(1)}, f32[16,768]{1,0:T(8,128)S(1)}, u32[]{:S(2)}, u32[]{:S(2)}) %collective-permute-start.11) | collective-permute-done | bytes 49184 | tf_op jit(solution)/shard_map/ppermute | solution.py:366
  90.2 1.9 %collective-permute-start.12 = (f32[16,768]{1,0:T(8,128)S(1)}, f32[16,768]{1,0:T(8,128)S(1)}, u32[]{:S(2)}, u32[]{:S(2)}) collective-permute-start(f32[16,768]{1,0:T(8,128)S(1)} %add.21), channel_id=1, source_target_pairs={{0,2},{1,3},{2,0},{3,1},{4,6},{5,7},{6,4},{7,5},{8,10},{9,11},{10,... | collective-permute-start | bytes 147464 | tf_op jit(solution)/shard_map/ppermute | solution.py:366
  92.1 2.3 %collective-permute-done.12 = f32[16,768]{1,0:T(8,128)S(1)} collective-permute-done((f32[16,768]{1,0:T(8,128)S(1)}, f32[16,768]{1,0:T(8,128)S(1)}, u32[]{:S(2)}, u32[]{:S(2)}) %collective-permute-start.12) | collective-permute-done | bytes 49184 | tf_op jit(solution)/shard_map/ppermute | solution.py:366
  94.4 3.1 %collective-permute-start.13 = (f32[16,768]{1,0:T(8,128)S(1)}, f32[16,768]{1,0:T(8,128)S(1)}, u32[]{:S(2)}, u32[]{:S(2)}) collective-permute-start(f32[16,768]{1,0:T(8,128)S(1)} %add.22), channel_id=1, source_target_pairs={{0,4},{1,5},{2,6},{3,7},{4,0},{5,1},{6,2},{7,3},{8,12},{9,13},{10,... | collective-permute-start | bytes 147464 | tf_op jit(solution)/shard_map/ppermute | solution.py:366
  97.5 2.1 %collective-permute-done.13 = f32[16,768]{1,0:T(8,128)S(1)} collective-permute-done((f32[16,768]{1,0:T(8,128)S(1)}, f32[16,768]{1,0:T(8,128)S(1)}, u32[]{:S(2)}, u32[]{:S(2)}) %collective-permute-start.13) | collective-permute-done | bytes 49184 | tf_op jit(solution)/shard_map/ppermute | solution.py:366
  99.5 0.6 add.23.pack
  100.2 1.4 %shard_map.277 = (f32[768]{0:T(1024)}, f32[768]{0:T(1024)}, f32[4,4,4]{2,1,0:T(4,128)}, f32[4,192]{1,0:T(4,128)}, f32[4,12]{1,0:T(4,128)}, /*index=5*/f32[4,12]{...) custom-call(f32[16,768]{1,0:T(8,128)} %add.23.pack), custom_call_target="tpu_custom_call" | custom-call | tf_op jit(solution)/shard_map/pallas_call | solution.py:466
  101.6 0.0 collective-permute-done.6.sib
  101.6 0.0 collective-permute-done.8.far
  101.6 0.0 copy-done
  101.6 0.0 copy-done.1
  101.6 0.0 copy-done.3
  101.7 1.3 %copy-done.2 = f32[384,768]{1,0:T(8,128)S(1)} copy-done((f32[384,768]{1,0:T(8,128)S(1)}, f32[384,768]{1,0:T(8,128)}, u32[]{:S(2)}) %copy-start.2) | copy-done | bytes 1179672
  102.9 1.5 %shard_map.276 = bf16[3,128,768]{2,1,0:T(8,128)(2,1)} custom-call(f32[384,768]{1,0:T(8,128)S(1)} %copy-done.1, bf16[3,128,768]{2,1,0:T(8,128)(2,1)S(1)} %collective-permute-done.6.sib, bf16[3,128,768]{2,1,0:T(8,128)(2,1)S(1)} %collective-permute-done.8.far, bf16[3,128,768]{2,1,0:T(8,128)(2,1)S(1)} %copy-done, f32[768]{0:T(1024)S(1)} %copy-done.3, ...), custom_call_target="tpu_custom_call" | custom-call | tf_op jit(solution)/shard_map/pallas_call | solution.py:457
  (12 shorter events, 0.0 us)
Async XLA Ops:
  0.6 16.6 %collective-permute-start.1 = (bf16[3,128,768]{2,1,0:T(8,128)(2,1)}, bf16[3,128,768]{2,1,0:T(8,128)(2,1)S(1)}, u32[]{:S(2)}, u32[]{:S(2)}) collective-permute-start(bf16[3,128,768]{2,1,0:T(8,128)(2,1)} %x_ref.1), channel_id=1, source_target_pairs={{0,16},{8,24},{16,0},{24,8},{1,17},{9,25},{17,1},{25,9},{2,18},{10... | collective-permute-start | bytes 1769480 | tf_op jit(solution)/shard_map/ppermute | solution.py:366
  3.7 18.7 %collective-permute-start = (bf16[3,128,768]{2,1,0:T(8,128)(2,1)}, bf16[3,128,768]{2,1,0:T(8,128)(2,1)S(1)}, u32[]{:S(2)}, u32[]{:S(2)}) collective-permute-start(bf16[3,128,768]{2,1,0:T(8,128)(2,1)} %x_ref.1), channel_id=1, source_target_pairs={{0,8},{8,0},{16,24},{24,16},{1,9},{9,1},{17,25},{25,17},{2,10},{10... | collective-permute-start | bytes 1769480 | tf_op jit(solution)/shard_map/ppermute | solution.py:366
  17.2 5.2 %copy-start.4 = (bf16[3,128,768]{2,1,0:T(8,128)(2,1)}, bf16[3,128,768]{2,1,0:T(8,128)(2,1)S(1)}, u32[]{:S(2)}) copy-start(bf16[3,128,768]{2,1,0:T(8,128)(2,1)S(1)} %collective-permute-done.1.refs_2_) | copy-start | bytes 1769476
  17.2 5.2 %collective-permute-start.2 = (bf16[3,128,768]{2,1,0:T(8,128)(2,1)S(1)}, bf16[3,128,768]{2,1,0:T(8,128)(2,1)S(1)}, u32[]{:S(2)}, u32[]{:S(2)}) collective-permute-start(bf16[3,128,768]{2,1,0:T(8,128)(2,1)S(1)} %collective-permute-done.1.refs_2_), channel_id=1, source_target_pairs={{0,8},{8,0},{16,24},{24,16},{1,9},{9,1},{17,25},{25,17},{2,10},{10... | collective-permute-start | bytes 1769480 | tf_op jit(solution)/shard_map/ppermute | solution.py:366
  17.2 3.8 %collective-permute-start.4 = (s32[3,128]{1,0:T(4,128)}, s32[3,128]{1,0:T(4,128)S(1)}, u32[]{:S(2)}, u32[]{:S(2)}) collective-permute-start(s32[3,128]{1,0:T(4,128)} %refs_5_.1), channel_id=1, source_target_pairs={{0,16},{8,24},{16,0},{24,8},{1,17},{9,25},{17,1},{25,9},{2,18},{10... | collective-permute-start | bytes 4616 | tf_op jit(solution)/shard_map/ppermute | solution.py:366
  19.0 3.4 %collective-permute-start.3 = (s32[3,128]{1,0:T(4,128)}, s32[3,128]{1,0:T(4,128)S(1)}, u32[]{:S(2)}, u32[]{:S(2)}) collective-permute-start(s32[3,128]{1,0:T(4,128)} %refs_5_.1), channel_id=1, source_target_pairs={{0,8},{8,0},{16,24},{24,16},{1,9},{9,1},{17,25},{25,17},{2,10},{10... | collective-permute-start | bytes 4616 | tf_op jit(solution)/shard_map/ppermute | solution.py:366
  21.0 1.4 %copy-start.8 = (s32[3,128]{1,0:T(4,128)}, s32[3,128]{1,0:T(4,128)S(1)}, u32[]{:S(2)}) copy-start(s32[3,128]{1,0:T(4,128)S(1)} %collective-permute-done.4.refs_7_) | copy-start | bytes 4612
  21.0 1.4 %collective-permute-start.5 = (s32[3,128]{1,0:T(4,128)S(1)}, s32[3,128]{1,0:T(4,128)S(1)}, u32[]{:S(2)}, u32[]{:S(2)}) collective-permute-start(s32[3,128]{1,0:T(4,128)S(1)} %collective-permute-done.4.refs_7_), channel_id=1, source_target_pairs={{0,8},{8,0},{16,24},{24,16},{1,9},{9,1},{17,25},{25,17},{2,10},{10... | collective-permute-start | bytes 4616 | tf_op jit(solution)/shard_map/ppermute | solution.py:366
  22.4 0.6 copy-start.9
  22.4 0.6 copy-start.10
  22.4 0.8 copy-start.5
  23.2 0.8 copy-start.6
  65.5 5.6 %copy-start.7 = (f32[16,768]{1,0:T(8,128)S(1)}, f32[16,768]{1,0:T(8,128)}, u32[]{:S(2)}) copy-start(f32[16,768]{1,0:T(8,128)} %get-tuple-element.33) | copy-start | bytes 147460
  65.5 2.5 %collective-permute-start.7 = (bf16[3,128,768]{2,1,0:T(8,128)(2,1)}, bf16[3,128,768]{2,1,0:T(8,128)(2,1)S(1)}, u32[]{:S(2)}, u32[]{:S(2)}) collective-permute-start(bf16[3,128,768]{2,1,0:T(8,128)(2,1)} %get-tuple-element.31), channel_id=1, source_target_pairs={{0,8},{8,0},{16,24},{24,16},{1,9},{9,1},{17,25},{25,17},{2,10},{10... | collective-permute-start | bytes 1769480 | tf_op jit(solution)/shard_map/ppermute | solution.py:366
  66.2 35.4 %collective-permute-start.6 = (bf16[3,128,768]{2,1,0:T(8,128)(2,1)}, bf16[3,128,768]{2,1,0:T(8,128)(2,1)S(1)}, u32[]{:S(2)}, u32[]{:S(2)}) collective-permute-start(bf16[3,128,768]{2,1,0:T(8,128)(2,1)} %get-tuple-element.29), channel_id=1, source_target_pairs={{0,8},{8,0},{16,24},{24,16},{1,9},{9,1},{17,25},{25,17},{2,10},{10... | collective-permute-start | bytes 1769480 | tf_op jit(solution)/shard_map/ppermute | solution.py:366
  68.0 33.6 %copy-start = (bf16[3,128,768]{2,1,0:T(8,128)(2,1)S(1)}, bf16[3,128,768]{2,1,0:T(8,128)(2,1)}, u32[]{:S(2)}) copy-start(bf16[3,128,768]{2,1,0:T(8,128)(2,1)} %x_ref.1) | copy-start | bytes 1769476
  68.0 33.6 %copy-start.1 = (f32[384,768]{1,0:T(8,128)S(1)}, f32[384,768]{1,0:T(8,128)}, u32[]{:S(2)}) copy-start(f32[384,768]{1,0:T(8,128)} %get-tuple-element.28.own) | copy-start | bytes 3538948
  68.0 33.6 %copy-start.3 = (f32[768]{0:T(1024)S(1)}, f32[768]{0:T(1024)}, u32[]{:S(2)}) copy-start(f32[768]{0:T(1024)} %gain1.1) | copy-start | bytes 9220
  69.3 32.3 %collective-permute-start.8 = (bf16[3,128,768]{2,1,0:T(8,128)(2,1)S(1)}, bf16[3,128,768]{2,1,0:T(8,128)(2,1)S(1)}, u32[]{:S(2)}, u32[]{:S(2)}) collective-permute-start(bf16[3,128,768]{2,1,0:T(8,128)(2,1)S(1)} %add.18), channel_id=1, source_target_pairs={{0,16},{8,24},{16,0},{24,8},{1,17},{9,25},{17,1},{25,9},{2,18},{10... | collective-permute-start | bytes 1769480 | tf_op jit(solution)/shard_map/ppermute | solution.py:366
  71.1 1.2 %collective-permute-start.9 = (f32[16,768]{1,0:T(8,128)S(1)}, f32[16,768]{1,0:T(8,128)S(1)}, u32[]{:S(2)}, u32[]{:S(2)}) collective-permute-start(f32[16,768]{1,0:T(8,128)S(1)} %copy-done.7), channel_id=1, source_target_pairs={{0,8},{8,0},{16,24},{24,16},{1,9},{9,1},{17,25},{25,17},{2,10},{10... | collective-permute-start | bytes 147464 | tf_op jit(solution)/shard_map/ppermute | solution.py:366
  72.4 13.7 %collective-permute-start.10 = (f32[16,768]{1,0:T(8,128)S(1)}, f32[16,768]{1,0:T(8,128)S(1)}, u32[]{:S(2)}, u32[]{:S(2)}) collective-permute-start(f32[16,768]{1,0:T(8,128)S(1)} %add.19), channel_id=1, source_target_pairs={{0,16},{8,24},{16,0},{24,8},{1,17},{9,25},{17,1},{25,9},{2,18},{10... | collective-permute-start | bytes 147464 | tf_op jit(solution)/shard_map/ppermute | solution.py:366
  86.1 4.2 %collective-permute-start.11 = (f32[16,768]{1,0:T(8,128)S(1)}, f32[16,768]{1,0:T(8,128)S(1)}, u32[]{:S(2)}, u32[]{:S(2)}) collective-permute-start(f32[16,768]{1,0:T(8,128)S(1)} %add.20), channel_id=1, source_target_pairs={{0,1},{1,0},{2,3},{3,2},{4,5},{5,4},{6,7},{7,6},{8,9},{9,8},{10,11... | collective-permute-start | bytes 147464 | tf_op jit(solution)/shard_map/ppermute | solution.py:366
  90.2 4.2 %collective-permute-start.12 = (f32[16,768]{1,0:T(8,128)S(1)}, f32[16,768]{1,0:T(8,128)S(1)}, u32[]{:S(2)}, u32[]{:S(2)}) collective-permute-start(f32[16,768]{1,0:T(8,128)S(1)} %add.21), channel_id=1, source_target_pairs={{0,2},{1,3},{2,0},{3,1},{4,6},{5,7},{6,4},{7,5},{8,10},{9,11},{10,... | collective-permute-start | bytes 147464 | tf_op jit(solution)/shard_map/ppermute | solution.py:366
  94.4 5.2 %collective-permute-start.13 = (f32[16,768]{1,0:T(8,128)S(1)}, f32[16,768]{1,0:T(8,128)S(1)}, u32[]{:S(2)}, u32[]{:S(2)}) collective-permute-start(f32[16,768]{1,0:T(8,128)S(1)} %add.22), channel_id=1, source_target_pairs={{0,4},{1,5},{2,6},{3,7},{4,0},{5,1},{6,2},{7,3},{8,12},{9,13},{10,... | collective-permute-start | bytes 147464 | tf_op jit(solution)/shard_map/ppermute | solution.py:366
  101.6 1.3 %copy-start.2 = (f32[384,768]{1,0:T(8,128)S(1)}, f32[384,768]{1,0:T(8,128)}, u32[]{:S(2)}) copy-start(f32[384,768]{1,0:T(8,128)} %get-tuple-element.32.hidden_grad) | copy-start | bytes 3538948

commit v2 on v0

v2 whole, which is shorter than its diff:
```python
import functools

import jax
import jax.numpy as jnp
from jax import lax
from jax.experimental import pallas as pl
from jax.experimental.pallas import tpu as pltpu
from jax.sharding import PartitionSpec as P

F32 = jnp.float32
BF16 = jnp.bfloat16
HI = lax.Precision.HIGHEST
epsilon = 1e-06
masked = -1e30
gelu_a = 0.7978845608028654
gelu_b = 0.044715
MIB = 1024 * 1024
shared_slots = (192, 448, 576, 704)
VM = pl.BlockSpec(memory_space=pltpu.VMEM)


def dot(a, b, precision=None):
    return lax.dot_general(a, b, (((1,), (0,)), ((), ())), precision=precision, preferred_element_type=F32)


def dot_nt(a, b, precision=None):
    return lax.dot_general(a, b, (((1,), (1,)), ((), ())), precision=precision, preferred_element_type=F32)


def dot_tn(a, b, precision=None):
    return lax.dot_general(a, b, (((0,), (0,)), ((), ())), precision=precision, preferred_element_type=F32)


def iota(shape, axis):
    return lax.broadcasted_iota(jnp.int32, shape, axis)


def block_of(index, size, count):
    total = jnp.zeros_like(index)
    for k in range(1, count):
        total = total + (index >= k * size).astype(jnp.int32)
    return total


def gelu_pair(v):
    square = v * v
    h = 0.5 + 0.5 * jnp.tanh(v * (gelu_a + gelu_a * gelu_b * square))
    g = v * h
    slope = h + (g - g * h) * (2.0 * gelu_a + 6.0 * gelu_a * gelu_b * square)
    return g, slope


def inverse_rms(x):
    return lax.rsqrt(jnp.mean(x * x, -1, keepdims=True) + epsilon)


class Far:
    def __init__(self, value):
        self.value = value


def near(value):
    return pltpu.with_memory_space_constraint(value, pltpu.VMEM)


def call(kernel, outs, args, limit, micros, scratch=(), copies=0, last=False):
    specs = [pl.BlockSpec(memory_space=pl.ANY) if isinstance(a, Far) else VM for a in args]
    args = [pltpu.with_memory_space_constraint(a.value, pltpu.HBM) if isinstance(a, Far) else near(a) for a in args]
    scratch = [pltpu.VMEM(shape, kind) for shape, kind in scratch]
    if copies:
        scratch.append(pltpu.SemaphoreType.DMA((copies,)))
    made = jax.ShapeDtypeStruct if last else pltpu.VMEM
    return pl.pallas_call(
        kernel,
        out_shape=[made(shape, kind) for shape, kind in outs],
        in_specs=specs,
        out_specs=[VM] * len(outs),
        scratch_shapes=scratch,
        compiler_params=pltpu.CompilerParams(vmem_limit_bytes=limit * MIB),
        cost_estimate=pl.CostEstimate(flops=int(micros * 1.1e9), bytes_accessed=0, transcendentals=0),
    )(*args)


def start_copies(pairs, sems):
    started = [pltpu.make_async_copy(source, target, sems.at[k]) for k, (source, target) in enumerate(pairs)]
    for one in started:
        one.start()
    return started


def pick_kernel(inputs, cotangent, segment_ids, own, a_send, b_send, cot_send, ids, sems):
    rows, shard, width = inputs.shape
    extra = own.shape[1] - shard
    row = moved_row(rows)
    other = rows - 1 - row
    body = pl.ds(0, shard)
    started = start_copies(
        [
            (segment_ids, ids),
            (inputs.at[other], a_send.at[0, body]),
            (inputs.at[1], b_send.at[0, body]),
            (inputs.at[row], own.at[0, body]),
            (inputs.at[1], own.at[1, body]),
            (cotangent.at[other], cot_send.at[0]),
        ],
        sems,
    )
    started[0].wait()
    for target, k, source in ((own, 0, row), (own, 1, 1), (a_send, 0, other), (b_send, 0, 1)):
        line = jnp.broadcast_to(ids[pl.ds(source, 1), :].astype(F32).astype(BF16), (extra, shard))
        target[k, shard:, :] = jnp.zeros((extra, width), BF16)
        target[k, shard:, 0:shard] = line
    for one in started[1:]:
        one.wait()


def setup_kernel(
    shard, parts, table_far, position_far, shared_far, dl_far, dr_far, ul_far, ur_far, bd_far, bu_far, g1_far, g2_far,
    wq_far, wk_far, wv_far, wo_far, win_far, wout_far,
    tiles, down_t, up, shx, shtx, drx, ulx, dlx, urx, bd, bu, g1, g2, wq, wk, wv, wo, win, wout,
    tab, sh16, sh16t, table, position_bias, shared, dl, dr, ul, ur, sems,
):
    started = start_copies(
        [
            (table_far, table), (position_far, position_bias), (shared_far, shared), (dl_far, dl), (dr_far, dr),
            (ul_far, ul), (ur_far, ur), (bd_far, bd), (bu_far, bu), (g1_far, g1), (g2_far, g2),
            (wq_far, wq), (wk_far, wk), (wv_far, wv), (wo_far, wo), (win_far, win), (wout_far, wout),
        ],
        sems,
    )
    for one in started[:11]:
        one.wait()
    heads = position_bias.shape[0]
    ranks, (mid, width) = shared.shape[0], down_t.shape
    inner, outer = mid // ranks, width // ranks
    square = ranks * ranks
    hits = (table[...][None, :] == iota((position_bias.shape[1], table.shape[0]), 0)).astype(F32)
    tab[0:heads, 0 : table.shape[0]] = dot(position_bias[...], hits, HI)
    for k in range(2 * parts - 1):
        for h in range(heads):
            line = tab[h : h + 1, k * shard : (k + 2) * shard]
            turned = pltpu.roll(jnp.broadcast_to(line, (shard, 2 * shard)), shard + 1, 1, stride=1, stride_axis=0)
            tiles[k, h // 2, (h % 2) * shard : (h % 2 + 1) * shard, :] = turned[:, :shard]
    eye = (iota((ranks, ranks), 0) == iota((ranks, ranks), 1)).astype(F32)
    for i in range(ranks):
        block = shared[i]
        sh16[i * ranks : (i + 1) * ranks, :] = block
        sh16t[i * ranks : (i + 1) * ranks, :] = dot_tn(block, eye, HI)
    spread, by_c, by_j, by_b, own_block = selectors(ranks, mid, width)
    shx[...] = dot(sh16[...], by_c, HI)
    shtx[...] = dot(sh16t[...], by_c, HI)
    drx[...] = dot(dot(spread, dr[...], HI), by_j, HI)
    ulx[...] = dot(dot(spread, ul[...], HI), by_j, HI)
    dlx[...] = dot(dot(spread, dl[...], HI), by_b, HI) * own_block
    urx[...] = dot(dot(spread, ur[...], HI), by_b, HI) * own_block
    down_t[...] = dot_tn(shx[...] * drx[...], dlx[...], HI).astype(BF16)
    up[...] = dot_tn(shtx[...] * ulx[...], urx[...], HI).astype(BF16)
    for one in started[11:]:
        one.wait()


def selectors(ranks, mid, width):
    inner, outer, square = mid // ranks, width // ranks, ranks * ranks
    spread = (block_of(iota((square, ranks), 0), ranks, ranks) == iota((square, ranks), 1)).astype(F32)
    by_c = (block_of(iota((ranks, mid), 1), inner, ranks) == iota((ranks, mid), 0)).astype(F32)
    column = iota((inner, mid), 1)
    by_j = (column - inner * block_of(column, inner, ranks) == iota((inner, mid), 0)).astype(F32)
    column = iota((outer, width), 1)
    by_b = (column - outer * block_of(column, outer, ranks) == iota((outer, width), 0)).astype(F32)
    line = iota((square, width), 0)
    own_block = (
        line - ranks * block_of(line, ranks, ranks) == block_of(iota((square, width), 1), outer, ranks)
    ).astype(F32)
    return spread, by_c, by_j, by_b, own_block


def moved_row(rows):
    half = lax.axis_size("seq") // 2
    return jnp.where(lax.axis_index("seq") < half, 0, rows - 1)


def normed(x, gain):
    x = x.astype(F32)
    return (x * inverse_rms(x) * gain[...][None, :]).astype(BF16)


def project(x, weight, target, at):
    pairs, _, lanes = target.shape
    count = x.shape[0]
    for t in range(pairs // 2):
        result = dot(x, weight[:, 2 * t * lanes : (2 * t + 2) * lanes]).astype(BF16)
        target[2 * t, at : at + count, :] = result[:, :lanes]
        target[2 * t + 1, at : at + count, :] = result[:, lanes:]


def local_kernel(own, sib, wq, wk, wv, gain, k_loc, v_loc, q_loc):
    shard = q_loc.shape[1] // 2
    blocks = [normed(x, gain) for x in (own[0, :shard], sib[0, :shard], own[1, :shard], sib[1, :shard])]
    x = jnp.concatenate(blocks, 0)
    project(x, wk, k_loc, 0)
    project(x, wv, v_loc, 0)
    project(jnp.concatenate([blocks[0], blocks[2]], 0), wq, q_loc, 0)


def segment_features(blocks, shard, lanes):
    lane = iota((shard, lanes), 1)
    keys, queries = [], []
    for block in blocks:
        line = block[shard : shard + 1, 0:shard].astype(F32)
        same = lane.astype(F32) == jnp.transpose(jnp.broadcast_to(line, (lanes, shard)))
        keys.append(same.astype(F32).astype(BF16))
        queries.append(jnp.where((lane < 3) & jnp.logical_not(same), masked, 0.0).astype(BF16))
    return jnp.concatenate(keys, 0), queries


def halves(lanes):
    low = iota((1, lanes), 1) < lanes // 2
    low_lane = low.astype(F32).astype(BF16)
    return low, low_lane, 1.0 - low_lane


def attend(p, q, feature, keys, key_feature, values, bias):
    shard, lanes = q.shape
    low, low_lane, high_lane = halves(lanes)
    left = jnp.concatenate(
        [jnp.concatenate([q * low_lane, feature], 1), jnp.concatenate([q * high_lane, feature], 1)], 0
    )
    scores = dot_nt(left, jnp.concatenate([keys, key_feature], 1)) + bias
    weights = jnp.exp(scores - jnp.max(scores, 1, keepdims=True)).astype(BF16)
    both = dot(weights, jnp.concatenate([values, jnp.ones(values.shape, BF16)], 1))
    scale = 1.0 / both[:, lanes:]
    mixed = both[:, :lanes] * scale
    return weights, jnp.where(low, mixed[:shard], mixed[shard:]), jnp.where(low, scale[:shard], scale[shard:])


def attention_kernel(
    is_moved, own, sib, far, far_sib, k_loc, v_loc, q_loc, tiles,
    wq, wk, wv, wo, gain, k_rem, v_rem, *rest,
):
    pairs, _, lanes = k_rem.shape
    shard = q_loc.shape[1] // 2
    if is_moved:
        q_rem, e, ctx, rinv, hid = rest
        first, queries = 0, [0, 2]
    else:
        e, ctx, rinv, hid = rest
        first, queries = 1, [0]
    place = lax.axis_index("seq")
    parts = lax.axis_size("seq")
    far_low = normed(far[0, :shard], gain)
    x = jnp.concatenate([far_low, normed(far_sib[0, :shard], gain)], 0)
    project(x, wk, k_rem, 0)
    project(x, wv, v_rem, 0)
    if is_moved:
        project(far_low, wq, q_rem, 0)
    key_feature, query_feature = segment_features(
        (own.at[first], sib.at[first], far.at[0], far_sib.at[0]), shard, lanes
    )
    local = slice(2 * first * shard, 2 * (first + 1) * shard)
    contexts = [[] for _ in queries]
    for p in range(pairs):
        keys = jnp.concatenate([k_loc[p, local, :], k_rem[p]], 0)
        values = jnp.concatenate([v_loc[p, local, :], v_rem[p]], 0)
        for b, block in enumerate(queries):
            q = q_rem[p] if block == 2 else q_loc[p, first * shard : (first + 1) * shard, :]
            at = jnp.bitwise_xor(place, block)
            bias = jnp.concatenate(
                [tiles[jnp.bitwise_xor(place, k) - at + parts - 1, p] for k in range(parts)], 1
            )
            weights, kept, scale = attend(p, q, query_feature[block], keys, key_feature, values, bias)
            e[b * pairs + p] = weights
            span = slice(b * shard, (b + 1) * shard)
            ctx[p, span, :] = kept
            rinv[p, span, :] = scale
            contexts[b].append(kept.astype(BF16))
    context = jnp.concatenate([jnp.concatenate(c, 1) for c in contexts], 0)
    x = jnp.concatenate([own[first, :shard]] + ([far[0, :shard]] if is_moved else []), 0).astype(F32)
    hid[...] = x + dot(context, wo[...])


def middle_kernel(
    hid_a, hid_b, cot, cot_far, win, wout, wo, gain2, bd, bu, down_t, up,
    out, hidden_grad, dctx, grad_up, grad_down_t, lines, low, act, gslope,
):
    rows, shard, width = cot.shape
    hidden = win.shape[1]
    pairs, _, lanes = dctx.shape
    state = jnp.concatenate([hid_a[...], hid_b[...]], 0)
    inv2 = inverse_rms(state)
    low[...] = (state * inv2 * gain2[...][None, :]).astype(BF16)
    chunk = 2 * lanes
    for j in range(hidden // chunk):
        cols = slice(j * chunk, (j + 1) * chunk)
        g, slope = gelu_pair(dot(low[...], win[:, cols]))
        gslope[:, cols] = slope.astype(BF16)
        act[:, cols] = g.astype(BF16)
    branch = dot(act[...], wout[...])
    row = moved_row(rows)
    branch_low = branch.astype(BF16)
    g, slope = gelu_pair(dot_nt(branch_low, down_t[...]) + bd[...][None, :])
    g_low = g.astype(BF16)
    up_low = jnp.concatenate([cot[row], cot_far[0], cot[1]], 0)
    upstream = up_low.astype(F32)
    gb = dot_nt(up_low, up[...]) * slope
    gb_low = gb.astype(BF16)
    low[...] = (upstream + dot(gb_low, down_t[...])).astype(BF16)
    result = state + branch + dot(g_low, up[...]) + bu[...][None, :]
    for b in range(rows):
        out[b] = result[b * shard : (b + 1) * shard].astype(BF16)
    grad_up[...] = dot_tn(g_low, up_low)
    grad_down_t[...] = dot_tn(gb_low, branch_low)
    for j in range(hidden // chunk):
        cols = slice(j * chunk, (j + 1) * chunk)
        act[:, cols] = (dot_nt(low[...], wout[cols, :]) * gslope[:, cols].astype(F32)).astype(BF16)
    grad2 = dot_nt(act[...], win[...])
    state = jnp.concatenate([hid_a[...], hid_b[...]], 0)
    inv2 = inverse_rms(state)
    hat2 = state * inv2
    c = grad2 * gain2[...][None, :]
    total = upstream + inv2 * (c - hat2 * jnp.mean(hat2 * c, -1, keepdims=True))
    hidden_grad[...] = total
    low[...] = total.astype(BF16)
    lines[...] = jnp.zeros(lines.shape, F32)
    lines[0:1, :] = jnp.sum(grad2 * hat2, 0, keepdims=True)
    lines[1:2, :] = jnp.sum(upstream, 0, keepdims=True)
    lines[2:3, 0 : gb.shape[1]] = jnp.sum(gb, 0, keepdims=True)
    for t in range(pairs // 2):
        part = dot_nt(low[...], wo[2 * t * lanes : (2 * t + 2) * lanes, :]).astype(BF16)
        dctx[2 * t] = part[:, :lanes]
        dctx[2 * t + 1] = part[:, lanes:]


def backward_kernel(
    is_moved, ranks, own, sib, far, far_sib, dctx, ctx, rinv, e, k_loc, v_loc, q_loc, k_rem, v_rem, *rest,
):
    pairs, _, lanes = dctx.shape
    shard, width = q_loc.shape[1] // 2, pairs * lanes
    if is_moved:
        q_rem, wq, wk, wv, *rest = rest
        *small, own_part, sib_part, pack, dkt, dvt = rest
        first, blocks, start = 0, 2, 0
    else:
        wq, wk, wv, pack_a, own_part, far_part, sib_part, pack, dkt, dvt = rest
        first, blocks, start = 1, 1, 2
    low, low_lane, high_lane = halves(lanes)
    low_row = (iota((lanes, 1), 0) < lanes // 2).astype(F32).astype(BF16)
    high_row = 1.0 - low_row
    local = slice(2 * first * shard, 2 * (first + 1) * shard)
    query_grads = [[] for _ in range(blocks)]
    for p in range(pairs):
        keys = jnp.concatenate([k_loc[p, local, :], k_rem[p]], 0)
        values = jnp.concatenate([v_loc[p, local, :], v_rem[p]], 0)
        turned_q, turned_s, steeps, weight_list = [], [], [], []
        for b in range(blocks):
            span = slice(b * shard, (b + 1) * shard)
            scaled = dctx[p, (start + b) * shard : (start + b + 1) * shard, :].astype(F32) * rinv[p, span, :]
            product = scaled * ctx[p, span, :]
            delta = jnp.concatenate(
                [
                    jnp.sum(jnp.where(low, product, 0.0), 1, keepdims=True),
                    jnp.sum(jnp.where(low, 0.0, product), 1, keepdims=True),
                ],
                0,
            )
            scaled = scaled.astype(BF16)
            left = jnp.concatenate([scaled * low_lane, scaled * high_lane], 0)
            weights = e[b * pairs + p]
            steep = weights * (dot_nt(left, values) - delta).astype(BF16)
            grad_q = dot(steep, keys)
            query_grads[b].append(jnp.where(low, grad_q[:shard], grad_q[shard:]).astype(BF16))
            q = q_rem[p] if b == 1 else q_loc[p, first * shard : (first + 1) * shard, :]
            q_t, s_t = jnp.transpose(q), jnp.transpose(scaled)
            turned_q += [q_t * low_row, q_t * high_row]
            turned_s += [s_t * low_row, s_t * high_row]
            steeps.append(steep)
            weight_list.append(weights)
        dkt[p] = dot(jnp.concatenate(turned_q, 1), jnp.concatenate(steeps, 0)).astype(BF16)
        dvt[p] = dot(jnp.concatenate(turned_s, 1), jnp.concatenate(weight_list, 0)).astype(BF16)
    keys = dkt.shape[2]
    key_t = dkt[...].reshape(width, keys)
    value_t = dvt[...].reshape(width, keys)
    part = jnp.transpose(dot(wk[...], key_t) + dot(wv[...], value_t))
    from_q = dot_nt(jnp.concatenate([jnp.concatenate(g, 1) for g in query_grads], 0), wq[...])
    pieces = [part[k * shard : (k + 1) * shard] for k in range(4)]
    pieces[0] = pieces[0] + from_q[:shard]
    if is_moved:
        pieces[2] = pieces[2] + from_q[shard:]
    gain = jnp.zeros((1, width), F32)
    for piece, x in zip(pieces, (own[first], sib[first], far[0], far_sib[0])):
        x = x[:shard].astype(F32)
        gain = gain + jnp.sum(piece * (x * inverse_rms(x)), 0, keepdims=True)
    if is_moved:
        pack_small(ranks, *small, pack)
        pack[0:1, :] = gain
        own_part[0] = pieces[0]
        own_part[1] = pieces[2]
    else:
        pack[...] = pack_a[...]
        pack[0:1, :] = pack_a[0:1, :] + gain
        sib_part[0, shard:, :] = jnp.zeros((16, width), BF16)
        sib_part[1, shard:, :] = jnp.concatenate(two_parts(pack[...]), 0)
        own_part[0] = pieces[0]
        far_part[0] = pieces[2].astype(BF16)
    sib_part[0, :shard] = pieces[1].astype(BF16)
    sib_part[1, :shard] = pieces[3].astype(BF16)


def pack_small(ranks, grad_up, grad_down_t, lines, shx, shtx, drx, ulx, dlx, urx, pack):
    mid, width = grad_up.shape
    inner, outer = mid // ranks, width // ranks
    spread, by_c, by_j, by_b, own_block = selectors(ranks, mid, width)
    pack[...] = jnp.zeros(pack.shape, F32)
    pack[1:4, :] = lines[0:3, :]
    down_t, up = grad_down_t[...], grad_up[...]
    p_down = dot_nt(dlx[...], down_t)
    p_up = dot_nt(urx[...], up)
    left = dot_tn(spread, dot(shx[...] * drx[...], down_t) * own_block)
    right = dot_tn(spread, dot(shtx[...] * ulx[...], up) * own_block)
    pack[4:8, 0:outer] = dot_nt(left, by_b)
    pack[4:8, 256 : 256 + outer] = dot_nt(right, by_b)
    pack[4:8, 512 : 512 + inner] = dot_nt(dot_tn(spread, p_down * shx[...]), by_j)
    pack[4:8, 640 : 640 + inner] = dot_nt(dot_tn(spread, p_up * shtx[...]), by_j)
    shared_down = dot_nt(p_down * drx[...], by_c)
    shared_up = dot_nt(p_up * ulx[...], by_c)
    eye = (iota((ranks, ranks), 0) == iota((ranks, ranks), 1)).astype(F32)
    for i, at in enumerate(shared_slots):
        one = slice(i * ranks, (i + 1) * ranks)
        pack[4:8, at : at + ranks] = shared_down[one] + dot_tn(shared_up[one], eye)


def norm_back(x, grad, hidden_grad, gain):
    x = x.astype(F32)
    inv = inverse_rms(x)
    hat = x * inv
    c = grad * gain[...][None, :]
    return hidden_grad + inv * (c - hat * jnp.mean(hat * c, -1, keepdims=True))


def return_kernel(_, far, own_part, from_sib, far_part, from_sib_b, out, hidden_grad, gain, result):
    shard = out.shape[1]
    result[0] = (far_part[0].astype(F32) + from_sib_b[1, :shard].astype(F32)).astype(BF16)
    result[1] = out[1]
    grad = own_part[1] + from_sib[1].astype(F32)
    result[2] = norm_back(far[0, :shard], grad, hidden_grad[shard : 2 * shard, :], gain).astype(BF16)


def last_kernel(
    own, part_a, sib_a, part_b, sib_b, returned, hidden_grad, gain, out, output, grad_input
):
    rows, shard, width = out.shape
    row = moved_row(rows)
    other = rows - 1 - row
    output[row] = out[0]
    output[1] = out[2]
    output[other] = returned[1]
    grad_input[other] = returned[2]
    grad = part_a[0] + sib_a[0].astype(F32)
    grad_input[row] = norm_back(own[0, :shard], grad, hidden_grad[0:shard, :], gain).astype(BF16)
    grad = part_b[0] + sib_b[0, :shard].astype(F32) + returned[0].astype(F32)
    grad_input[1] = norm_back(own[1, :shard], grad, hidden_grad[2 * shard :, :], gain).astype(BF16)


def unpack_kernel(ranks, mid, near_pack, far_pack, _, g1, g2, shared, dl, dr, ul, ur, bd, bu):
    width = near_pack.shape[1]
    pack = near_pack[...] + far_pack[...]
    inner, outer = mid // ranks, width // ranks
    g1[...] = pack[0]
    g2[...] = pack[1]
    bu[...] = pack[2]
    bd[...] = pack[3, 0:mid]
    dl[...] = pack[4:8, 0:outer]
    ur[...] = pack[4:8, 256 : 256 + outer]
    dr[...] = pack[4:8, 512 : 512 + inner]
    ul[...] = pack[4:8, 640 : 640 + inner]
    for i, at in enumerate(shared_slots):
        shared[i] = pack[4:8, at : at + ranks]


def two_parts(value):
    high = value.astype(BF16)
    return high, (value - high.astype(F32)).astype(BF16)


def sum_kernel(pack, from_sib, total):
    shard = from_sib.shape[1] - 16
    high, low = two_parts(pack[...])
    theirs = from_sib[1, shard:, :].astype(F32)
    total[...] = (high.astype(F32) + low.astype(F32)) + (theirs[0:8] + theirs[8:16])


def exchange(value, axis, bit):
    count = lax.axis_size(axis)
    return lax.ppermute(value, axis, [(k, k ^ bit) for k in range(count)])


def shards(
    inputs, cotangent, segment_ids, bucket_table, position_bias, query_weight, key_weight, value_weight, out_weight,
    hidden_in, hidden_out, gain_first, gain_second, shared, down_left, down_right, up_left_vectors, up_right,
    bias_down, bias_up,
):
    rows, shard, width = inputs.shape
    heads = position_bias.shape[1]
    hidden = hidden_in.shape[1]
    parts = lax.axis_size("seq")
    ranks, mid = shared.shape[0], bias_down.shape[0]
    pairs, tokens, keys = heads // 2, rows * shard, shard * parts
    lanes = width // pairs
    inner, outer, square = mid // ranks, width // ranks, ranks * ranks
    padded = shard + 16

    own, a_send, b_send, cot_send = call(
        pick_kernel,
        [((2, padded, width), BF16), ((1, padded, width), BF16), ((1, padded, width), BF16), ((1, shard, width), BF16)],
        (Far(inputs), Far(cotangent), Far(segment_ids)),
        8,
        1.0,
        [((rows, shard), jnp.int32)],
        6,
    )
    a_far = exchange(a_send, "seq", 2)
    b_far = exchange(b_send, "seq", 2)
    cot_far = exchange(cot_send, "seq", 2)
    sib = exchange(own, "seq", 1)

    small = (
        bucket_table, jnp.transpose(position_bias), shared, down_left, down_right, up_left_vectors, up_right,
        bias_down, bias_up, gain_first, gain_second,
    )
    large = (query_weight, key_weight, value_weight, out_weight, hidden_in, hidden_out)
    tiles, down_t, up, *expanded = call(
        functools.partial(setup_kernel, shard, parts),
        [((2 * parts - 1, pairs, 2 * shard, shard), F32), ((mid, width), BF16), ((mid, width), BF16)]
        + [((square, mid), F32)] * 4 + [((square, width), F32)] * 2
        + [(x.shape, x.dtype) for x in small[7:] + large],
        [Far(x) for x in small + large],
        8,
        4.0,
        [((16, 2 * keys), F32), ((square, ranks), F32), ((square, ranks), F32)]
        + [(x.shape, x.dtype) for x in small[:7]],
        len(small) + len(large),
    )
    bd, bu, gain1, gain2, wq, wk, wv, wo, win, wout = expanded[6:]
    expanded = expanded[:6]
    k_loc, v_loc, q_loc = call(
        local_kernel,
        [((pairs, 4 * shard, lanes), BF16), ((pairs, 4 * shard, lanes), BF16), ((pairs, 2 * shard, lanes), BF16)],
        (own, sib, wq, wk, wv, gain1),
        8,
        2.0,
    )
    a_far, k_loc = lax.optimization_barrier((a_far, k_loc))
    a_far_sib = exchange(a_far, "seq", 1)
    a_far_sib, b_far = lax.optimization_barrier((a_far_sib, b_far))
    b_far_sib = exchange(b_far, "seq", 1)
    proj = ((pairs, 2 * shard, lanes), BF16)
    weights = (wq, wk, wv, wo, gain1)
    ka, va, qa, ea, ctx_a, rinv_a, hid_a = call(
        functools.partial(attention_kernel, True),
        [
            proj, proj, ((pairs, shard, lanes), BF16), ((2 * pairs, 2 * shard, keys), BF16),
            ((pairs, 2 * shard, lanes), F32), ((pairs, 2 * shard, lanes), F32), ((2 * shard, width), F32),
        ],
        (own, sib, a_far, a_far_sib, k_loc, v_loc, q_loc, tiles, *weights),
        12,
        3.0,
    )
    kb, vb, eb, ctx_b, rinv_b, hid_b = call(
        functools.partial(attention_kernel, False),
        [
            proj, proj, ((pairs, 2 * shard, keys), BF16),
            ((pairs, shard, lanes), F32), ((pairs, shard, lanes), F32), ((shard, width), F32),
        ],
        (own, sib, b_far, b_far_sib, k_loc, v_loc, q_loc, tiles, *weights),
        12,
        3.0,
    )
    out, hidden_grad, dctx, grad_up, grad_down_t, lines = call(
        middle_kernel,
        [
            ((rows, shard, width), BF16), ((tokens, width), F32), ((pairs, tokens, lanes), BF16),
            ((mid, width), F32), ((mid, width), F32), ((8, width), F32),
        ],
        (
            hid_a, hid_b, cotangent, cot_far, win, wout, wo, gain2, bd, bu, down_t, up,
        ),
        20,
        12.0,
        [((tokens, width), BF16), ((tokens, hidden), BF16), ((tokens, hidden), BF16)],
    )
    turned = [((pairs, lanes, keys), BF16)] * 2
    part_a, sib_part_a, pack_a = call(
        functools.partial(backward_kernel, True, ranks),
        [((2, shard, width), F32), ((2, shard, width), BF16), ((8, width), F32)],
        (
            own, sib, a_far, a_far_sib, dctx, ctx_a, rinv_a, ea, k_loc, v_loc, q_loc, ka, va, qa,
            wq, wk, wv, grad_up, grad_down_t, lines, *expanded,
        ),
        14,
        6.0,
        turned,
    )
    sib_a = exchange(sib_part_a, "seq", 1)
    part_b, far_part, sib_part_b, pack = call(
        functools.partial(backward_kernel, False, ranks),
        [((1, shard, width), F32), ((1, shard, width), BF16), ((2, padded, width), BF16), ((8, width), F32)],
        (
            own, sib, b_far, b_far_sib, dctx, ctx_b, rinv_b, eb, k_loc, v_loc, q_loc, kb, vb,
            wq, wk, wv, pack_a,
        ),
        14,
        3.6,
        turned,
    )
    sib_part_b, sib_a = lax.optimization_barrier((sib_part_b, sib_a))
    sib_b = exchange(sib_part_b, "seq", 1)
    (pack,) = call(sum_kernel, [((8, width), F32)], (pack, sib_b), 8, 0.1)
    (back,) = call(
        return_kernel,
        [((rows, shard, width), BF16)],
        (pack, a_far, part_a, sib_a, far_part, sib_b, out, hidden_grad, gain1),
        16,
        0.5,
    )
    returned = exchange(back, "seq", 2)
    bit = 1
    while bit < lax.axis_size("batch"):
        pack = pack + exchange(pack, "batch", bit)
        bit *= 2
    far_pack = exchange(pack, "seq", 2)
    output, grad_input = call(
        last_kernel,
        [((rows, shard, width), BF16), ((rows, shard, width), BF16)],
        (own, part_a, sib_a, part_b, sib_b, returned, hidden_grad, gain1, out),
        16,
        1.0,
        last=True,
    )
    grads = call(
        functools.partial(unpack_kernel, ranks, mid),
        [
            ((width,), F32), ((width,), F32), ((ranks, ranks, ranks), F32), ((ranks, outer), F32),
            ((ranks, inner), F32), ((ranks, inner), F32), ((ranks, outer), F32), ((mid,), F32), ((width,), F32),
        ],
        (pack, far_pack, Far(grad_input)),
        8,
        0.5,
        last=True,
    )
    return (output, grad_input, *grads)


def solution(mesh):
    rows = P("batch", "seq", None)
    in_specs = (rows, rows, P("batch", "seq")) + (P(),) * 17
    out_specs = (rows, rows) + (P(),) * 9
    return jax.shard_map(shards, mesh=mesh, in_specs=in_specs, out_specs=out_specs, check_vma=False)
```

time: 352 us -> 66.3 us (0.19); the launches traced: 346 us -> 66.1 us
  local copies, waits for them, and re-layouts: 108 us -> 0.01 us
  matrix products: 103 us -> 0 us
  blocking collectives: 57.3 us -> 0 us
  Pallas kernels: 0 us -> 39.7 us
  other arithmetic: 29.1 us -> 0.01 us
  between operations: 15.5 us -> 0.77 us
  waiting for transfers between devices: 18 us -> 12 us
    dot_general x52 -> x0, matrix products: 103 us -> none  [the longest x5 18 us: project_back(): lax.dot_general(gradient, weight, (((1,), (1,)), ((), ())), preferred_ele...]
    psum x1 -> x0, blocking collectives: 40.8 us -> none  [shards(): gain_one_grad = lax.psum(gain_one_grad, ('seq', 'batch'))]
    pallas_call x0 -> x12, Pallas kernels: none -> 39.7 us  [call(): pl.pallas_call(kernel, out_shape=[made(shape, kind) for shape, kind in ou...]
    reshape x13 -> x0, local copies, waits for them, and re-layouts: 32.8 us -> none  [the longest x1 8.67 us: toeplitz_bias(): skewed = tiled.reshape(by_head.shape[0], shard_len, table_len - 1)]
    another operation x7 -> x0, local copies, waits for them, and re-layouts: 21 us -> none  [the longest x2 12.1 us: toeplitz_bias(): tiled = jnp.tile(turned, (1, shard_len))[:, :shard_len * (table_len - 1)]]
    all_gather x1 -> x0, blocking collectives: 16.5 us -> none  [shards(): seg_piece = lax.all_gather(segment_ids, 'seq', axis=1, tiled=True)]
    convert_element_type x9 -> x0, other arithmetic: 16.1 us -> none  [the longest x3 6.1 us: shards(): value_sum.astype(jnp.bfloat16)]
    slice x2 -> x0, local copies, waits for them, and re-layouts: 11.2 us -> none  [the longest x1 7.25 us: toeplitz_bias(): tiled = jnp.tile(turned, (1, shard_len))[:, :shard_len * (table_len - 1)]]
  transfers between devices with their start and end apart: 19 -> 13, of which waited for: 6 -> 7; matrix products, arithmetic and copies ran while one was open for 43% -> 0% of each run, Pallas kernels for 0% -> 29%
where the time goes in v2:
time: 66.3 us; the launch traced here: 66.1 us
  Pallas kernels  39.7 us (60%)
  starting transfers between devices  13.6 us (21%)
  waiting for transfers between devices  12 us (18%)
  between operations  0.77 us (1%)
    pallas_call x12, Pallas kernels, call(): pl.pallas_call(kernel, out_shape=[made(shape, kind) for shape, kind in ou...  39.7 us
    ppermute x13, starting transfers between devices, exchange(): return lax.ppermute(value, axis, [(k, k ^ bit) for k in range(count)])  13.6 us
    ppermute x13, waiting for transfers between devices, exchange(): return lax.ppermute(value, axis, [(k, k ^ bit) for k in range(count)])  12 us
  transfers between devices with their start and end apart: 13, of which 7 were waited for; matrix products, arithmetic and copies ran while one was open for 0% of the time, Pallas kernels for 29%

profile of v2, /device:TPU:0, one launch (start us, length us, event | category | flops | bytes accessed | tf_op | source)
XLA Modules:
  0.0 66.1 jit_solution(11726135207845470465)
XLA Ops:
  0.6 1.3 %shard_map.275 = (bf16[2,144,768]{2,1,0:T(8,128)(2,1)S(1)}, bf16[1,144,768]{2,1,0:T(8,128)(2,1)S(1)}, bf16[1,144,768]{2,1,0:T(8,128)(2,1)S(1)}, bf16[1,128,768]{2,1,0:T(8,128)(2,1)S(1)}) custom-call(bf16[3,128,768]{2,1,0:T(8,128)(2,1)} %inputs.1, bf16[3,128,768]{2,1,0:T(8,128)(2,1)} %cot.1, s32[3,128]{1,0:T(4,128)} %segment_ids.1), custom_call_target="tpu_custom_call" | custom-call | flops 1100000000 | tf_op jit(solution)/shard_map/pallas_call | solution.py:73
  2.0 0.5 collective-permute-start
  2.5 2.6 %collective-permute-start.1 = (bf16[1,144,768]{2,1,0:T(8,128)(2,1)S(1)}, bf16[1,144,768]{2,1,0:T(8,128)(2,1)S(1)}, u32[]{:S(2)}, u32[]{:S(2)}) collective-permute-start(bf16[1,144,768]{2,1,0:T(8,128)(2,1)S(1)} %get-tuple-element.81), channel_id=1, source_target_pairs={{0,16},{8,24},{16,0},{24,8},{1,17},{9,25},{17,1},{25,9},{2,18},{10... | collective-permute-start | bytes 663560 | tf_op jit(solution)/shard_map/ppermute | solution.py:493
  5.1 0.1 collective-permute-start.3
  5.2 5.4 %shard_map.276 = (f32[7,6,256,128]{3,2,1,0:T(8,128)S(1)}, bf16[48,768]{1,0:T(8,128)(2,1)S(1)}, bf16[48,768]{1,0:T(8,128)(2,1)S(1)}, f32[16,48]{1,0:T(8,128)S(1)}...) custom-call(s32[1023]{0:T(1024)} %table_far.1, ...), custom_call_target="tpu_custom_call" | custom-call | flops 4400000000 | tf_op jit(solution)/shard_map/pallas_call | solution.py:73
  10.6 0.0 collective-permute-done.sib
  10.6 1.8 %shard_map.277 = (bf16[6,512,128]{2,1,0:T(8,128)(2,1)S(1)}, bf16[6,512,128]{2,1,0:T(8,128)(2,1)S(1)}, bf16[6,256,128]{2,1,0:T(8,128)(2,1)S(1)}) custom-call(bf16[2,144,768]{2,1,0:T(8,128)(2,1)S(1)} %get-tuple-element.80.own, bf16[2,144,768]{2,1,0:T(8,128)(2,1)S(1)} %collective-permute-done.sib, bf16[768,768]{1,0:T(8,128)(2,1)S(1)} %get-tuple-element.82.wq.rest_1_.rest_0_, ...), custom_call_target="tpu_custom_call" | custom-call | flops 2200000000 | tf_op jit(solution)/shard_map/pallas_call | solution.py:73
  12.5 0.0 collective-permute-done.1.far
  12.5 0.2 collective-permute-start.2
  12.6 1.9 %collective-permute-start.5 = (bf16[1,128,768]{2,1,0:T(8,128)(2,1)S(1)}, bf16[1,128,768]{2,1,0:T(8,128)(2,1)S(1)}, u32[]{:S(2)}, u32[]{:S(2)}) collective-permute-start(bf16[1,128,768]{2,1,0:T(8,128)(2,1)S(1)} %get-tuple-element.98), channel_id=1, source_target_pairs={{0,16},{8,24},{16,0},{24,8},{1,17},{9,25},{17,1},{25,9},{2,18},{10... | collective-permute-start | bytes 589832 | tf_op jit(solution)/shard_map/ppermute | solution.py:493
  14.5 1.3 %collective-permute-done.3.far = bf16[1,144,768]{2,1,0:T(8,128)(2,1)S(1)} collective-permute-done((bf16[1,144,768]{2,1,0:T(8,128)(2,1)S(1)}, bf16[1,144,768]{2,1,0:T(8,128)(2,1)S(1)}, u32[]{:S(2)}, u32[]{:S(2)}) %collective-permute-start.3) | collective-permute-done | bytes 221216 | tf_op jit(solution)/shard_map/ppermute | solution.py:493
  15.9 0.0 collective-permute-done.2.far_sib
  15.9 0.0 collective-permute-start.4
  15.9 4.2 %shard_map.278 = (bf16[6,256,128]{2,1,0:T(8,128)(2,1)S(1)}, bf16[6,256,128]{2,1,0:T(8,128)(2,1)S(1)}, bf16[6,128,128]{2,1,0:T(8,128)(2,1)S(1)}, bf16[12,256,512]...) custom-call(bf16[2,144,768]{2,1,0:T(8,128)(2,1)S(1)} %get-tuple-element.80., ...), custom_call_target="tpu_custom_call" | custom-call | flops 3300000000 | tf_op jit(solution)/shard_map/pallas_call | solution.py:73
  20.1 0.0 copy-start
  20.1 0.0 collective-permute-done.4.far_sib
  20.1 2.4 %shard_map.279 = (bf16[6,256,128]{2,1,0:T(8,128)(2,1)S(1)}, bf16[6,256,128]{2,1,0:T(8,128)(2,1)S(1)}, bf16[6,256,512]{2,1,0:T(8,128)(2,1)S(1)}, f32[6,128,128]{2...) custom-call(bf16[2,144,768]{2,1,0:T(8,128)(2,1)S(1)} %get-tuple-element.80.own, ...), custom_call_target="tpu_custom_call" | custom-call | flops 3300000000 | tf_op jit(solution)/shard_map/pallas_call | solution.py:73
  22.5 0.0 collective-permute-done.5.cot_far
  22.5 0.0 copy-done
  22.5 11.8 %shard_map.280 = (bf16[3,128,768]{2,1,0:T(8,128)(2,1)S(1)}, f32[384,768]{1,0:T(8,128)S(1)}, bf16[6,384,128]{2,1,0:T(8,128)(2,1)S(1)}, f32[48,768]{1,0:T(8,128)S(...) custom-call(f32[256,768]{1,0:T(8,128)S(1)} %get-tuple-element.95.hid_a, f32[128,768]{1,0:T(8,128)S(1)} %get-tuple-element.97.hid_b, ...), custom_call_target="tpu_custom_call" | custom-call | flops 13200000000 | tf_op jit(solution)/shard_map/pallas_call | solution.py:73
  34.4 6.5 %shard_map.281 = (f32[2,128,768]{2,1,0:T(8,128)S(1)}, bf16[2,128,768]{2,1,0:T(8,128)(2,1)S(1)}, f32[8,768]{1,0:T(8,128)S(1)}) custom-call(bf16[2,144,768]{2,1,0:T(8,128)(2,1)S(1)} %get-tuple-element.80.own, bf16[2,144,768]{2,1,0:T(8,128)(2,1)S(1)} %collective-permute-done.sib, bf16[1,144,768]{2,1,0:T(8,128)(2,1)S(1)} %collective-permute-done.1.far, ...), custom_call_target="tpu_custom_call" | custom-call | flops 6600000000 | tf_op jit(solution)/shard_map/pallas_call | solution.py:73
  40.8 0.5 collective-permute-start.6
  41.4 3.7 %shard_map.282 = (f32[1,128,768]{2,1,0:T(8,128)S(1)}, bf16[1,128,768]{2,1,0:T(8,128)(2,1)S(1)}, bf16[2,144,768]{2,1,0:T(8,128)(2,1)S(1)}, f32[8,768]{1,0:T(8,128)S(1)}) custom-call(bf16[2,144,768]{2,1,0:T(8,128)(2,1)S(1)} %get-tuple-element.80.own, bf16[2,144,768]{2,1,0:T(8,128)(2,1)S(1)} %collective-permute-done.sib, ...), custom_call_target="tpu_custom_call" | custom-call | flops 3960000000 | tf_op jit(solution)/shard_map/pallas_call | solution.py:73
  45.1 0.0 collective-permute-done.6.from_sib.sib_a
  45.1 0.1 collective-permute-start.7
  45.2 1.8 %collective-permute-done.7.from_sib.from_sib_b.sib_b = bf16[2,144,768]{2,1,0:T(8,128)(2,1)S(1)} collective-permute-done((bf16[2,144,768]{2,1,0:T(8,128)(2,1)S(1)}, bf16[2,144,768]{2,1,0:T(8,128)(2,1)S(1)}, u32[]{:S(2)}, u32[]{:S(2)}) %collective-permute-start.7) | collective-permute-done | bytes 442400 | tf_op jit(solution)/shard_map/ppermute | solution.py:493
  47.0 0.3 shard_map.284
  47.3 1.8 %collective-permute-start.8 = (bf16[3,128,768]{2,1,0:T(8,128)(2,1)S(1)}, bf16[3,128,768]{2,1,0:T(8,128)(2,1)S(1)}, u32[]{:S(2)}, u32[]{:S(2)}) collective-permute-start(bf16[3,128,768]{2,1,0:T(8,128)(2,1)S(1)} %shard_map.284), channel_id=1, source_target_pairs={{0,16},{8,24},{16,0},{24,8},{1,17},{9,25},{17,1},{25,9},{2,18},{10... | collective-permute-start | bytes 1769480 | tf_op jit(solution)/shard_map/ppermute | solution.py:493
  49.2 1.5 %collective-permute-start.9 = (f32[8,768]{1,0:T(8,128)S(1)}, f32[8,768]{1,0:T(8,128)S(1)}, u32[]{:S(2)}, u32[]{:S(2)}) collective-permute-start(f32[8,768]{1,0:T(8,128)S(1)} %shard_map.283._), channel_id=1, source_target_pairs={{0,1},{1,0},{2,3},{3,2},{4,5},{5,4},{6,7},{7,6},{8,9},{9,8},{10,11... | collective-permute-start | bytes 73736 | tf_op jit(solution)/shard_map/ppermute | solution.py:493
  50.6 2.4 %collective-permute-done.9 = f32[8,768]{1,0:T(8,128)S(1)} collective-permute-done((f32[8,768]{1,0:T(8,128)S(1)}, f32[8,768]{1,0:T(8,128)S(1)}, u32[]{:S(2)}, u32[]{:S(2)}) %collective-permute-start.9) | collective-permute-done | bytes 24608 | tf_op jit(solution)/shard_map/ppermute | solution.py:493
  53.0 1.6 %collective-permute-start.10 = (f32[8,768]{1,0:T(8,128)S(1)}, f32[8,768]{1,0:T(8,128)S(1)}, u32[]{:S(2)}, u32[]{:S(2)}) collective-permute-start(f32[8,768]{1,0:T(8,128)S(1)} %add.9), channel_id=1, source_target_pairs={{0,2},{1,3},{2,0},{3,1},{4,6},{5,7},{6,4},{7,5},{8,10},{9,11},{10,... | collective-permute-start | bytes 73736 | tf_op jit(solution)/shard_map/ppermute | solution.py:493
  54.6 2.2 %collective-permute-done.10 = f32[8,768]{1,0:T(8,128)S(1)} collective-permute-done((f32[8,768]{1,0:T(8,128)S(1)}, f32[8,768]{1,0:T(8,128)S(1)}, u32[]{:S(2)}, u32[]{:S(2)}) %collective-permute-start.10) | collective-permute-done | bytes 24608 | tf_op jit(solution)/shard_map/ppermute | solution.py:493
  56.8 2.6 %collective-permute-start.11 = (f32[8,768]{1,0:T(8,128)S(1)}, f32[8,768]{1,0:T(8,128)S(1)}, u32[]{:S(2)}, u32[]{:S(2)}) collective-permute-start(f32[8,768]{1,0:T(8,128)S(1)} %add.10), channel_id=1, source_target_pairs={{0,4},{1,5},{2,6},{3,7},{4,0},{5,1},{6,2},{7,3},{8,12},{9,13},{10,... | collective-permute-start | bytes 73736 | tf_op jit(solution)/shard_map/ppermute | solution.py:493
  59.4 2.1 %collective-permute-done.11 = f32[8,768]{1,0:T(8,128)S(1)} collective-permute-done((f32[8,768]{1,0:T(8,128)S(1)}, f32[8,768]{1,0:T(8,128)S(1)}, u32[]{:S(2)}, u32[]{:S(2)}) %collective-permute-start.11) | collective-permute-done | bytes 24608 | tf_op jit(solution)/shard_map/ppermute | solution.py:493
  61.6 0.3 collective-permute-start.12
  61.8 1.2 %collective-permute-done.8.returned = bf16[3,128,768]{2,1,0:T(8,128)(2,1)S(1)} collective-permute-done((bf16[3,128,768]{2,1,0:T(8,128)(2,1)S(1)}, bf16[3,128,768]{2,1,0:T(8,128)(2,1)S(1)}, u32[]{:S(2)}, u32[]{:S(2)}) %collective-permute-start.8) | collective-permute-done | bytes 589856 | tf_op jit(solution)/shard_map/ppermute | solution.py:493
  63.1 1.4 %shard_map.285 = (bf16[3,128,768]{2,1,0:T(8,128)(2,1)}, bf16[3,128,768]{2,1,0:T(8,128)(2,1)}) custom-call(bf16[2,144,768]{2,1,0:T(8,128)(2,1)S(1)} %get-tuple-element.80.own, f32[2,128,768]{2,1,0:T(8,128)S(1)} %get-tuple-element.122.own_part.part_a, bf16[2,128,768]{2,1,0:T(8,128)(2,1)S(1)} %collective-permute-done.6.from_sib.sib_a, ...), custom_call_target="tpu_custom_call" | custom-call | flops 1100000000 | tf_op jit(solution)/shard_map/pallas_call | solution.py:73
  64.5 0.9 %collective-permute-done.12.far_pack = f32[8,768]{1,0:T(8,128)S(1)} collective-permute-done((f32[8,768]{1,0:T(8,128)S(1)}, f32[8,768]{1,0:T(8,128)S(1)}, u32[]{:S(2)}, u32[]{:S(2)}) %collective-permute-start.12) | collective-permute-done | bytes 24608 | tf_op jit(solution)/shard_map/ppermute | solution.py:493
  65.4 0.7 %shard_map.286 = (f32[768]{0:T(1024)}, f32[768]{0:T(1024)}, f32[4,4,4]{2,1,0:T(4,128)}, f32[4,192]{1,0:T(4,128)}, f32[4,12]{1,0:T(4,128)}, /*index=5*/f32[4,12]{...) custom-call(f32[8,768]{1,0:T(8,128)S(1)} %add.11.near_pack, f32[8,768]{1,0:T(8,128)S(1)} %collective-permute-done.12.far_pack, ...), custom_call_target="tpu_custom_call" | custom-call | flops 550000000 | tf_op jit(solution)/shard_map/pallas_call | solution.py:73
  (4 shorter events, 0.0 us)
Async XLA Ops:
  2.0 8.6 %collective-permute-start = (bf16[2,144,768]{2,1,0:T(8,128)(2,1)S(1)}, bf16[2,144,768]{2,1,0:T(8,128)(2,1)S(1)}, u32[]{:S(2)}, u32[]{:S(2)}) collective-permute-start(bf16[2,144,768]{2,1,0:T(8,128)(2,1)S(1)} %get-tuple-element.80.own), channel_id=1, source_target_pairs={{0,8},{8,0},{16,24},{24,16},{1,9},{9,1},{17,25},{25,17},{2,10},{10... | collective-permute-start | bytes 1327112 | tf_op jit(solution)/shard_map/ppermute | solution.py:493
  2.5 9.9 %collective-permute-start.1 = (bf16[1,144,768]{2,1,0:T(8,128)(2,1)S(1)}, bf16[1,144,768]{2,1,0:T(8,128)(2,1)S(1)}, u32[]{:S(2)}, u32[]{:S(2)}) collective-permute-start(bf16[1,144,768]{2,1,0:T(8,128)(2,1)S(1)} %get-tuple-element.81), channel_id=1, source_target_pairs={{0,16},{8,24},{16,0},{24,8},{1,17},{9,25},{17,1},{25,9},{2,18},{10... | collective-permute-start | bytes 663560 | tf_op jit(solution)/shard_map/ppermute | solution.py:493
  5.1 10.8 %collective-permute-start.3 = (bf16[1,144,768]{2,1,0:T(8,128)(2,1)S(1)}, bf16[1,144,768]{2,1,0:T(8,128)(2,1)S(1)}, u32[]{:S(2)}, u32[]{:S(2)}) collective-permute-start(bf16[1,144,768]{2,1,0:T(8,128)(2,1)S(1)} %get-tuple-element.88), channel_id=1, source_target_pairs={{0,16},{8,24},{16,0},{24,8},{1,17},{9,25},{17,1},{25,9},{2,18},{10... | collective-permute-start | bytes 663560 | tf_op jit(solution)/shard_map/ppermute | solution.py:493
  12.5 3.4 %collective-permute-start.2 = (bf16[1,144,768]{2,1,0:T(8,128)(2,1)S(1)}, bf16[1,144,768]{2,1,0:T(8,128)(2,1)S(1)}, u32[]{:S(2)}, u32[]{:S(2)}) collective-permute-start(bf16[1,144,768]{2,1,0:T(8,128)(2,1)S(1)} %collective-permute-done.1.far), channel_id=1, source_target_pairs={{0,8},{8,0},{16,24},{24,16},{1,9},{9,1},{17,25},{25,17},{2,10},{10... | collective-permute-start | bytes 663560 | tf_op jit(solution)/shard_map/ppermute | solution.py:493
  12.6 9.9 %collective-permute-start.5 = (bf16[1,128,768]{2,1,0:T(8,128)(2,1)S(1)}, bf16[1,128,768]{2,1,0:T(8,128)(2,1)S(1)}, u32[]{:S(2)}, u32[]{:S(2)}) collective-permute-start(bf16[1,128,768]{2,1,0:T(8,128)(2,1)S(1)} %get-tuple-element.98), channel_id=1, source_target_pairs={{0,16},{8,24},{16,0},{24,8},{1,17},{9,25},{17,1},{25,9},{2,18},{10... | collective-permute-start | bytes 589832 | tf_op jit(solution)/shard_map/ppermute | solution.py:493
  15.9 4.2 %collective-permute-start.4 = (bf16[1,144,768]{2,1,0:T(8,128)(2,1)S(1)}, bf16[1,144,768]{2,1,0:T(8,128)(2,1)S(1)}, u32[]{:S(2)}, u32[]{:S(2)}) collective-permute-start(bf16[1,144,768]{2,1,0:T(8,128)(2,1)S(1)} %collective-permute-done.3.far), channel_id=1, source_target_pairs={{0,8},{8,0},{16,24},{24,16},{1,9},{9,1},{17,25},{25,17},{2,10},{10... | collective-permute-start | bytes 663560 | tf_op jit(solution)/shard_map/ppermute | solution.py:493
  20.1 2.5 %copy-start = (bf16[3,128,768]{2,1,0:T(8,128)(2,1)S(1)}, bf16[3,128,768]{2,1,0:T(8,128)(2,1)}, u32[]{:S(2)}) copy-start(bf16[3,128,768]{2,1,0:T(8,128)(2,1)} %cot.1) | copy-start | bytes 1769476
  40.8 4.3 %collective-permute-start.6 = (bf16[2,128,768]{2,1,0:T(8,128)(2,1)S(1)}, bf16[2,128,768]{2,1,0:T(8,128)(2,1)S(1)}, u32[]{:S(2)}, u32[]{:S(2)}) collective-permute-start(bf16[2,128,768]{2,1,0:T(8,128)(2,1)S(1)} %get-tuple-element.130), channel_id=1, source_target_pairs={{0,8},{8,0},{16,24},{24,16},{1,9},{9,1},{17,25},{25,17},{2,10},{10... | collective-permute-start | bytes 1179656 | tf_op jit(solution)/shard_map/ppermute | solution.py:493
  45.1 1.9 %collective-permute-start.7 = (bf16[2,144,768]{2,1,0:T(8,128)(2,1)S(1)}, bf16[2,144,768]{2,1,0:T(8,128)(2,1)S(1)}, u32[]{:S(2)}, u32[]{:S(2)}) collective-permute-start(bf16[2,144,768]{2,1,0:T(8,128)(2,1)S(1)} %get-tuple-element.133), channel_id=1, source_target_pairs={{0,8},{8,0},{16,24},{24,16},{1,9},{9,1},{17,25},{25,17},{2,10},{10... | collective-permute-start | bytes 1327112 | tf_op jit(solution)/shard_map/ppermute | solution.py:493
  47.3 15.7 %collective-permute-start.8 = (bf16[3,128,768]{2,1,0:T(8,128)(2,1)S(1)}, bf16[3,128,768]{2,1,0:T(8,128)(2,1)S(1)}, u32[]{:S(2)}, u32[]{:S(2)}) collective-permute-start(bf16[3,128,768]{2,1,0:T(8,128)(2,1)S(1)} %shard_map.284), channel_id=1, source_target_pairs={{0,16},{8,24},{16,0},{24,8},{1,17},{9,25},{17,1},{25,9},{2,18},{10... | collective-permute-start | bytes 1769480 | tf_op jit(solution)/shard_map/ppermute | solution.py:493
  49.2 3.8 %collective-permute-start.9 = (f32[8,768]{1,0:T(8,128)S(1)}, f32[8,768]{1,0:T(8,128)S(1)}, u32[]{:S(2)}, u32[]{:S(2)}) collective-permute-start(f32[8,768]{1,0:T(8,128)S(1)} %shard_map.283._), channel_id=1, source_target_pairs={{0,1},{1,0},{2,3},{3,2},{4,5},{5,4},{6,7},{7,6},{8,9},{9,8},{10,11... | collective-permute-start | bytes 73736 | tf_op jit(solution)/shard_map/ppermute | solution.py:493
  53.0 3.8 %collective-permute-start.10 = (f32[8,768]{1,0:T(8,128)S(1)}, f32[8,768]{1,0:T(8,128)S(1)}, u32[]{:S(2)}, u32[]{:S(2)}) collective-permute-start(f32[8,768]{1,0:T(8,128)S(1)} %add.9), channel_id=1, source_target_pairs={{0,2},{1,3},{2,0},{3,1},{4,6},{5,7},{6,4},{7,5},{8,10},{9,11},{10,... | collective-permute-start | bytes 73736 | tf_op jit(solution)/shard_map/ppermute | solution.py:493
  56.8 4.7 %collective-permute-start.11 = (f32[8,768]{1,0:T(8,128)S(1)}, f32[8,768]{1,0:T(8,128)S(1)}, u32[]{:S(2)}, u32[]{:S(2)}) collective-permute-start(f32[8,768]{1,0:T(8,128)S(1)} %add.10), channel_id=1, source_target_pairs={{0,4},{1,5},{2,6},{3,7},{4,0},{5,1},{6,2},{7,3},{8,12},{9,13},{10,... | collective-permute-start | bytes 73736 | tf_op jit(solution)/shard_map/ppermute | solution.py:493
  61.6 3.8 %collective-permute-start.12 = (f32[8,768]{1,0:T(8,128)S(1)}, f32[8,768]{1,0:T(8,128)S(1)}, u32[]{:S(2)}, u32[]{:S(2)}) collective-permute-start(f32[8,768]{1,0:T(8,128)S(1)} %add.11.near_pack), channel_id=1, source_target_pairs={{0,16},{8,24},{16,0},{24,8},{1,17},{9,25},{17,1},{25,9},{2,18},{10... | collective-permute-start | bytes 73736 | tf_op jit(solution)/shard_map/ppermute | solution.py:493

commit v3 on v2

--- a/solution.py
+++ b/solution.py
@@ -15,7 +15,6 @@
 gelu_a = 0.7978845608028654
 gelu_b = 0.044715
 MIB = 1024 * 1024
-shared_slots = (192, 448, 576, 704)
 VM = pl.BlockSpec(memory_space=pltpu.VMEM)
 
 
@@ -117,7 +116,7 @@
 def setup_kernel(
     shard, parts, table_far, position_far, shared_far, dl_far, dr_far, ul_far, ur_far, bd_far, bu_far, g1_far, g2_far,
     wq_far, wk_far, wv_far, wo_far, win_far, wout_far,
-    tiles, down_t, up, shx, shtx, drx, ulx, dlx, urx, bd, bu, g1, g2, wq, wk, wv, wo, win, wout,
+    tiles, down_t, up, mix, side, left, bd, bu, g1, g2, wq, wk, wv, wo, win, wout,
     tab, sh16, sh16t, table, position_bias, shared, dl, dr, ul, ur, sems,
 ):
     started = start_copies(
@@ -147,14 +146,20 @@
         sh16[i * ranks : (i + 1) * ranks, :] = block
         sh16t[i * ranks : (i + 1) * ranks, :] = dot_tn(block, eye, HI)
     spread, by_c, by_j, by_b, own_block = selectors(ranks, mid, width)
-    shx[...] = dot(sh16[...], by_c, HI)
-    shtx[...] = dot(sh16t[...], by_c, HI)
-    drx[...] = dot(dot(spread, dr[...], HI), by_j, HI)
-    ulx[...] = dot(dot(spread, ul[...], HI), by_j, HI)
-    dlx[...] = dot(dot(spread, dl[...], HI), by_b, HI) * own_block
-    urx[...] = dot(dot(spread, ur[...], HI), by_b, HI) * own_block
-    down_t[...] = dot_tn(shx[...] * drx[...], dlx[...], HI).astype(BF16)
-    up[...] = dot_tn(shtx[...] * ulx[...], urx[...], HI).astype(BF16)
+    mix[...] = jnp.zeros(mix.shape, F32)
+    side[...] = jnp.zeros(side.shape, F32)
+    shx, shtx = dot(sh16[...], by_c, HI), dot(sh16t[...], by_c, HI)
+    drx, ulx = dot(dot(spread, dr[...], HI), by_j, HI), dot(dot(spread, ul[...], HI), by_j, HI)
+    dlx = dot(dot(spread, dl[...], HI), by_b, HI) * own_block
+    urx = dot(dot(spread, ur[...], HI), by_b, HI) * own_block
+    mix[:square, :mid] = shx
+    mix[square:, mid:] = shtx
+    side[:square, :mid] = drx
+    side[square:, mid:] = ulx
+    left[:square, :] = dlx
+    left[square:, :] = urx
+    down_t[...] = dot_tn(shx * drx, dlx, HI).astype(BF16)
+    up[...] = dot_tn(shtx * ulx, urx, HI).astype(BF16)
     for one in started[11:]:
         one.wait()
 
@@ -217,20 +222,6 @@
     low = iota((1, lanes), 1) < lanes // 2
     low_lane = low.astype(F32).astype(BF16)
     return low, low_lane, 1.0 - low_lane
-
-
-def attend(p, q, feature, keys, key_feature, values, bias):
-    shard, lanes = q.shape
-    low, low_lane, high_lane = halves(lanes)
-    left = jnp.concatenate(
-        [jnp.concatenate([q * low_lane, feature], 1), jnp.concatenate([q * high_lane, feature], 1)], 0
-    )
-    scores = dot_nt(left, jnp.concatenate([keys, key_feature], 1)) + bias
-    weights = jnp.exp(scores - jnp.max(scores, 1, keepdims=True)).astype(BF16)
-    both = dot(weights, jnp.concatenate([values, jnp.ones(values.shape, BF16)], 1))
-    scale = 1.0 / both[:, lanes:]
-    mixed = both[:, :lanes] * scale
-    return weights, jnp.where(low, mixed[:shard], mixed[shard:]), jnp.where(low, scale[:shard], scale[shard:])
 
 
 def attention_kernel(
@@ -258,20 +249,34 @@
     )
     local = slice(2 * first * shard, 2 * (first + 1) * shard)
     contexts = [[] for _ in queries]
+    low, low_lane, high_lane = halves(lanes)
     for p in range(pairs):
         keys = jnp.concatenate([k_loc[p, local, :], k_rem[p]], 0)
         values = jnp.concatenate([v_loc[p, local, :], v_rem[p]], 0)
-        for b, block in enumerate(queries):
+        lefts, biases = [], []
+        for block in queries:
             q = q_rem[p] if block == 2 else q_loc[p, first * shard : (first + 1) * shard, :]
+            feature = query_feature[block]
+            lefts.append(jnp.concatenate([q * low_lane, feature], 1))
+            lefts.append(jnp.concatenate([q * high_lane, feature], 1))
             at = jnp.bitwise_xor(place, block)
-            bias = jnp.concatenate(
-                [tiles[jnp.bitwise_xor(place, k) - at + parts - 1, p] for k in range(parts)], 1
+            biases.append(
+                jnp.concatenate([tiles[jnp.bitwise_xor(place, k) - at + parts - 1, p] for k in range(parts)], 1)
             )
-            weights, kept, scale = attend(p, q, query_feature[block], keys, key_feature, values, bias)
-            e[b * pairs + p] = weights
+        scores = dot_nt(jnp.concatenate(lefts, 0), jnp.concatenate([keys, key_feature], 1))
+        scores = scores + jnp.concatenate(biases, 0)
+        weights = jnp.exp(scores - jnp.max(scores, 1, keepdims=True)).astype(BF16)
+        both = dot(weights, jnp.concatenate([values, jnp.ones(values.shape, BF16)], 1))
+        scale = 1.0 / both[:, lanes:]
+        mixed = both[:, :lanes] * scale
+        for b in range(len(queries)):
+            one = slice(2 * b * shard, (2 * b + 1) * shard)
+            two = slice((2 * b + 1) * shard, (2 * b + 2) * shard)
             span = slice(b * shard, (b + 1) * shard)
+            e[b * pairs + p] = weights[2 * b * shard : 2 * (b + 1) * shard]
+            kept = jnp.where(low, mixed[one], mixed[two])
             ctx[p, span, :] = kept
-            rinv[p, span, :] = scale
+            rinv[p, span, :] = jnp.where(low, scale[one], scale[two])
             contexts[b].append(kept.astype(BF16))
     context = jnp.concatenate([jnp.concatenate(c, 1) for c in contexts], 0)
     x = jnp.concatenate([own[first, :shard]] + ([far[0, :shard]] if is_moved else []), 0).astype(F32)
@@ -280,7 +285,7 @@
 
 def middle_kernel(
     hid_a, hid_b, cot, cot_far, win, wout, wo, gain2, bd, bu, down_t, up,
-    out, hidden_grad, dctx, grad_up, grad_down_t, lines, low, act, gslope,
+    out, hidden_grad, dctx, adapter_grad, lines, low, act, gslope,
 ):
     rows, shard, width = cot.shape
     hidden = win.shape[1]
@@ -307,12 +312,15 @@
     result = state + branch + dot(g_low, up[...]) + bu[...][None, :]
     for b in range(rows):
         out[b] = result[b * shard : (b + 1) * shard].astype(BF16)
-    grad_up[...] = dot_tn(g_low, up_low)
-    grad_down_t[...] = dot_tn(gb_low, branch_low)
+    mid = g.shape[1]
+    adapter_grad[:mid, :] = dot_tn(gb_low, branch_low)
+    adapter_grad[mid:, :] = dot_tn(g_low, up_low)
+    grad2 = jnp.zeros((rows * shard, width), F32)
+    chunk = 6 * lanes
     for j in range(hidden // chunk):
         cols = slice(j * chunk, (j + 1) * chunk)
-        act[:, cols] = (dot_nt(low[...], wout[cols, :]) * gslope[:, cols].astype(F32)).astype(BF16)
-    grad2 = dot_nt(act[...], win[...])
+        pre = (dot_nt(low[...], wout[cols, :]) * gslope[:, cols].astype(F32)).astype(BF16)
+        grad2 = grad2 + dot_nt(pre, win[:, cols])
     state = jnp.concatenate([hid_a[...], hid_b[...]], 0)
     inv2 = inverse_rms(state)
     hat2 = state * inv2
@@ -347,35 +355,37 @@
     high_row = 1.0 - low_row
     local = slice(2 * first * shard, 2 * (first + 1) * shard)
     query_grads = [[] for _ in range(blocks)]
-    for p in range(pairs):
-        keys = jnp.concatenate([k_loc[p, local, :], k_rem[p]], 0)
-        values = jnp.concatenate([v_loc[p, local, :], v_rem[p]], 0)
-        turned_q, turned_s, steeps, weight_list = [], [], [], []
+
+    def prepare(p):
+        lefts, deltas, turned_q, turned_s = [], [], [], []
         for b in range(blocks):
             span = slice(b * shard, (b + 1) * shard)
             scaled = dctx[p, (start + b) * shard : (start + b + 1) * shard, :].astype(F32) * rinv[p, span, :]
             product = scaled * ctx[p, span, :]
-            delta = jnp.concatenate(
-                [
-                    jnp.sum(jnp.where(low, product, 0.0), 1, keepdims=True),
-                    jnp.sum(jnp.where(low, 0.0, product), 1, keepdims=True),
-                ],
-                0,
-            )
+            deltas.append(jnp.sum(jnp.where(low, product, 0.0), 1, keepdims=True))
+            deltas.append(jnp.sum(jnp.where(low, 0.0, product), 1, keepdims=True))
             scaled = scaled.astype(BF16)
-            left = jnp.concatenate([scaled * low_lane, scaled * high_lane], 0)
-            weights = e[b * pairs + p]
-            steep = weights * (dot_nt(left, values) - delta).astype(BF16)
-            grad_q = dot(steep, keys)
-            query_grads[b].append(jnp.where(low, grad_q[:shard], grad_q[shard:]).astype(BF16))
+            lefts += [scaled * low_lane, scaled * high_lane]
             q = q_rem[p] if b == 1 else q_loc[p, first * shard : (first + 1) * shard, :]
             q_t, s_t = jnp.transpose(q), jnp.transpose(scaled)
             turned_q += [q_t * low_row, q_t * high_row]
             turned_s += [s_t * low_row, s_t * high_row]
-            steeps.append(steep)
-            weight_list.append(weights)
-        dkt[p] = dot(jnp.concatenate(turned_q, 1), jnp.concatenate(steeps, 0)).astype(BF16)
-        dvt[p] = dot(jnp.concatenate(turned_s, 1), jnp.concatenate(weight_list, 0)).astype(BF16)
+        weights = jnp.concatenate([e[b * pairs + p] for b in range(blocks)], 0)
+        values = jnp.concatenate([v_loc[p, local, :], v_rem[p]], 0)
+        slopes = dot_nt(jnp.concatenate(lefts, 0), values) - jnp.concatenate(deltas, 0)
+        steep = weights * slopes.astype(BF16)
+        return jnp.concatenate(turned_q, 1), jnp.concatenate(turned_s, 1), weights, steep
+
+    prepared = [prepare(p) for p in range(pairs)]
+    for p, (turned_q, turned_s, weights, steep) in enumerate(prepared):
+        keys = jnp.concatenate([k_loc[p, local, :], k_rem[p]], 0)
+        grad_q = dot(steep, keys)
+        for b in range(blocks):
+            one = grad_q[2 * b * shard : (2 * b + 1) * shard]
+            two = grad_q[(2 * b + 1) * shard : (2 * b + 2) * shard]
+            query_grads[b].append(jnp.where(low, one, two).astype(BF16))
+        dkt[p] = dot(turned_q, steep).astype(BF16)
+        dvt[p] = dot(turned_s, weights).astype(BF16)
     keys = dkt.shape[2]
     key_t = dkt[...].reshape(width, keys)
     value_t = dvt[...].reshape(width, keys)
@@ -397,35 +407,50 @@
     else:
         pack[...] = pack_a[...]
         pack[0:1, :] = pack_a[0:1, :] + gain
-        sib_part[0, shard:, :] = jnp.zeros((16, width), BF16)
-        sib_part[1, shard:, :] = jnp.concatenate(two_parts(pack[...]), 0)
         own_part[0] = pieces[0]
         far_part[0] = pieces[2].astype(BF16)
     sib_part[0, :shard] = pieces[1].astype(BF16)
     sib_part[1, :shard] = pieces[3].astype(BF16)
 
 
-def pack_small(ranks, grad_up, grad_down_t, lines, shx, shtx, drx, ulx, dlx, urx, pack):
-    mid, width = grad_up.shape
-    inner, outer = mid // ranks, width // ranks
-    spread, by_c, by_j, by_b, own_block = selectors(ranks, mid, width)
+def pack_small(ranks, grads, lines, mix, side, left, pack):
+    mid, width = grads.shape[0] // 2, grads.shape[1]
+    inner, outer, square = mid // ranks, width // ranks, ranks * ranks
+    line = iota((2 * square, width), 0)
+    line = line - ranks * block_of(line, ranks, 2 * ranks)
+    own_block = (line == block_of(iota((2 * square, width), 1), outer, ranks)).astype(F32)
+    factor = block_of(iota((2 * ranks, 2 * square), 1), ranks, 2 * ranks)
+    spread = (factor == iota((2 * ranks, 2 * square), 0)).astype(F32)
+    column = iota((outer, width), 1)
+    by_b = (column - outer * block_of(column, outer, ranks) == iota((outer, width), 0)).astype(F32)
+    group = block_of(iota((2 * ranks, 2 * mid), 1), inner, 2 * ranks)
+    by_c = (group == iota((2 * ranks, 2 * mid), 0)).astype(F32)
+    column = iota((2 * inner, 2 * mid), 1)
+    place = column - inner * block_of(column, inner, 2 * ranks) + inner * (column >= mid).astype(jnp.int32)
+    by_j = (place == iota((2 * inner, 2 * mid), 0)).astype(F32)
+    column = iota((2 * ranks, square), 1)
+    major = block_of(column, ranks, ranks)
+    minor = column - ranks * major
+    row = iota((2 * ranks, square), 0)
+    widen = jnp.where(row < ranks, (row == minor).astype(F32), (row - ranks == major).astype(F32))
+    column = iota((2 * square, square), 1)
+    major = block_of(column, ranks, ranks)
+    minor = column - ranks * major
+    row = iota((2 * square, square), 0)
+    inside = row - ranks * block_of(row, ranks, 2 * ranks)
+    keep = jnp.where(row < square, (inside == major).astype(F32), (inside == minor).astype(F32))
+    grads = grads[...]
+    product = dot_nt(left[...], grads)
+    ends = dot_nt(dot(spread, dot(mix[...] * side[...], grads) * own_block), by_b)
+    sides = dot_nt(dot(spread, product * mix[...]), by_j)
+    core = dot(spread, dot(dot_nt(product * side[...], by_c), widen) * keep)
     pack[...] = jnp.zeros(pack.shape, F32)
     pack[1:4, :] = lines[0:3, :]
-    down_t, up = grad_down_t[...], grad_up[...]
-    p_down = dot_nt(dlx[...], down_t)
-    p_up = dot_nt(urx[...], up)
-    left = dot_tn(spread, dot(shx[...] * drx[...], down_t) * own_block)
-    right = dot_tn(spread, dot(shtx[...] * ulx[...], up) * own_block)
-    pack[4:8, 0:outer] = dot_nt(left, by_b)
-    pack[4:8, 256 : 256 + outer] = dot_nt(right, by_b)
-    pack[4:8, 512 : 512 + inner] = dot_nt(dot_tn(spread, p_down * shx[...]), by_j)
-    pack[4:8, 640 : 640 + inner] = dot_nt(dot_tn(spread, p_up * shtx[...]), by_j)
-    shared_down = dot_nt(p_down * drx[...], by_c)
-    shared_up = dot_nt(p_up * ulx[...], by_c)
-    eye = (iota((ranks, ranks), 0) == iota((ranks, ranks), 1)).astype(F32)
-    for i, at in enumerate(shared_slots):
-        one = slice(i * ranks, (i + 1) * ranks)
-        pack[4:8, at : at + ranks] = shared_down[one] + dot_tn(shared_up[one], eye)
+    pack[4:8, 0:outer] = ends[:ranks]
+    pack[4:8, 256 : 256 + outer] = ends[ranks:]
+    pack[4:8, 512 : 512 + inner] = sides[:ranks, :inner]
+    pack[4:8, 640 : 640 + inner] = sides[ranks:, inner:]
+    pack[4:8, 704 : 704 + square] = core[:ranks] + core[ranks:]
 
 
 def norm_back(x, grad, hidden_grad, gain):
@@ -472,20 +497,8 @@
     ur[...] = pack[4:8, 256 : 256 + outer]
     dr[...] = pack[4:8, 512 : 512 + inner]
     ul[...] = pack[4:8, 640 : 640 + inner]
-    for i, at in enumerate(shared_slots):
-        shared[i] = pack[4:8, at : at + ranks]
-
-
-def two_parts(value):
-    high = value.astype(BF16)
-    return high, (value - high.astype(F32)).astype(BF16)
-
-
-def sum_kernel(pack, from_sib, total):
-    shard = from_sib.shape[1] - 16
-    high, low = two_parts(pack[...])
-    theirs = from_sib[1, shard:, :].astype(F32)
-    total[...] = (high.astype(F32) + low.astype(F32)) + (theirs[0:8] + theirs[8:16])
+    for k in range(ranks):
+        shared[:, k, :] = pack[4:8, 704 + k * ranks : 704 + (k + 1) * ranks]
 
 
 def exchange(value, axis, bit):
@@ -506,7 +519,7 @@
     pairs, tokens, keys = heads // 2, rows * shard, shard * parts
     lanes = width // pairs
     inner, outer, square = mid // ranks, width // ranks, ranks * ranks
-    padded = shard + 16
+    padded = shard + 8
 
     own, a_send, b_send, cot_send = call(
         pick_kernel,
@@ -530,7 +543,7 @@
     tiles, down_t, up, *expanded = call(
         functools.partial(setup_kernel, shard, parts),
         [((2 * parts - 1, pairs, 2 * shard, shard), F32), ((mid, width), BF16), ((mid, width), BF16)]
-        + [((square, mid), F32)] * 4 + [((square, width), F32)] * 2
+        + [((2 * square, 2 * mid), F32)] * 2 + [((2 * square, width), F32)]
         + [(x.shape, x.dtype) for x in small[7:] + large],
         [Far(x) for x in small + large],
         8,
@@ -539,8 +552,8 @@
         + [(x.shape, x.dtype) for x in small[:7]],
         len(small) + len(large),
     )
-    bd, bu, gain1, gain2, wq, wk, wv, wo, win, wout = expanded[6:]
-    expanded = expanded[:6]
+    bd, bu, gain1, gain2, wq, wk, wv, wo, win, wout = expanded[3:]
+    expanded = expanded[:3]
     k_loc, v_loc, q_loc = call(
         local_kernel,
         [((pairs, 4 * shard, lanes), BF16), ((pairs, 4 * shard, lanes), BF16), ((pairs, 2 * shard, lanes), BF16)],
@@ -574,11 +587,11 @@
         12,
         3.0,
     )
-    out, hidden_grad, dctx, grad_up, grad_down_t, lines = call(
+    out, hidden_grad, dctx, adapter_grad, lines = call(
         middle_kernel,
         [
             ((rows, shard, width), BF16), ((tokens, width), F32), ((pairs, tokens, lanes), BF16),
-            ((mid, width), F32), ((mid, width), F32), ((8, width), F32),
+            ((2 * mid, width), F32), ((8, width), F32),
         ],
         (
             hid_a, hid_b, cotangent, cot_far, win, wout, wo, gain2, bd, bu, down_t, up,
@@ -593,7 +606,7 @@
         [((2, shard, width), F32), ((2, shard, width), BF16), ((8, width), F32)],
         (
             own, sib, a_far, a_far_sib, dctx, ctx_a, rinv_a, ea, k_loc, v_loc, q_loc, ka, va, qa,
-            wq, wk, wv, grad_up, grad_down_t, lines, *expanded,
+            wq, wk, wv, adapter_grad, lines, *expanded,
         ),
         14,
         6.0,
@@ -602,7 +615,7 @@
     sib_a = exchange(sib_part_a, "seq", 1)
     part_b, far_part, sib_part_b, pack = call(
         functools.partial(backward_kernel, False, ranks),
-        [((1, shard, width), F32), ((1, shard, width), BF16), ((2, padded, width), BF16), ((8, width), F32)],
+        [((1, shard, width), F32), ((1, shard, width), BF16), ((2, shard, width), BF16), ((8, width), F32)],
         (
             own, sib, b_far, b_far_sib, dctx, ctx_b, rinv_b, eb, k_loc, v_loc, q_loc, kb, vb,
             wq, wk, wv, pack_a,
@@ -613,7 +626,7 @@
     )
     sib_part_b, sib_a = lax.optimization_barrier((sib_part_b, sib_a))
     sib_b = exchange(sib_part_b, "seq", 1)
-    (pack,) = call(sum_kernel, [((8, width), F32)], (pack, sib_b), 8, 0.1)
+    pack = pack + exchange(pack, "seq", 1)
     (back,) = call(
         return_kernel,
         [((rows, shard, width), BF16)],

time: 66.3 us -> 63.5 us (0.958)
  Pallas kernels: 39.7 us -> 37.4 us
  waiting for transfers between devices: 12 us -> 10.9 us
    pallas_call x12 -> x11, Pallas kernels: 39.7 us -> 37.4 us  [call(): pl.pallas_call(kernel, out_shape=[made(shape, kind) for shape, kind in ou...]
    ppermute x13 -> x14, waiting for transfers between devices: 12 us -> 10.9 us  [exchange(): return lax.ppermute(value, axis, [(k, k ^ bit) for k in range(count)])]
    ppermute x13 -> x14, starting transfers between devices: 13.6 us -> 14.1 us  [exchange(): return lax.ppermute(value, axis, [(k, k ^ bit) for k in range(count)])]
  transfers between devices with their start and end apart: 13 -> 14, of which waited for: 7 -> 7; matrix products, arithmetic and copies ran while one was open for 0% -> 0% of each run, Pallas kernels for 29% -> 29%
where the time goes in v3:
time: 63.5 us; the launch traced here: 63.3 us
  Pallas kernels  37.4 us (59%)
  starting transfers between devices  14.1 us (22%)
  waiting for transfers between devices  10.9 us (17%)
  between operations  0.78 us (1%)
    pallas_call x11, Pallas kernels, call(): pl.pallas_call(kernel, out_shape=[made(shape, kind) for shape, kind in ou...  37.4 us
    ppermute x14, starting transfers between devices, exchange(): return lax.ppermute(value, axis, [(k, k ^ bit) for k in range(count)])  14.1 us
    ppermute x14, waiting for transfers between devices, exchange(): return lax.ppermute(value, axis, [(k, k ^ bit) for k in range(count)])  10.9 us
  transfers between devices with their start and end apart: 14, of which 7 were waited for; matrix products, arithmetic and copies ran while one was open for 0% of the time, Pallas kernels for 29%

profile of v3, /device:TPU:0, one launch (start us, length us, event | category | flops | bytes accessed | tf_op | source)
XLA Modules:
  0.0 63.3 jit_solution(7470133971323081544)
XLA Ops:
  0.6 1.3 %shard_map.275 = (bf16[2,136,768]{2,1,0:T(8,128)(2,1)S(1)}, bf16[1,136,768]{2,1,0:T(8,128)(2,1)S(1)}, bf16[1,136,768]{2,1,0:T(8,128)(2,1)S(1)}, bf16[1,128,768]{2,1,0:T(8,128)(2,1)S(1)}) custom-call(bf16[3,128,768]{2,1,0:T(8,128)(2,1)} %inputs.1, bf16[3,128,768]{2,1,0:T(8,128)(2,1)} %cot.1, s32[3,128]{1,0:T(4,128)} %segment_ids.1), custom_call_target="tpu_custom_call" | custom-call | flops 1100000000 | tf_op jit(solution)/shard_map/pallas_call | solution.py:72
  2.0 0.5 collective-permute-start
  2.5 2.6 %collective-permute-start.1 = (bf16[1,136,768]{2,1,0:T(8,128)(2,1)S(1)}, bf16[1,136,768]{2,1,0:T(8,128)(2,1)S(1)}, u32[]{:S(2)}, u32[]{:S(2)}) collective-permute-start(bf16[1,136,768]{2,1,0:T(8,128)(2,1)S(1)} %get-tuple-element.77), channel_id=1, source_target_pairs={{0,16},{8,24},{16,0},{24,8},{1,17},{9,25},{17,1},{25,9},{2,18},{10... | collective-permute-start | bytes 626696 | tf_op jit(solution)/shard_map/ppermute | solution.py:506
  5.1 0.1 collective-permute-start.3
  5.2 5.4 %shard_map.276 = (f32[7,6,256,128]{3,2,1,0:T(8,128)S(1)}, bf16[48,768]{1,0:T(8,128)(2,1)S(1)}, bf16[48,768]{1,0:T(8,128)(2,1)S(1)}, f32[32,96]{1,0:T(8,128)S(1)}...) custom-call(s32[1023]{0:T(1024)} %table_far.1, ...), custom_call_target="tpu_custom_call" | custom-call | flops 4400000000 | tf_op jit(solution)/shard_map/pallas_call | solution.py:72
  10.6 0.0 collective-permute-done.sib
  10.6 1.9 %shard_map.277 = (bf16[6,512,128]{2,1,0:T(8,128)(2,1)S(1)}, bf16[6,512,128]{2,1,0:T(8,128)(2,1)S(1)}, bf16[6,256,128]{2,1,0:T(8,128)(2,1)S(1)}) custom-call(bf16[2,136,768]{2,1,0:T(8,128)(2,1)S(1)} %get-tuple-element.76.own, bf16[2,136,768]{2,1,0:T(8,128)(2,1)S(1)} %collective-permute-done.sib, bf16[768,768]{1,0:T(8,128)(2,1)S(1)} %get-tuple-element.78.wq.rest_1_.rest_0_, ...), custom_call_target="tpu_custom_call" | custom-call | flops 2200000000 | tf_op jit(solution)/shard_map/pallas_call | solution.py:72
  12.5 0.0 collective-permute-done.1.far
  12.5 0.2 collective-permute-start.2
  12.6 1.9 %collective-permute-start.5 = (bf16[1,128,768]{2,1,0:T(8,128)(2,1)S(1)}, bf16[1,128,768]{2,1,0:T(8,128)(2,1)S(1)}, u32[]{:S(2)}, u32[]{:S(2)}) collective-permute-start(bf16[1,128,768]{2,1,0:T(8,128)(2,1)S(1)} %get-tuple-element.94), channel_id=1, source_target_pairs={{0,16},{8,24},{16,0},{24,8},{1,17},{9,25},{17,1},{25,9},{2,18},{10... | collective-permute-start | bytes 589832 | tf_op jit(solution)/shard_map/ppermute | solution.py:506
  14.6 0.8 %collective-permute-done.3.far = bf16[1,136,768]{2,1,0:T(8,128)(2,1)S(1)} collective-permute-done((bf16[1,136,768]{2,1,0:T(8,128)(2,1)S(1)}, bf16[1,136,768]{2,1,0:T(8,128)(2,1)S(1)}, u32[]{:S(2)}, u32[]{:S(2)}) %collective-permute-start.3) | collective-permute-done | bytes 208928 | tf_op jit(solution)/shard_map/ppermute | solution.py:506
  15.3 0.0 collective-permute-done.2.far_sib
  15.3 0.0 collective-permute-start.4
  15.3 3.9 %shard_map.278 = (bf16[6,256,128]{2,1,0:T(8,128)(2,1)S(1)}, bf16[6,256,128]{2,1,0:T(8,128)(2,1)S(1)}, bf16[6,128,128]{2,1,0:T(8,128)(2,1)S(1)}, bf16[12,256,512]...) custom-call(bf16[2,136,768]{2,1,0:T(8,128)(2,1)S(1)} %get-tuple-element.76., ...), custom_call_target="tpu_custom_call" | custom-call | flops 3300000000 | tf_op jit(solution)/shard_map/pallas_call | solution.py:72
  19.2 0.0 copy-start
  19.3 0.0 collective-permute-done.4.far_sib
  19.3 2.4 %shard_map.279 = (bf16[6,256,128]{2,1,0:T(8,128)(2,1)S(1)}, bf16[6,256,128]{2,1,0:T(8,128)(2,1)S(1)}, bf16[6,256,512]{2,1,0:T(8,128)(2,1)S(1)}, f32[6,128,128]{2...) custom-call(bf16[2,136,768]{2,1,0:T(8,128)(2,1)S(1)} %get-tuple-element.76.own, ...), custom_call_target="tpu_custom_call" | custom-call | flops 3300000000 | tf_op jit(solution)/shard_map/pallas_call | solution.py:72
  21.7 0.0 collective-permute-done.5.cot_far
  21.7 0.0 copy-done
  21.7 11.4 %shard_map.280 = (bf16[3,128,768]{2,1,0:T(8,128)(2,1)S(1)}, f32[384,768]{1,0:T(8,128)S(1)}, bf16[6,384,128]{2,1,0:T(8,128)(2,1)S(1)}, f32[96,768]{1,0:T(8,128)S(1)}, f32[8,768]{1,0:T(8,128)S(1)}) custom-call(f32[256,768]{1,0:T(8,128)S(1)} %get-tuple-element.91.hid_a, f32[128,768]{1,0:T(8,128)S(1)} %get-tuple-element.93.hid_b, ...), custom_call_target="tpu_custom_call" | custom-call | flops 13200000000 | tf_op jit(solution)/shard_map/pallas_call | solution.py:72
  33.1 5.2 %shard_map.281 = (f32[2,128,768]{2,1,0:T(8,128)S(1)}, bf16[2,128,768]{2,1,0:T(8,128)(2,1)S(1)}, f32[8,768]{1,0:T(8,128)S(1)}) custom-call(bf16[2,136,768]{2,1,0:T(8,128)(2,1)S(1)} %get-tuple-element.76.own, bf16[2,136,768]{2,1,0:T(8,128)(2,1)S(1)} %collective-permute-done.sib, bf16[1,136,768]{2,1,0:T(8,128)(2,1)S(1)} %collective-permute-done.1.far, ...), custom_call_target="tpu_custom_call" | custom-call | flops 6600000000 | tf_op jit(solution)/shard_map/pallas_call | solution.py:72
  38.3 0.6 collective-permute-start.6
  38.9 3.5 %shard_map.282 = (f32[1,128,768]{2,1,0:T(8,128)S(1)}, bf16[1,128,768]{2,1,0:T(8,128)(2,1)S(1)}, bf16[2,128,768]{2,1,0:T(8,128)(2,1)S(1)}, f32[8,768]{1,0:T(8,128)S(1)}) custom-call(bf16[2,136,768]{2,1,0:T(8,128)(2,1)S(1)} %get-tuple-element.76.own, bf16[2,136,768]{2,1,0:T(8,128)(2,1)S(1)} %collective-permute-done.sib, ...), custom_call_target="tpu_custom_call" | custom-call | flops 3960000000 | tf_op jit(solution)/shard_map/pallas_call | solution.py:72
  42.4 0.0 collective-permute-done.6.from_sib.sib_a
  42.4 0.1 collective-permute-start.7
  42.5 0.5 collective-permute-start.8
  43.0 1.2 %collective-permute-done.8 = f32[8,768]{1,0:T(8,128)S(1)} collective-permute-done((f32[8,768]{1,0:T(8,128)S(1)}, f32[8,768]{1,0:T(8,128)S(1)}, u32[]{:S(2)}, u32[]{:S(2)}) %collective-permute-start.8) | collective-permute-done | bytes 24608 | tf_op jit(solution)/shard_map/ppermute | solution.py:506
  44.2 0.0 collective-permute-done.7.from_sib_b.sib_b
  44.2 0.3 shard_map.283
  44.5 1.8 %collective-permute-start.9 = (bf16[3,128,768]{2,1,0:T(8,128)(2,1)S(1)}, bf16[3,128,768]{2,1,0:T(8,128)(2,1)S(1)}, u32[]{:S(2)}, u32[]{:S(2)}) collective-permute-start(bf16[3,128,768]{2,1,0:T(8,128)(2,1)S(1)} %shard_map.283), channel_id=1, source_target_pairs={{0,16},{8,24},{16,0},{24,8},{1,17},{9,25},{17,1},{25,9},{2,18},{10... | collective-permute-start | bytes 1769480 | tf_op jit(solution)/shard_map/ppermute | solution.py:506
  46.4 1.5 %collective-permute-start.10 = (f32[8,768]{1,0:T(8,128)S(1)}, f32[8,768]{1,0:T(8,128)S(1)}, u32[]{:S(2)}, u32[]{:S(2)}) collective-permute-start(f32[8,768]{1,0:T(8,128)S(1)} %add.12._), channel_id=1, source_target_pairs={{0,1},{1,0},{2,3},{3,2},{4,5},{5,4},{6,7},{7,6},{8,9},{9,8},{10,11... | collective-permute-start | bytes 73736 | tf_op jit(solution)/shard_map/ppermute | solution.py:506
  47.9 2.3 %collective-permute-done.10 = f32[8,768]{1,0:T(8,128)S(1)} collective-permute-done((f32[8,768]{1,0:T(8,128)S(1)}, f32[8,768]{1,0:T(8,128)S(1)}, u32[]{:S(2)}, u32[]{:S(2)}) %collective-permute-start.10) | collective-permute-done | bytes 24608 | tf_op jit(solution)/shard_map/ppermute | solution.py:506
  50.2 1.6 %collective-permute-start.11 = (f32[8,768]{1,0:T(8,128)S(1)}, f32[8,768]{1,0:T(8,128)S(1)}, u32[]{:S(2)}, u32[]{:S(2)}) collective-permute-start(f32[8,768]{1,0:T(8,128)S(1)} %add.13), channel_id=1, source_target_pairs={{0,2},{1,3},{2,0},{3,1},{4,6},{5,7},{6,4},{7,5},{8,10},{9,11},{10,... | collective-permute-start | bytes 73736 | tf_op jit(solution)/shard_map/ppermute | solution.py:506
  51.8 2.3 %collective-permute-done.11 = f32[8,768]{1,0:T(8,128)S(1)} collective-permute-done((f32[8,768]{1,0:T(8,128)S(1)}, f32[8,768]{1,0:T(8,128)S(1)}, u32[]{:S(2)}, u32[]{:S(2)}) %collective-permute-start.11) | collective-permute-done | bytes 24608 | tf_op jit(solution)/shard_map/ppermute | solution.py:506
  54.0 2.6 %collective-permute-start.12 = (f32[8,768]{1,0:T(8,128)S(1)}, f32[8,768]{1,0:T(8,128)S(1)}, u32[]{:S(2)}, u32[]{:S(2)}) collective-permute-start(f32[8,768]{1,0:T(8,128)S(1)} %add.14), channel_id=1, source_target_pairs={{0,4},{1,5},{2,6},{3,7},{4,0},{5,1},{6,2},{7,3},{8,12},{9,13},{10,... | collective-permute-start | bytes 73736 | tf_op jit(solution)/shard_map/ppermute | solution.py:506
  56.6 2.2 %collective-permute-done.12 = f32[8,768]{1,0:T(8,128)S(1)} collective-permute-done((f32[8,768]{1,0:T(8,128)S(1)}, f32[8,768]{1,0:T(8,128)S(1)}, u32[]{:S(2)}, u32[]{:S(2)}) %collective-permute-start.12) | collective-permute-done | bytes 24608 | tf_op jit(solution)/shard_map/ppermute | solution.py:506
  58.8 0.3 collective-permute-start.13
  59.0 1.2 %collective-permute-done.9.returned = bf16[3,128,768]{2,1,0:T(8,128)(2,1)S(1)} collective-permute-done((bf16[3,128,768]{2,1,0:T(8,128)(2,1)S(1)}, bf16[3,128,768]{2,1,0:T(8,128)(2,1)S(1)}, u32[]{:S(2)}, u32[]{:S(2)}) %collective-permute-start.9) | collective-permute-done | bytes 589856 | tf_op jit(solution)/shard_map/ppermute | solution.py:506
  60.3 1.4 %shard_map.284 = (bf16[3,128,768]{2,1,0:T(8,128)(2,1)}, bf16[3,128,768]{2,1,0:T(8,128)(2,1)}) custom-call(bf16[2,136,768]{2,1,0:T(8,128)(2,1)S(1)} %get-tuple-element.76.own, f32[2,128,768]{2,1,0:T(8,128)S(1)} %get-tuple-element.114.own_part.part_a, bf16[2,128,768]{2,1,0:T(8,128)(2,1)S(1)} %collective-permute-done.6.from_sib.sib_a, ...), custom_call_target="tpu_custom_call" | custom-call | flops 1100000000 | tf_op jit(solution)/shard_map/pallas_call | solution.py:72
  61.7 0.9 %collective-permute-done.13.far_pack = f32[8,768]{1,0:T(8,128)S(1)} collective-permute-done((f32[8,768]{1,0:T(8,128)S(1)}, f32[8,768]{1,0:T(8,128)S(1)}, u32[]{:S(2)}, u32[]{:S(2)}) %collective-permute-start.13) | collective-permute-done | bytes 24608 | tf_op jit(solution)/shard_map/ppermute | solution.py:506
  62.6 0.7 %shard_map.285 = (f32[768]{0:T(1024)}, f32[768]{0:T(1024)}, f32[4,4,4]{2,1,0:T(4,128)}, f32[4,192]{1,0:T(4,128)}, f32[4,12]{1,0:T(4,128)}, /*index=5*/f32[4,12]{...) custom-call(f32[8,768]{1,0:T(8,128)S(1)} %add.15.near_pack, f32[8,768]{1,0:T(8,128)S(1)} %collective-permute-done.13.far_pack, ...), custom_call_target="tpu_custom_call" | custom-call | flops 550000000 | tf_op jit(solution)/shard_map/pallas_call | solution.py:72
  (4 shorter events, 0.0 us)
Async XLA Ops:
  2.0 8.6 %collective-permute-start = (bf16[2,136,768]{2,1,0:T(8,128)(2,1)S(1)}, bf16[2,136,768]{2,1,0:T(8,128)(2,1)S(1)}, u32[]{:S(2)}, u32[]{:S(2)}) collective-permute-start(bf16[2,136,768]{2,1,0:T(8,128)(2,1)S(1)} %get-tuple-element.76.own), channel_id=1, source_target_pairs={{0,8},{8,0},{16,24},{24,16},{1,9},{9,1},{17,25},{25,17},{2,10},{10... | collective-permute-start | bytes 1253384 | tf_op jit(solution)/shard_map/ppermute | solution.py:506
  2.5 10.0 %collective-permute-start.1 = (bf16[1,136,768]{2,1,0:T(8,128)(2,1)S(1)}, bf16[1,136,768]{2,1,0:T(8,128)(2,1)S(1)}, u32[]{:S(2)}, u32[]{:S(2)}) collective-permute-start(bf16[1,136,768]{2,1,0:T(8,128)(2,1)S(1)} %get-tuple-element.77), channel_id=1, source_target_pairs={{0,16},{8,24},{16,0},{24,8},{1,17},{9,25},{17,1},{25,9},{2,18},{10... | collective-permute-start | bytes 626696 | tf_op jit(solution)/shard_map/ppermute | solution.py:506
  5.1 10.2 %collective-permute-start.3 = (bf16[1,136,768]{2,1,0:T(8,128)(2,1)S(1)}, bf16[1,136,768]{2,1,0:T(8,128)(2,1)S(1)}, u32[]{:S(2)}, u32[]{:S(2)}) collective-permute-start(bf16[1,136,768]{2,1,0:T(8,128)(2,1)S(1)} %get-tuple-element.84), channel_id=1, source_target_pairs={{0,16},{8,24},{16,0},{24,8},{1,17},{9,25},{17,1},{25,9},{2,18},{10... | collective-permute-start | bytes 626696 | tf_op jit(solution)/shard_map/ppermute | solution.py:506
  12.5 2.9 %collective-permute-start.2 = (bf16[1,136,768]{2,1,0:T(8,128)(2,1)S(1)}, bf16[1,136,768]{2,1,0:T(8,128)(2,1)S(1)}, u32[]{:S(2)}, u32[]{:S(2)}) collective-permute-start(bf16[1,136,768]{2,1,0:T(8,128)(2,1)S(1)} %collective-permute-done.1.far), channel_id=1, source_target_pairs={{0,8},{8,0},{16,24},{24,16},{1,9},{9,1},{17,25},{25,17},{2,10},{10... | collective-permute-start | bytes 626696 | tf_op jit(solution)/shard_map/ppermute | solution.py:506
  12.6 9.1 %collective-permute-start.5 = (bf16[1,128,768]{2,1,0:T(8,128)(2,1)S(1)}, bf16[1,128,768]{2,1,0:T(8,128)(2,1)S(1)}, u32[]{:S(2)}, u32[]{:S(2)}) collective-permute-start(bf16[1,128,768]{2,1,0:T(8,128)(2,1)S(1)} %get-tuple-element.94), channel_id=1, source_target_pairs={{0,16},{8,24},{16,0},{24,8},{1,17},{9,25},{17,1},{25,9},{2,18},{10... | collective-permute-start | bytes 589832 | tf_op jit(solution)/shard_map/ppermute | solution.py:506
  15.3 3.9 %collective-permute-start.4 = (bf16[1,136,768]{2,1,0:T(8,128)(2,1)S(1)}, bf16[1,136,768]{2,1,0:T(8,128)(2,1)S(1)}, u32[]{:S(2)}, u32[]{:S(2)}) collective-permute-start(bf16[1,136,768]{2,1,0:T(8,128)(2,1)S(1)} %collective-permute-done.3.far), channel_id=1, source_target_pairs={{0,8},{8,0},{16,24},{24,16},{1,9},{9,1},{17,25},{25,17},{2,10},{10... | collective-permute-start | bytes 626696 | tf_op jit(solution)/shard_map/ppermute | solution.py:506
  19.2 2.5 %copy-start = (bf16[3,128,768]{2,1,0:T(8,128)(2,1)S(1)}, bf16[3,128,768]{2,1,0:T(8,128)(2,1)}, u32[]{:S(2)}) copy-start(bf16[3,128,768]{2,1,0:T(8,128)(2,1)} %cot.1) | copy-start | bytes 1769476
  38.3 4.0 %collective-permute-start.6 = (bf16[2,128,768]{2,1,0:T(8,128)(2,1)S(1)}, bf16[2,128,768]{2,1,0:T(8,128)(2,1)S(1)}, u32[]{:S(2)}, u32[]{:S(2)}) collective-permute-start(bf16[2,128,768]{2,1,0:T(8,128)(2,1)S(1)} %get-tuple-element.122), channel_id=1, source_target_pairs={{0,8},{8,0},{16,24},{24,16},{1,9},{9,1},{17,25},{25,17},{2,10},{10... | collective-permute-start | bytes 1179656 | tf_op jit(solution)/shard_map/ppermute | solution.py:506
  42.4 1.8 %collective-permute-start.7 = (bf16[2,128,768]{2,1,0:T(8,128)(2,1)S(1)}, bf16[2,128,768]{2,1,0:T(8,128)(2,1)S(1)}, u32[]{:S(2)}, u32[]{:S(2)}) collective-permute-start(bf16[2,128,768]{2,1,0:T(8,128)(2,1)S(1)} %get-tuple-element.125), channel_id=1, source_target_pairs={{0,8},{8,0},{16,24},{24,16},{1,9},{9,1},{17,25},{25,17},{2,10},{10... | collective-permute-start | bytes 1179656 | tf_op jit(solution)/shard_map/ppermute | solution.py:506
  42.5 1.7 %collective-permute-start.8 = (f32[8,768]{1,0:T(8,128)S(1)}, f32[8,768]{1,0:T(8,128)S(1)}, u32[]{:S(2)}, u32[]{:S(2)}) collective-permute-start(f32[8,768]{1,0:T(8,128)S(1)} %get-tuple-element.126), channel_id=1, source_target_pairs={{0,8},{8,0},{16,24},{24,16},{1,9},{9,1},{17,25},{25,17},{2,10},{10... | collective-permute-start | bytes 73736 | tf_op jit(solution)/shard_map/ppermute | solution.py:506
  44.5 15.7 %collective-permute-start.9 = (bf16[3,128,768]{2,1,0:T(8,128)(2,1)S(1)}, bf16[3,128,768]{2,1,0:T(8,128)(2,1)S(1)}, u32[]{:S(2)}, u32[]{:S(2)}) collective-permute-start(bf16[3,128,768]{2,1,0:T(8,128)(2,1)S(1)} %shard_map.283), channel_id=1, source_target_pairs={{0,16},{8,24},{16,0},{24,8},{1,17},{9,25},{17,1},{25,9},{2,18},{10... | collective-permute-start | bytes 1769480 | tf_op jit(solution)/shard_map/ppermute | solution.py:506
  46.4 3.8 %collective-permute-start.10 = (f32[8,768]{1,0:T(8,128)S(1)}, f32[8,768]{1,0:T(8,128)S(1)}, u32[]{:S(2)}, u32[]{:S(2)}) collective-permute-start(f32[8,768]{1,0:T(8,128)S(1)} %add.12._), channel_id=1, source_target_pairs={{0,1},{1,0},{2,3},{3,2},{4,5},{5,4},{6,7},{7,6},{8,9},{9,8},{10,11... | collective-permute-start | bytes 73736 | tf_op jit(solution)/shard_map/ppermute | solution.py:506
  50.2 3.8 %collective-permute-start.11 = (f32[8,768]{1,0:T(8,128)S(1)}, f32[8,768]{1,0:T(8,128)S(1)}, u32[]{:S(2)}, u32[]{:S(2)}) collective-permute-start(f32[8,768]{1,0:T(8,128)S(1)} %add.13), channel_id=1, source_target_pairs={{0,2},{1,3},{2,0},{3,1},{4,6},{5,7},{6,4},{7,5},{8,10},{9,11},{10,... | collective-permute-start | bytes 73736 | tf_op jit(solution)/shard_map/ppermute | solution.py:506
  54.0 4.7 %collective-permute-start.12 = (f32[8,768]{1,0:T(8,128)S(1)}, f32[8,768]{1,0:T(8,128)S(1)}, u32[]{:S(2)}, u32[]{:S(2)}) collective-permute-start(f32[8,768]{1,0:T(8,128)S(1)} %add.14), channel_id=1, source_target_pairs={{0,4},{1,5},{2,6},{3,7},{4,0},{5,1},{6,2},{7,3},{8,12},{9,13},{10,... | collective-permute-start | bytes 73736 | tf_op jit(solution)/shard_map/ppermute | solution.py:506
  58.8 3.8 %collective-permute-start.13 = (f32[8,768]{1,0:T(8,128)S(1)}, f32[8,768]{1,0:T(8,128)S(1)}, u32[]{:S(2)}, u32[]{:S(2)}) collective-permute-start(f32[8,768]{1,0:T(8,128)S(1)} %add.15.near_pack), channel_id=1, source_target_pairs={{0,16},{8,24},{16,0},{24,8},{1,17},{9,25},{17,1},{25,9},{2,18},{10... | collective-permute-start | bytes 73736 | tf_op jit(solution)/shard_map/ppermute | solution.py:506

commit v4 on v3

--- a/solution.py
+++ b/solution.py
@@ -115,15 +115,15 @@
 
 def setup_kernel(
     shard, parts, table_far, position_far, shared_far, dl_far, dr_far, ul_far, ur_far, bd_far, bu_far, g1_far, g2_far,
-    wq_far, wk_far, wv_far, wo_far, win_far, wout_far,
-    tiles, down_t, up, mix, side, left, bd, bu, g1, g2, wq, wk, wv, wo, win, wout,
+    wq_far, wk_far, wv_far, wo_far, wout_far,
+    tiles, down_t, up, mix, side, left, bd, bu, g1, g2, wq, wk, wv, wo, wout,
     tab, sh16, sh16t, table, position_bias, shared, dl, dr, ul, ur, sems,
 ):
     started = start_copies(
         [
             (table_far, table), (position_far, position_bias), (shared_far, shared), (dl_far, dl), (dr_far, dr),
             (ul_far, ul), (ur_far, ur), (bd_far, bd), (bu_far, bu), (g1_far, g1), (g2_far, g2),
-            (wq_far, wq), (wk_far, wk), (wv_far, wv), (wo_far, wo), (win_far, win), (wout_far, wout),
+            (wq_far, wq), (wk_far, wk), (wv_far, wv), (wo_far, wo), (wout_far, wout),
         ],
         sems,
     )
@@ -226,15 +226,17 @@
 
 def attention_kernel(
     is_moved, own, sib, far, far_sib, k_loc, v_loc, q_loc, tiles,
-    wq, wk, wv, wo, gain, k_rem, v_rem, *rest,
+    wq, wk, wv, wo, gain, *rest,
 ):
-    pairs, _, lanes = k_rem.shape
+    pairs, _, lanes = k_loc.shape
     shard = q_loc.shape[1] // 2
     if is_moved:
-        q_rem, e, ctx, rinv, hid = rest
+        win_far, k_rem, v_rem, q_rem, e, ctx, rinv, hid, win, sems = rest
+        fetches = start_copies([(win_far, win)], sems)
         first, queries = 0, [0, 2]
     else:
-        e, ctx, rinv, hid = rest
+        k_rem, v_rem, e, ctx, rinv, hid = rest
+        fetches = []
         first, queries = 1, [0]
     place = lax.axis_index("seq")
     parts = lax.axis_size("seq")
@@ -281,11 +283,13 @@
     context = jnp.concatenate([jnp.concatenate(c, 1) for c in contexts], 0)
     x = jnp.concatenate([own[first, :shard]] + ([far[0, :shard]] if is_moved else []), 0).astype(F32)
     hid[...] = x + dot(context, wo[...])
+    for one in fetches:
+        one.wait()
 
 
 def middle_kernel(
     hid_a, hid_b, cot, cot_far, win, wout, wo, gain2, bd, bu, down_t, up,
-    out, hidden_grad, dctx, adapter_grad, lines, low, act, gslope,
+    out, out_send, hidden_grad, dctx, adapter_grad, lines, low, act, gslope,
 ):
     rows, shard, width = cot.shape
     hidden = win.shape[1]
@@ -312,6 +316,7 @@
     result = state + branch + dot(g_low, up[...]) + bu[...][None, :]
     for b in range(rows):
         out[b] = result[b * shard : (b + 1) * shard].astype(BF16)
+    out_send[0] = result[shard : 2 * shard].astype(BF16)
     mid = g.shape[1]
     adapter_grad[:mid, :] = dot_tn(gb_low, branch_low)
     adapter_grad[mid:, :] = dot_tn(g_low, up_low)
@@ -461,27 +466,26 @@
     return hidden_grad + inv * (c - hat * jnp.mean(hat * c, -1, keepdims=True))
 
 
-def return_kernel(_, far, own_part, from_sib, far_part, from_sib_b, out, hidden_grad, gain, result):
-    shard = out.shape[1]
-    result[0] = (far_part[0].astype(F32) + from_sib_b[1, :shard].astype(F32)).astype(BF16)
-    result[1] = out[1]
+def return_kernel(far, own_part, from_sib, far_part, from_sib_b, hidden_grad, gain, far_sum, back):
+    shard = back.shape[1]
+    far_sum[0] = (far_part[0].astype(F32) + from_sib_b[1, :shard].astype(F32)).astype(BF16)
     grad = own_part[1] + from_sib[1].astype(F32)
-    result[2] = norm_back(far[0, :shard], grad, hidden_grad[shard : 2 * shard, :], gain).astype(BF16)
+    back[0] = norm_back(far[0, :shard], grad, hidden_grad[shard : 2 * shard, :], gain).astype(BF16)
 
 
 def last_kernel(
-    own, part_a, sib_a, part_b, sib_b, returned, hidden_grad, gain, out, output, grad_input
+    own, part_a, sib_a, part_b, sib_b, far_sum, hidden_grad, gain, out, out_far, back, output, grad_input
 ):
     rows, shard, width = out.shape
     row = moved_row(rows)
     other = rows - 1 - row
     output[row] = out[0]
     output[1] = out[2]
-    output[other] = returned[1]
-    grad_input[other] = returned[2]
+    output[other] = out_far[0]
+    grad_input[other] = back[0]
     grad = part_a[0] + sib_a[0].astype(F32)
     grad_input[row] = norm_back(own[0, :shard], grad, hidden_grad[0:shard, :], gain).astype(BF16)
-    grad = part_b[0] + sib_b[0, :shard].astype(F32) + returned[0].astype(F32)
+    grad = part_b[0] + sib_b[0].astype(F32) + far_sum[0].astype(F32)
     grad_input[1] = norm_back(own[1, :shard], grad, hidden_grad[2 * shard :, :], gain).astype(BF16)
 
 
@@ -501,6 +505,10 @@
         shared[:, k, :] = pack[4:8, 704 + k * ranks : 704 + (k + 1) * ranks]
 
 
+def add_kernel(a, b, c):
+    c[...] = a[...] + b[...]
+
+
 def exchange(value, axis, bit):
     count = lax.axis_size(axis)
     return lax.ppermute(value, axis, [(k, k ^ bit) for k in range(count)])
@@ -539,7 +547,7 @@
         bucket_table, jnp.transpose(position_bias), shared, down_left, down_right, up_left_vectors, up_right,
         bias_down, bias_up, gain_first, gain_second,
     )
-    large = (query_weight, key_weight, value_weight, out_weight, hidden_in, hidden_out)
+    large = (query_weight, key_weight, value_weight, out_weight, hidden_out)
     tiles, down_t, up, *expanded = call(
         functools.partial(setup_kernel, shard, parts),
         [((2 * parts - 1, pairs, 2 * shard, shard), F32), ((mid, width), BF16), ((mid, width), BF16)]
@@ -547,19 +555,19 @@
         + [(x.shape, x.dtype) for x in small[7:] + large],
         [Far(x) for x in small + large],
         8,
-        4.0,
+        20.0,
         [((16, 2 * keys), F32), ((square, ranks), F32), ((square, ranks), F32)]
         + [(x.shape, x.dtype) for x in small[:7]],
         len(small) + len(large),
     )
-    bd, bu, gain1, gain2, wq, wk, wv, wo, win, wout = expanded[3:]
+    bd, bu, gain1, gain2, wq, wk, wv, wo, wout = expanded[3:]
     expanded = expanded[:3]
     k_loc, v_loc, q_loc = call(
         local_kernel,
         [((pairs, 4 * shard, lanes), BF16), ((pairs, 4 * shard, lanes), BF16), ((pairs, 2 * shard, lanes), BF16)],
         (own, sib, wq, wk, wv, gain1),
         8,
-        2.0,
+        20.0,
     )
     a_far, k_loc = lax.optimization_barrier((a_far, k_loc))
     a_far_sib = exchange(a_far, "seq", 1)
@@ -567,15 +575,17 @@
     b_far_sib = exchange(b_far, "seq", 1)
     proj = ((pairs, 2 * shard, lanes), BF16)
     weights = (wq, wk, wv, wo, gain1)
-    ka, va, qa, ea, ctx_a, rinv_a, hid_a = call(
+    ka, va, qa, ea, ctx_a, rinv_a, hid_a, win = call(
         functools.partial(attention_kernel, True),
         [
             proj, proj, ((pairs, shard, lanes), BF16), ((2 * pairs, 2 * shard, keys), BF16),
             ((pairs, 2 * shard, lanes), F32), ((pairs, 2 * shard, lanes), F32), ((2 * shard, width), F32),
+            (hidden_in.shape, BF16),
         ],
-        (own, sib, a_far, a_far_sib, k_loc, v_loc, q_loc, tiles, *weights),
+        (own, sib, a_far, a_far_sib, k_loc, v_loc, q_loc, tiles, *weights, Far(hidden_in)),
         12,
         3.0,
+        copies=1,
     )
     kb, vb, eb, ctx_b, rinv_b, hid_b = call(
         functools.partial(attention_kernel, False),
@@ -587,10 +597,10 @@
         12,
         3.0,
     )
-    out, hidden_grad, dctx, adapter_grad, lines = call(
+    out, out_send, hidden_grad, dctx, adapter_grad, lines = call(
         middle_kernel,
         [
-            ((rows, shard, width), BF16), ((tokens, width), F32), ((pairs, tokens, lanes), BF16),
+            ((rows, shard, width), BF16), ((1, shard, width), BF16), ((tokens, width), F32), ((pairs, tokens, lanes), BF16),
             ((2 * mid, width), F32), ((8, width), F32),
         ],
         (
@@ -626,24 +636,28 @@
     )
     sib_part_b, sib_a = lax.optimization_barrier((sib_part_b, sib_a))
     sib_b = exchange(sib_part_b, "seq", 1)
-    pack = pack + exchange(pack, "seq", 1)
-    (back,) = call(
+    far_sum, back = call(
         return_kernel,
-        [((rows, shard, width), BF16)],
-        (pack, a_far, part_a, sib_a, far_part, sib_b, out, hidden_grad, gain1),
+        [((1, shard, width), BF16), ((1, shard, width), BF16)],
+        (a_far, part_a, sib_a, far_part, sib_b, hidden_grad, gain1),
         16,
         0.5,
     )
-    returned = exchange(back, "seq", 2)
+    far_sum = exchange(far_sum, "seq", 2)
+    back = exchange(back, "seq", 2)
+    out_far = exchange(out_send, "seq", 2)
+    (pack,) = call(add_kernel, [((8, width), F32)], (pack, exchange(pack, "seq", 2)), 4, 10.0)
     bit = 1
-    while bit < lax.axis_size("batch"):
+    while 2 * bit < lax.axis_size("batch"):
         pack = pack + exchange(pack, "batch", bit)
         bit *= 2
-    far_pack = exchange(pack, "seq", 2)
+    pack = pack + exchange(pack, "seq", 1)
+    far_pack = exchange(pack, "batch", bit)
+    rowed = ((rows, shard, width), BF16)
     output, grad_input = call(
         last_kernel,
-        [((rows, shard, width), BF16), ((rows, shard, width), BF16)],
-        (own, part_a, sib_a, part_b, sib_b, returned, hidden_grad, gain1, out),
+        [rowed, rowed],
+        (own, part_a, sib_a, part_b, sib_b, far_sum, hidden_grad, gain1, out, out_far, back),
         16,
         1.0,
         last=True,

time: 63.5 us -> 61.5 us (0.969)
  waiting for transfers between devices: 10.9 us -> 6.89 us
  starting transfers between devices: 14.1 us -> 16.8 us
  Pallas kernels: 37.4 us -> 36.7 us
    ppermute x14 -> x16, waiting for transfers between devices: 10.9 us -> 6.89 us  [exchange(): return lax.ppermute(value, axis, [(k, k ^ bit) for k in range(count)])]
    ppermute x14 -> x16, starting transfers between devices: 14.1 us -> 16.8 us  [exchange(): return lax.ppermute(value, axis, [(k, k ^ bit) for k in range(count)])]
    pallas_call x11 -> x12, Pallas kernels: 37.4 us -> 36.7 us  [call(): pl.pallas_call(kernel, out_shape=[made(shape, kind) for shape, kind in ou...]
  transfers between devices with their start and end apart: 14 -> 16, of which waited for: 7 -> 5; matrix products, arithmetic and copies ran while one was open for 0% -> 0% of each run, Pallas kernels for 29% -> 29%
where the time goes in v4:
time: 61.5 us; the launch traced here: 61.2 us
  Pallas kernels  36.7 us (60%)
  starting transfers between devices  16.8 us (27%)
  waiting for transfers between devices  6.89 us (11%)
  between operations  0.78 us (1%)
    pallas_call x12, Pallas kernels, call(): pl.pallas_call(kernel, out_shape=[made(shape, kind) for shape, kind in ou...  36.7 us
    ppermute x16, starting transfers between devices, exchange(): return lax.ppermute(value, axis, [(k, k ^ bit) for k in range(count)])  16.8 us
    ppermute x16, waiting for transfers between devices, exchange(): return lax.ppermute(value, axis, [(k, k ^ bit) for k in range(count)])  6.89 us
  transfers between devices with their start and end apart: 16, of which 5 were waited for; matrix products, arithmetic and copies ran while one was open for 0% of the time, Pallas kernels for 29%

profile of v4, /device:TPU:0, one launch (start us, length us, event | category | flops | bytes accessed | tf_op | source)
XLA Modules:
  0.0 61.2 jit_solution(2138783136998446364)
XLA Ops:
  0.6 1.3 %shard_map.275 = (bf16[2,136,768]{2,1,0:T(8,128)(2,1)S(1)}, bf16[1,136,768]{2,1,0:T(8,128)(2,1)S(1)}, bf16[1,136,768]{2,1,0:T(8,128)(2,1)S(1)}, bf16[1,128,768]{2,1,0:T(8,128)(2,1)S(1)}) custom-call(bf16[3,128,768]{2,1,0:T(8,128)(2,1)} %inputs.1, bf16[3,128,768]{2,1,0:T(8,128)(2,1)} %cot.1, s32[3,128]{1,0:T(4,128)} %segment_ids.1), custom_call_target="tpu_custom_call" | custom-call | flops 1100000000 | tf_op jit(solution)/shard_map/pallas_call | solution.py:72
  2.0 3.0 %collective-permute-start.1 = (bf16[1,136,768]{2,1,0:T(8,128)(2,1)S(1)}, bf16[1,136,768]{2,1,0:T(8,128)(2,1)S(1)}, u32[]{:S(2)}, u32[]{:S(2)}) collective-permute-start(bf16[1,136,768]{2,1,0:T(8,128)(2,1)S(1)} %get-tuple-element.80), channel_id=1, source_target_pairs={{0,16},{8,24},{16,0},{24,8},{1,17},{9,25},{17,1},{25,9},{2,18},{10... | collective-permute-start | bytes 626696 | tf_op jit(solution)/shard_map/ppermute | solution.py:514
  5.0 0.1 collective-permute-start.3
  5.1 0.0 collective-permute-start
  5.1 4.6 %shard_map.276 = (f32[7,6,256,128]{3,2,1,0:T(8,128)S(1)}, bf16[48,768]{1,0:T(8,128)(2,1)S(1)}, bf16[48,768]{1,0:T(8,128)(2,1)S(1)}, f32[32,96]{1,0:T(8,128)S(1)}...) custom-call(s32[1023]{0:T(1024)} %table_far.1, ...), custom_call_target="tpu_custom_call" | custom-call | flops 22000001024 | tf_op jit(solution)/shard_map/pallas_call | solution.py:72
  9.7 0.0 collective-permute-done.sib
  9.7 1.9 %shard_map.277 = (bf16[6,512,128]{2,1,0:T(8,128)(2,1)S(1)}, bf16[6,512,128]{2,1,0:T(8,128)(2,1)S(1)}, bf16[6,256,128]{2,1,0:T(8,128)(2,1)S(1)}) custom-call(bf16[2,136,768]{2,1,0:T(8,128)(2,1)S(1)} %get-tuple-element.79.own, bf16[2,136,768]{2,1,0:T(8,128)(2,1)S(1)} %collective-permute-done.sib, bf16[768,768]{1,0:T(8,128)(2,1)S(1)} %get-tuple-element.81.wq.rest_1_.rest_0_, ...), custom_call_target="tpu_custom_call" | custom-call | flops 22000001024 | tf_op jit(solution)/shard_map/pallas_call | solution.py:72
  11.6 0.0 collective-permute-done.1.far
  11.6 0.6 collective-permute-start.2
  12.1 1.9 %collective-permute-start.5 = (bf16[1,128,768]{2,1,0:T(8,128)(2,1)S(1)}, bf16[1,128,768]{2,1,0:T(8,128)(2,1)S(1)}, u32[]{:S(2)}, u32[]{:S(2)}) collective-permute-start(bf16[1,128,768]{2,1,0:T(8,128)(2,1)S(1)} %get-tuple-element.97), channel_id=1, source_target_pairs={{0,16},{8,24},{16,0},{24,8},{1,17},{9,25},{17,1},{25,9},{2,18},{10... | collective-permute-start | bytes 589832 | tf_op jit(solution)/shard_map/ppermute | solution.py:514
  14.1 0.6 collective-permute-done.3.far
  14.7 0.0 collective-permute-done.2.far_sib
  14.7 0.0 collective-permute-start.4
  14.7 3.9 %shard_map.278 = (bf16[6,256,128]{2,1,0:T(8,128)(2,1)S(1)}, bf16[6,256,128]{2,1,0:T(8,128)(2,1)S(1)}, bf16[6,128,128]{2,1,0:T(8,128)(2,1)S(1)}, bf16[12,256,512]...) custom-call(bf16[2,136,768]{2,1,0:T(8,128)(2,1)S(1)} %get-tuple-elem, ...), custom_call_target="tpu_custom_call" | custom-call | flops 3300000000 | tf_op jit(solution)/shard_map/pallas_call | solution.py:72
  18.6 0.0 copy-start
  18.6 0.0 collective-permute-done.4.far_sib
  18.6 2.4 %shard_map.279 = (bf16[6,256,128]{2,1,0:T(8,128)(2,1)S(1)}, bf16[6,256,128]{2,1,0:T(8,128)(2,1)S(1)}, bf16[6,256,512]{2,1,0:T(8,128)(2,1)S(1)}, f32[6,128,128]{2...) custom-call(bf16[2,136,768]{2,1,0:T(8,128)(2,1)S(1)} %get-tuple-element.79.own, ...), custom_call_target="tpu_custom_call" | custom-call | flops 3300000000 | tf_op jit(solution)/shard_map/pallas_call | solution.py:72
  21.0 0.0 collective-permute-done.5.cot_far
  21.1 0.0 copy-done
  21.1 11.4 %shard_map.280 = (bf16[3,128,768]{2,1,0:T(8,128)(2,1)S(1)}, bf16[1,128,768]{2,1,0:T(8,128)(2,1)S(1)}, f32[384,768]{1,0:T(8,128)S(1)}, bf16[6,384,128]{2,1,0:T(8,...) custom-call(f32[256,768]{1,0:T(8,128)S(1)} %get-tuple-element.94.hid_a, ...), custom_call_target="tpu_custom_call" | custom-call | flops 13200000000 | tf_op jit(solution)/shard_map/pallas_call | solution.py:72
  32.5 5.3 %shard_map.281 = (f32[2,128,768]{2,1,0:T(8,128)S(1)}, bf16[2,128,768]{2,1,0:T(8,128)(2,1)S(1)}, f32[8,768]{1,0:T(8,128)S(1)}) custom-call(bf16[2,136,768]{2,1,0:T(8,128)(2,1)S(1)} %get-tuple-element.79.own, bf16[2,136,768]{2,1,0:T(8,128)(2,1)S(1)} %collective-permute-done.sib, bf16[1,136,768]{2,1,0:T(8,128)(2,1)S(1)} %collective-permute-done.1.far, ...), custom_call_target="tpu_custom_call" | custom-call | flops 6600000000 | tf_op jit(solution)/shard_map/pallas_call | solution.py:72
  37.7 0.6 collective-permute-start.6
  38.3 3.5 %shard_map.282 = (f32[1,128,768]{2,1,0:T(8,128)S(1)}, bf16[1,128,768]{2,1,0:T(8,128)(2,1)S(1)}, bf16[2,128,768]{2,1,0:T(8,128)(2,1)S(1)}, f32[8,768]{1,0:T(8,128)S(1)}) custom-call(bf16[2,136,768]{2,1,0:T(8,128)(2,1)S(1)} %get-tuple-element.79.own, bf16[2,136,768]{2,1,0:T(8,128)(2,1)S(1)} %collective-permute-done.sib, ...), custom_call_target="tpu_custom_call" | custom-call | flops 3960000000 | tf_op jit(solution)/shard_map/pallas_call | solution.py:72
  41.8 0.0 collective-permute-done.6.from_sib.sib_a
  41.8 0.1 collective-permute-start.7
  41.9 1.8 %collective-permute-start.11 = (f32[8,768]{1,0:T(8,128)S(1)}, f32[8,768]{1,0:T(8,128)S(1)}, u32[]{:S(2)}, u32[]{:S(2)}) collective-permute-start(f32[8,768]{1,0:T(8,128)S(1)} %get-tuple-element.137.a), channel_id=1, source_target_pairs={{0,16},{8,24},{16,0},{24,8},{1,17},{9,25},{17,1},{25,9},{2,18},{10... | collective-permute-start | bytes 73736 | tf_op jit(solution)/shard_map/ppermute | solution.py:514
  43.7 0.3 collective-permute-start.9
  44.0 0.0 collective-permute-done.7.from_sib_b.sib_b
  44.0 0.3 shard_map.283
  44.3 1.8 %collective-permute-start.8 = (bf16[1,128,768]{2,1,0:T(8,128)(2,1)S(1)}, bf16[1,128,768]{2,1,0:T(8,128)(2,1)S(1)}, u32[]{:S(2)}, u32[]{:S(2)}) collective-permute-start(bf16[1,128,768]{2,1,0:T(8,128)(2,1)S(1)} %get-tuple-element.131), channel_id=1, source_target_pairs={{0,16},{8,24},{16,0},{24,8},{1,17},{9,25},{17,1},{25,9},{2,18},{10... | collective-permute-start | bytes 589832 | tf_op jit(solution)/shard_map/ppermute | solution.py:514
  46.1 0.3 collective-permute-start.10
  46.4 0.0 collective-permute-done.11.b
  46.4 1.8 %collective-permute-start.12 = (f32[8,768]{1,0:T(8,128)S(1)}, f32[8,768]{1,0:T(8,128)S(1)}, u32[]{:S(2)}, u32[]{:S(2)}) collective-permute-start(f32[8,768]{1,0:T(8,128)S(1)} %shard_map.285), channel_id=1, source_target_pairs={{0,1},{1,0},{2,3},{3,2},{4,5},{5,4},{6,7},{7,6},{8,9},{9,8},{10,11... | collective-permute-start | bytes 73736 | tf_op jit(solution)/shard_map/ppermute | solution.py:514
  48.2 2.1 %collective-permute-done.12 = f32[8,768]{1,0:T(8,128)S(1)} collective-permute-done((f32[8,768]{1,0:T(8,128)S(1)}, f32[8,768]{1,0:T(8,128)S(1)}, u32[]{:S(2)}, u32[]{:S(2)}) %collective-permute-start.12) | collective-permute-done | bytes 24608 | tf_op jit(solution)/shard_map/ppermute | solution.py:514
  50.3 1.8 %collective-permute-start.13 = (f32[8,768]{1,0:T(8,128)S(1)}, f32[8,768]{1,0:T(8,128)S(1)}, u32[]{:S(2)}, u32[]{:S(2)}) collective-permute-start(f32[8,768]{1,0:T(8,128)S(1)} %add.9), channel_id=1, source_target_pairs={{0,2},{1,3},{2,0},{3,1},{4,6},{5,7},{6,4},{7,5},{8,10},{9,11},{10,... | collective-permute-start | bytes 73736 | tf_op jit(solution)/shard_map/ppermute | solution.py:514
  52.1 2.0 %collective-permute-done.13 = f32[8,768]{1,0:T(8,128)S(1)} collective-permute-done((f32[8,768]{1,0:T(8,128)S(1)}, f32[8,768]{1,0:T(8,128)S(1)}, u32[]{:S(2)}, u32[]{:S(2)}) %collective-permute-start.13) | collective-permute-done | bytes 24608 | tf_op jit(solution)/shard_map/ppermute | solution.py:514
  54.2 0.0 collective-permute-start.14
  54.2 1.2 %collective-permute-done.14 = f32[8,768]{1,0:T(8,128)S(1)} collective-permute-done((f32[8,768]{1,0:T(8,128)S(1)}, f32[8,768]{1,0:T(8,128)S(1)}, u32[]{:S(2)}, u32[]{:S(2)}) %collective-permute-start.14) | collective-permute-done | bytes 24608 | tf_op jit(solution)/shard_map/ppermute | solution.py:514
  55.4 2.8 %collective-permute-start.15 = (f32[8,768]{1,0:T(8,128)S(1)}, f32[8,768]{1,0:T(8,128)S(1)}, u32[]{:S(2)}, u32[]{:S(2)}) collective-permute-start(f32[8,768]{1,0:T(8,128)S(1)} %add.11.near_pack), channel_id=1, source_target_pairs={{0,4},{1,5},{2,6},{3,7},{4,0},{5,1},{6,2},{7,3},{8,12},{9,13},{10,... | collective-permute-start | bytes 73736 | tf_op jit(solution)/shard_map/ppermute | solution.py:514
  58.2 0.0 collective-permute-done.9.out_far
  58.2 0.0 collective-permute-done.8.far_sum
  58.2 0.9 %collective-permute-done.10.back = bf16[1,128,768]{2,1,0:T(8,128)(2,1)S(1)} collective-permute-done((bf16[1,128,768]{2,1,0:T(8,128)(2,1)S(1)}, bf16[1,128,768]{2,1,0:T(8,128)(2,1)S(1)}, u32[]{:S(2)}, u32[]{:S(2)}) %collective-permute-start.10) | collective-permute-done | bytes 196640 | tf_op jit(solution)/shard_map/ppermute | solution.py:514
  59.1 1.4 %shard_map.284 = (bf16[3,128,768]{2,1,0:T(8,128)(2,1)}, bf16[3,128,768]{2,1,0:T(8,128)(2,1)}) custom-call(bf16[2,136,768]{2,1,0:T(8,128)(2,1)S(1)} %get-tuple-element.79.own, f32[2,128,768]{2,1,0:T(8,128)S(1)} %get-tuple-element.117.own_part.part_a, bf16[2,128,768]{2,1,0:T(8,128)(2,1)S(1)} %collective-permute-done.6.from_sib.sib_a, ...), custom_call_target="tpu_custom_call" | custom-call | flops 1100000000 | tf_op jit(solution)/shard_map/pallas_call | solution.py:72
  60.5 0.0 collective-permute-done.15.far_pack
  60.5 0.7 %shard_map.286 = (f32[768]{0:T(1024)}, f32[768]{0:T(1024)}, f32[4,4,4]{2,1,0:T(4,128)}, f32[4,192]{1,0:T(4,128)}, f32[4,12]{1,0:T(4,128)}, /*index=5*/f32[4,12]{...) custom-call(f32[8,768]{1,0:T(8,128)S(1)} %add.11.near_pack, f32[8,768]{1,0:T(8,128)S(1)} %collective-permute-done.15.far_pack, ...), custom_call_target="tpu_custom_call" | custom-call | flops 550000000 | tf_op jit(solution)/shard_map/pallas_call | solution.py:72
  (4 shorter events, 0.0 us)
Async XLA Ops:
  2.0 9.6 %collective-permute-start.1 = (bf16[1,136,768]{2,1,0:T(8,128)(2,1)S(1)}, bf16[1,136,768]{2,1,0:T(8,128)(2,1)S(1)}, u32[]{:S(2)}, u32[]{:S(2)}) collective-permute-start(bf16[1,136,768]{2,1,0:T(8,128)(2,1)S(1)} %get-tuple-element.80), channel_id=1, source_target_pairs={{0,16},{8,24},{16,0},{24,8},{1,17},{9,25},{17,1},{25,9},{2,18},{10... | collective-permute-start | bytes 626696 | tf_op jit(solution)/shard_map/ppermute | solution.py:514
  5.0 9.6 %collective-permute-start.3 = (bf16[1,136,768]{2,1,0:T(8,128)(2,1)S(1)}, bf16[1,136,768]{2,1,0:T(8,128)(2,1)S(1)}, u32[]{:S(2)}, u32[]{:S(2)}) collective-permute-start(bf16[1,136,768]{2,1,0:T(8,128)(2,1)S(1)} %get-tuple-element.87), channel_id=1, source_target_pairs={{0,16},{8,24},{16,0},{24,8},{1,17},{9,25},{17,1},{25,9},{2,18},{10... | collective-permute-start | bytes 626696 | tf_op jit(solution)/shard_map/ppermute | solution.py:514
  5.1 4.6 %collective-permute-start = (bf16[2,136,768]{2,1,0:T(8,128)(2,1)S(1)}, bf16[2,136,768]{2,1,0:T(8,128)(2,1)S(1)}, u32[]{:S(2)}, u32[]{:S(2)}) collective-permute-start(bf16[2,136,768]{2,1,0:T(8,128)(2,1)S(1)} %get-tuple-element.79.own), channel_id=1, source_target_pairs={{0,8},{8,0},{16,24},{24,16},{1,9},{9,1},{17,25},{25,17},{2,10},{10... | collective-permute-start | bytes 1253384 | tf_op jit(solution)/shard_map/ppermute | solution.py:514
  11.6 3.1 %collective-permute-start.2 = (bf16[1,136,768]{2,1,0:T(8,128)(2,1)S(1)}, bf16[1,136,768]{2,1,0:T(8,128)(2,1)S(1)}, u32[]{:S(2)}, u32[]{:S(2)}) collective-permute-start(bf16[1,136,768]{2,1,0:T(8,128)(2,1)S(1)} %collective-permute-done.1.far), channel_id=1, source_target_pairs={{0,8},{8,0},{16,24},{24,16},{1,9},{9,1},{17,25},{25,17},{2,10},{10... | collective-permute-start | bytes 626696 | tf_op jit(solution)/shard_map/ppermute | solution.py:514
  12.1 8.9 %collective-permute-start.5 = (bf16[1,128,768]{2,1,0:T(8,128)(2,1)S(1)}, bf16[1,128,768]{2,1,0:T(8,128)(2,1)S(1)}, u32[]{:S(2)}, u32[]{:S(2)}) collective-permute-start(bf16[1,128,768]{2,1,0:T(8,128)(2,1)S(1)} %get-tuple-element.97), channel_id=1, source_target_pairs={{0,16},{8,24},{16,0},{24,8},{1,17},{9,25},{17,1},{25,9},{2,18},{10... | collective-permute-start | bytes 589832 | tf_op jit(solution)/shard_map/ppermute | solution.py:514
  14.7 3.9 %collective-permute-start.4 = (bf16[1,136,768]{2,1,0:T(8,128)(2,1)S(1)}, bf16[1,136,768]{2,1,0:T(8,128)(2,1)S(1)}, u32[]{:S(2)}, u32[]{:S(2)}) collective-permute-start(bf16[1,136,768]{2,1,0:T(8,128)(2,1)S(1)} %collective-permute-done.3.far), channel_id=1, source_target_pairs={{0,8},{8,0},{16,24},{24,16},{1,9},{9,1},{17,25},{25,17},{2,10},{10... | collective-permute-start | bytes 626696 | tf_op jit(solution)/shard_map/ppermute | solution.py:514
  18.6 2.5 %copy-start = (bf16[3,128,768]{2,1,0:T(8,128)(2,1)S(1)}, bf16[3,128,768]{2,1,0:T(8,128)(2,1)}, u32[]{:S(2)}) copy-start(bf16[3,128,768]{2,1,0:T(8,128)(2,1)} %cot.1) | copy-start | bytes 1769476
  37.7 4.1 %collective-permute-start.6 = (bf16[2,128,768]{2,1,0:T(8,128)(2,1)S(1)}, bf16[2,128,768]{2,1,0:T(8,128)(2,1)S(1)}, u32[]{:S(2)}, u32[]{:S(2)}) collective-permute-start(bf16[2,128,768]{2,1,0:T(8,128)(2,1)S(1)} %get-tuple-element.125), channel_id=1, source_target_pairs={{0,8},{8,0},{16,24},{24,16},{1,9},{9,1},{17,25},{25,17},{2,10},{10... | collective-permute-start | bytes 1179656 | tf_op jit(solution)/shard_map/ppermute | solution.py:514
  41.8 2.2 %collective-permute-start.7 = (bf16[2,128,768]{2,1,0:T(8,128)(2,1)S(1)}, bf16[2,128,768]{2,1,0:T(8,128)(2,1)S(1)}, u32[]{:S(2)}, u32[]{:S(2)}) collective-permute-start(bf16[2,128,768]{2,1,0:T(8,128)(2,1)S(1)} %get-tuple-element.128), channel_id=1, source_target_pairs={{0,8},{8,0},{16,24},{24,16},{1,9},{9,1},{17,25},{25,17},{2,10},{10... | collective-permute-start | bytes 1179656 | tf_op jit(solution)/shard_map/ppermute | solution.py:514
  41.9 4.5 %collective-permute-start.11 = (f32[8,768]{1,0:T(8,128)S(1)}, f32[8,768]{1,0:T(8,128)S(1)}, u32[]{:S(2)}, u32[]{:S(2)}) collective-permute-start(f32[8,768]{1,0:T(8,128)S(1)} %get-tuple-element.137.a), channel_id=1, source_target_pairs={{0,16},{8,24},{16,0},{24,8},{1,17},{9,25},{17,1},{25,9},{2,18},{10... | collective-permute-start | bytes 73736 | tf_op jit(solution)/shard_map/ppermute | solution.py:514
  43.7 14.5 %collective-permute-start.9 = (bf16[1,128,768]{2,1,0:T(8,128)(2,1)S(1)}, bf16[1,128,768]{2,1,0:T(8,128)(2,1)S(1)}, u32[]{:S(2)}, u32[]{:S(2)}) collective-permute-start(bf16[1,128,768]{2,1,0:T(8,128)(2,1)S(1)} %get-tuple-element.133), channel_id=1, source_target_pairs={{0,16},{8,24},{16,0},{24,8},{1,17},{9,25},{17,1},{25,9},{2,18},{10... | collective-permute-start | bytes 589832 | tf_op jit(solution)/shard_map/ppermute | solution.py:514
  44.3 13.9 %collective-permute-start.8 = (bf16[1,128,768]{2,1,0:T(8,128)(2,1)S(1)}, bf16[1,128,768]{2,1,0:T(8,128)(2,1)S(1)}, u32[]{:S(2)}, u32[]{:S(2)}) collective-permute-start(bf16[1,128,768]{2,1,0:T(8,128)(2,1)S(1)} %get-tuple-element.131), channel_id=1, source_target_pairs={{0,16},{8,24},{16,0},{24,8},{1,17},{9,25},{17,1},{25,9},{2,18},{10... | collective-permute-start | bytes 589832 | tf_op jit(solution)/shard_map/ppermute | solution.py:514
  46.1 13.0 %collective-permute-start.10 = (bf16[1,128,768]{2,1,0:T(8,128)(2,1)S(1)}, bf16[1,128,768]{2,1,0:T(8,128)(2,1)S(1)}, u32[]{:S(2)}, u32[]{:S(2)}) collective-permute-start(bf16[1,128,768]{2,1,0:T(8,128)(2,1)S(1)} %get-tuple-element.134), channel_id=1, source_target_pairs={{0,16},{8,24},{16,0},{24,8},{1,17},{9,25},{17,1},{25,9},{2,18},{10... | collective-permute-start | bytes 589832 | tf_op jit(solution)/shard_map/ppermute | solution.py:514
  46.4 3.9 %collective-permute-start.12 = (f32[8,768]{1,0:T(8,128)S(1)}, f32[8,768]{1,0:T(8,128)S(1)}, u32[]{:S(2)}, u32[]{:S(2)}) collective-permute-start(f32[8,768]{1,0:T(8,128)S(1)} %shard_map.285), channel_id=1, source_target_pairs={{0,1},{1,0},{2,3},{3,2},{4,5},{5,4},{6,7},{7,6},{8,9},{9,8},{10,11... | collective-permute-start | bytes 73736 | tf_op jit(solution)/shard_map/ppermute | solution.py:514
  50.3 3.8 %collective-permute-start.13 = (f32[8,768]{1,0:T(8,128)S(1)}, f32[8,768]{1,0:T(8,128)S(1)}, u32[]{:S(2)}, u32[]{:S(2)}) collective-permute-start(f32[8,768]{1,0:T(8,128)S(1)} %add.9), channel_id=1, source_target_pairs={{0,2},{1,3},{2,0},{3,1},{4,6},{5,7},{6,4},{7,5},{8,10},{9,11},{10,... | collective-permute-start | bytes 73736 | tf_op jit(solution)/shard_map/ppermute | solution.py:514
  54.2 1.2 %collective-permute-start.14 = (f32[8,768]{1,0:T(8,128)S(1)}, f32[8,768]{1,0:T(8,128)S(1)}, u32[]{:S(2)}, u32[]{:S(2)}) collective-permute-start(f32[8,768]{1,0:T(8,128)S(1)} %add.10), channel_id=1, source_target_pairs={{0,8},{8,0},{16,24},{24,16},{1,9},{9,1},{17,25},{25,17},{2,10},{10... | collective-permute-start | bytes 73736 | tf_op jit(solution)/shard_map/ppermute | solution.py:514
  55.4 5.2 %collective-permute-start.15 = (f32[8,768]{1,0:T(8,128)S(1)}, f32[8,768]{1,0:T(8,128)S(1)}, u32[]{:S(2)}, u32[]{:S(2)}) collective-permute-start(f32[8,768]{1,0:T(8,128)S(1)} %add.11.near_pack), channel_id=1, source_target_pairs={{0,4},{1,5},{2,6},{3,7},{4,0},{5,1},{6,2},{7,3},{8,12},{9,13},{10,... | collective-permute-start | bytes 73736 | tf_op jit(solution)/shard_map/ppermute | solution.py:514

commit v5 on v4

--- a/solution.py
+++ b/solution.py
@@ -62,7 +62,7 @@
     return pltpu.with_memory_space_constraint(value, pltpu.VMEM)
 
 
-def call(kernel, outs, args, limit, micros, scratch=(), copies=0, last=False):
+def call(kernel, outs, args, limit, micros, scratch=(), copies=0, last=False, aliases=()):
     specs = [pl.BlockSpec(memory_space=pl.ANY) if isinstance(a, Far) else VM for a in args]
     args = [pltpu.with_memory_space_constraint(a.value, pltpu.HBM) if isinstance(a, Far) else near(a) for a in args]
     scratch = [pltpu.VMEM(shape, kind) for shape, kind in scratch]
@@ -73,7 +73,8 @@
         kernel,
         out_shape=[made(shape, kind) for shape, kind in outs],
         in_specs=specs,
-        out_specs=[VM] * len(outs),
+        out_specs=[pl.BlockSpec(memory_space=pl.ANY if aliases else pltpu.VMEM)] * len(outs),
+        input_output_aliases=dict(aliases),
         scratch_shapes=scratch,
         compiler_params=pltpu.CompilerParams(vmem_limit_bytes=limit * MIB),
         cost_estimate=pl.CostEstimate(flops=int(micros * 1.1e9), bytes_accessed=0, transcendentals=0),
@@ -288,16 +289,15 @@
 
 
 def middle_kernel(
-    hid_a, hid_b, cot, cot_far, win, wout, wo, gain2, bd, bu, down_t, up,
-    out, out_send, hidden_grad, dctx, adapter_grad, lines, low, act, gslope,
+    ranks, hid_a, hid_b, cot, cot_far, win, wout, gain2, bd, bu, down_t, up, mix, side, left,
+    out, out_send, hidden_grad, low_grad, pack, low, act, gslope, adapter_grad,
 ):
     rows, shard, width = cot.shape
     hidden = win.shape[1]
-    pairs, _, lanes = dctx.shape
     state = jnp.concatenate([hid_a[...], hid_b[...]], 0)
     inv2 = inverse_rms(state)
     low[...] = (state * inv2 * gain2[...][None, :]).astype(BF16)
-    chunk = 2 * lanes
+    chunk = width // 3
     for j in range(hidden // chunk):
         cols = slice(j * chunk, (j + 1) * chunk)
         g, slope = gelu_pair(dot(low[...], win[:, cols]))
@@ -321,10 +321,12 @@
     adapter_grad[:mid, :] = dot_tn(gb_low, branch_low)
     adapter_grad[mid:, :] = dot_tn(g_low, up_low)
     grad2 = jnp.zeros((rows * shard, width), F32)
-    chunk = 6 * lanes
+    chunk = width
     for j in range(hidden // chunk):
         cols = slice(j * chunk, (j + 1) * chunk)
         pre = (dot_nt(low[...], wout[cols, :]) * gslope[:, cols].astype(F32)).astype(BF16)
+        if j == 1:
+            pack_small(ranks, adapter_grad, mix, side, left, pack)
         grad2 = grad2 + dot_nt(pre, win[:, cols])
     state = jnp.concatenate([hid_a[...], hid_b[...]], 0)
     inv2 = inverse_rms(state)
@@ -332,29 +334,28 @@
     c = grad2 * gain2[...][None, :]
     total = upstream + inv2 * (c - hat2 * jnp.mean(hat2 * c, -1, keepdims=True))
     hidden_grad[...] = total
-    low[...] = total.astype(BF16)
-    lines[...] = jnp.zeros(lines.shape, F32)
-    lines[0:1, :] = jnp.sum(grad2 * hat2, 0, keepdims=True)
-    lines[1:2, :] = jnp.sum(upstream, 0, keepdims=True)
-    lines[2:3, 0 : gb.shape[1]] = jnp.sum(gb, 0, keepdims=True)
-    for t in range(pairs // 2):
-        part = dot_nt(low[...], wo[2 * t * lanes : (2 * t + 2) * lanes, :]).astype(BF16)
-        dctx[2 * t] = part[:, :lanes]
-        dctx[2 * t + 1] = part[:, lanes:]
+    low_grad[...] = total.astype(BF16)
+    pack[1:2, :] = jnp.sum(grad2 * hat2, 0, keepdims=True)
+    pack[2:3, :] = jnp.sum(upstream, 0, keepdims=True)
+    pack[3:4, 0:mid] = jnp.sum(gb, 0, keepdims=True)
 
 
 def backward_kernel(
-    is_moved, ranks, own, sib, far, far_sib, dctx, ctx, rinv, e, k_loc, v_loc, q_loc, k_rem, v_rem, *rest,
+    is_moved, own, sib, far, far_sib, ctx, rinv, e, k_loc, v_loc, q_loc, k_rem, v_rem, *rest,
 ):
-    pairs, _, lanes = dctx.shape
+    pairs, _, lanes = k_loc.shape
     shard, width = q_loc.shape[1] // 2, pairs * lanes
     if is_moved:
-        q_rem, wq, wk, wv, *rest = rest
-        *small, own_part, sib_part, pack, dkt, dvt = rest
-        first, blocks, start = 0, 2, 0
+        q_rem, wq, wk, wv, wo, low_grad, pack_in, own_part, sib_part, pack, dctx_b, dkt, dvt, dctx = rest
+        first, blocks = 0, 2
+        for t in range(pairs // 2):
+            part = dot_nt(low_grad[...], wo[2 * t * lanes : (2 * t + 2) * lanes, :]).astype(BF16)
+            for k in range(2):
+                dctx[2 * t + k] = part[: 2 * shard, k * lanes : (k + 1) * lanes]
+                dctx_b[2 * t + k] = part[2 * shard :, k * lanes : (k + 1) * lanes]
     else:
-        wq, wk, wv, pack_a, own_part, far_part, sib_part, pack, dkt, dvt = rest
-        first, blocks, start = 1, 1, 2
+        wq, wk, wv, dctx, pack_in, own_part, far_part, sib_part, pack, dkt, dvt = rest
+        first, blocks = 1, 1
     low, low_lane, high_lane = halves(lanes)
     low_row = (iota((lanes, 1), 0) < lanes // 2).astype(F32).astype(BF16)
     high_row = 1.0 - low_row
@@ -365,7 +366,7 @@
         lefts, deltas, turned_q, turned_s = [], [], [], []
         for b in range(blocks):
             span = slice(b * shard, (b + 1) * shard)
-            scaled = dctx[p, (start + b) * shard : (start + b + 1) * shard, :].astype(F32) * rinv[p, span, :]
+            scaled = dctx[p, span, :].astype(F32) * rinv[p, span, :]
             product = scaled * ctx[p, span, :]
             deltas.append(jnp.sum(jnp.where(low, product, 0.0), 1, keepdims=True))
             deltas.append(jnp.sum(jnp.where(low, 0.0, product), 1, keepdims=True))
@@ -404,21 +405,19 @@
     for piece, x in zip(pieces, (own[first], sib[first], far[0], far_sib[0])):
         x = x[:shard].astype(F32)
         gain = gain + jnp.sum(piece * (x * inverse_rms(x)), 0, keepdims=True)
+    pack[...] = pack_in[...]
+    pack[0:1, :] = pack_in[0:1, :] + gain
     if is_moved:
-        pack_small(ranks, *small, pack)
-        pack[0:1, :] = gain
         own_part[0] = pieces[0]
         own_part[1] = pieces[2]
     else:
-        pack[...] = pack_a[...]
-        pack[0:1, :] = pack_a[0:1, :] + gain
         own_part[0] = pieces[0]
         far_part[0] = pieces[2].astype(BF16)
     sib_part[0, :shard] = pieces[1].astype(BF16)
     sib_part[1, :shard] = pieces[3].astype(BF16)
 
 
-def pack_small(ranks, grads, lines, mix, side, left, pack):
+def pack_small(ranks, grads, mix, side, left, pack):
     mid, width = grads.shape[0] // 2, grads.shape[1]
     inner, outer, square = mid // ranks, width // ranks, ranks * ranks
     line = iota((2 * square, width), 0)
@@ -450,7 +449,6 @@
     sides = dot_nt(dot(spread, product * mix[...]), by_j)
     core = dot(spread, dot(dot_nt(product * side[...], by_c), widen) * keep)
     pack[...] = jnp.zeros(pack.shape, F32)
-    pack[1:4, :] = lines[0:3, :]
     pack[4:8, 0:outer] = ends[:ranks]
     pack[4:8, 256 : 256 + outer] = ends[ranks:]
     pack[4:8, 512 : 512 + inner] = sides[:ranks, :inner]
@@ -466,27 +464,32 @@
     return hidden_grad + inv * (c - hat * jnp.mean(hat * c, -1, keepdims=True))
 
 
-def return_kernel(far, own_part, from_sib, far_part, from_sib_b, hidden_grad, gain, far_sum, back):
+def return_kernel(far, own_part, from_sib, far_part, from_sib_b, hidden_grad, gain, back):
     shard = back.shape[1]
-    far_sum[0] = (far_part[0].astype(F32) + from_sib_b[1, :shard].astype(F32)).astype(BF16)
+    back[0] = (far_part[0].astype(F32) + from_sib_b[1, :shard].astype(F32)).astype(BF16)
     grad = own_part[1] + from_sib[1].astype(F32)
-    back[0] = norm_back(far[0, :shard], grad, hidden_grad[shard : 2 * shard, :], gain).astype(BF16)
-
-
-def last_kernel(
-    own, part_a, sib_a, part_b, sib_b, far_sum, hidden_grad, gain, out, out_far, back, output, grad_input
-):
+    back[1] = norm_back(far[0, :shard], grad, hidden_grad[shard : 2 * shard, :], gain).astype(BF16)
+
+
+def own_rows_kernel(own, part_a, sib_a, hidden_grad, gain, out, output, grad_input):
     rows, shard, width = out.shape
     row = moved_row(rows)
-    other = rows - 1 - row
     output[row] = out[0]
     output[1] = out[2]
-    output[other] = out_far[0]
-    grad_input[other] = back[0]
     grad = part_a[0] + sib_a[0].astype(F32)
     grad_input[row] = norm_back(own[0, :shard], grad, hidden_grad[0:shard, :], gain).astype(BF16)
-    grad = part_b[0] + sib_b[0].astype(F32) + far_sum[0].astype(F32)
-    grad_input[1] = norm_back(own[1, :shard], grad, hidden_grad[2 * shard :, :], gain).astype(BF16)
+
+
+def last_kernel(own, part_b, sib_b, hidden_grad, gain, out_far, back, _, __, output, grad_input, grad_b, sems):
+    rows, shard, width = output.shape
+    other = rows - 1 - moved_row(rows)
+    started = start_copies([(out_far.at[0], output.at[other]), (back.at[1], grad_input.at[other])], sems)
+    grad = part_b[0] + sib_b[0].astype(F32) + back[0].astype(F32)
+    grad_b[...] = norm_back(own[1, :shard], grad, hidden_grad[2 * shard :, :], gain).astype(BF16)
+    own_copy = pltpu.make_async_copy(grad_b, grad_input.at[1], sems.at[2])
+    own_copy.start()
+    for one in (*started, own_copy):
+        one.wait()
 
 
 def unpack_kernel(ranks, mid, near_pack, far_pack, _, g1, g2, shared, dl, dr, ul, ur, bd, bu):
@@ -597,38 +600,40 @@
         12,
         3.0,
     )
-    out, out_send, hidden_grad, dctx, adapter_grad, lines = call(
-        middle_kernel,
+    out, out_send, hidden_grad, low_grad, pack_m = call(
+        functools.partial(middle_kernel, ranks),
         [
-            ((rows, shard, width), BF16), ((1, shard, width), BF16), ((tokens, width), F32), ((pairs, tokens, lanes), BF16),
-            ((2 * mid, width), F32), ((8, width), F32),
+            ((rows, shard, width), BF16), ((1, shard, width), BF16), ((tokens, width), F32), ((tokens, width), BF16),
+            ((8, width), F32),
         ],
         (
-            hid_a, hid_b, cotangent, cot_far, win, wout, wo, gain2, bd, bu, down_t, up,
+            hid_a, hid_b, cotangent, cot_far, win, wout, gain2, bd, bu, down_t, up, *expanded,
         ),
         20,
         12.0,
-        [((tokens, width), BF16), ((tokens, hidden), BF16), ((tokens, hidden), BF16)],
+        [((tokens, width), BF16), ((tokens, hidden), BF16), ((tokens, hidden), BF16), ((2 * mid, width), F32)],
     )
     turned = [((pairs, lanes, keys), BF16)] * 2
-    part_a, sib_part_a, pack_a = call(
-        functools.partial(backward_kernel, True, ranks),
-        [((2, shard, width), F32), ((2, shard, width), BF16), ((8, width), F32)],
+    part_a, sib_part_a, pack_a, dctx_b = call(
+        functools.partial(backward_kernel, True),
+        [
+            ((2, shard, width), F32), ((2, shard, width), BF16), ((8, width), F32), ((pairs, shard, lanes), BF16),
+        ],
         (
-            own, sib, a_far, a_far_sib, dctx, ctx_a, rinv_a, ea, k_loc, v_loc, q_loc, ka, va, qa,
-            wq, wk, wv, adapter_grad, lines, *expanded,
+            own, sib, a_far, a_far_sib, ctx_a, rinv_a, ea, k_loc, v_loc, q_loc, ka, va, qa,
+            wq, wk, wv, wo, low_grad, pack_m,
         ),
         14,
         6.0,
-        turned,
+        turned + [((pairs, 2 * shard, lanes), BF16)],
     )
     sib_a = exchange(sib_part_a, "seq", 1)
     part_b, far_part, sib_part_b, pack = call(
-        functools.partial(backward_kernel, False, ranks),
+        functools.partial(backward_kernel, False),
         [((1, shard, width), F32), ((1, shard, width), BF16), ((2, shard, width), BF16), ((8, width), F32)],
         (
-            own, sib, b_far, b_far_sib, dctx, ctx_b, rinv_b, eb, k_loc, v_loc, q_loc, kb, vb,
-            wq, wk, wv, pack_a,
+            own, sib, b_far, b_far_sib, ctx_b, rinv_b, eb, k_loc, v_loc, q_loc, kb, vb,
+            wq, wk, wv, dctx_b, pack_a,
         ),
         14,
         3.6,
@@ -636,14 +641,13 @@
     )
     sib_part_b, sib_a = lax.optimization_barrier((sib_part_b, sib_a))
     sib_b = exchange(sib_part_b, "seq", 1)
-    far_sum, back = call(
+    (back,) = call(
         return_kernel,
-        [((1, shard, width), BF16), ((1, shard, width), BF16)],
+        [((2, shard, width), BF16)],
         (a_far, part_a, sib_a, far_part, sib_b, hidden_grad, gain1),
         16,
         0.5,
     )
-    far_sum = exchange(far_sum, "seq", 2)
     back = exchange(back, "seq", 2)
     out_far = exchange(out_send, "seq", 2)
     (pack,) = call(add_kernel, [((8, width), F32)], (pack, exchange(pack, "seq", 2)), 4, 10.0)
@@ -655,12 +659,18 @@
     far_pack = exchange(pack, "batch", bit)
     rowed = ((rows, shard, width), BF16)
     output, grad_input = call(
+        own_rows_kernel, [rowed, rowed], (own, part_a, sib_a, hidden_grad, gain1, out), 16, 1.0, last=True
+    )
+    output, grad_input = call(
         last_kernel,
         [rowed, rowed],
-        (own, part_a, sib_a, part_b, sib_b, far_sum, hidden_grad, gain1, out, out_far, back),
+        (own, part_b, sib_b, hidden_grad, gain1, out_far, back, Far(output), Far(grad_input)),
         16,
         1.0,
+        [((shard, width), BF16)],
+        copies=3,
         last=True,
+        aliases={7: 0, 8: 1},
     )
     grads = call(
         functools.partial(unpack_kernel, ranks, mid),

time: 61.5 us -> 60.1 us (0.977)
  starting transfers between devices: 16.8 us -> 15.9 us
    ppermute x16 -> x15, starting transfers between devices: 16.8 us -> 15.9 us  [exchange(): return lax.ppermute(value, axis, [(k, k ^ bit) for k in range(count)])]
    ppermute x16 -> x15, waiting for transfers between devices: 6.89 us -> 6.64 us  [exchange(): return lax.ppermute(value, axis, [(k, k ^ bit) for k in range(count)])]
    pallas_call x12 -> x13, Pallas kernels: 36.7 us -> 36.5 us  [call(): pl.pallas_call(kernel, out_shape=[made(shape, kind) for shape, kind in ou...]
  transfers between devices with their start and end apart: 16 -> 15, of which waited for: 5 -> 5; matrix products, arithmetic and copies ran while one was open for 0% -> 0% of each run, Pallas kernels for 29% -> 31%
where the time goes in v5:
time: 60.1 us; the launch traced here: 59.9 us
  Pallas kernels  36.5 us (61%)
  starting transfers between devices  15.9 us (26%)
  waiting for transfers between devices  6.64 us (11%)
  between operations  0.8 us (1%)
    pallas_call x13, Pallas kernels, call(): pl.pallas_call(kernel, out_shape=[made(shape, kind) for shape, kind in ou...  36.5 us
    ppermute x15, starting transfers between devices, exchange(): return lax.ppermute(value, axis, [(k, k ^ bit) for k in range(count)])  15.9 us
    ppermute x15, waiting for transfers between devices, exchange(): return lax.ppermute(value, axis, [(k, k ^ bit) for k in range(count)])  6.64 us
  transfers between devices with their start and end apart: 15, of which 5 were waited for; matrix products, arithmetic and copies ran while one was open for 0% of the time, Pallas kernels for 31%

profile of v5, /device:TPU:0, one launch (start us, length us, event | category | flops | bytes accessed | tf_op | source)
XLA Modules:
  0.0 59.9 jit_solution(18352921221760190994)
XLA Ops:
  0.6 1.3 %shard_map.275 = (bf16[2,136,768]{2,1,0:T(8,128)(2,1)S(1)}, bf16[1,136,768]{2,1,0:T(8,128)(2,1)S(1)}, bf16[1,136,768]{2,1,0:T(8,128)(2,1)S(1)}, bf16[1,128,768]{2,1,0:T(8,128)(2,1)S(1)}) custom-call(bf16[3,128,768]{2,1,0:T(8,128)(2,1)} %inputs.1, bf16[3,128,768]{2,1,0:T(8,128)(2,1)} %cot.1, s32[3,128]{1,0:T(4,128)} %segment_ids.1), custom_call_target="tpu_custom_call" | custom-call | flops 1100000000 | tf_op jit(solution)/shard_map/pallas_call | solution.py:72
  2.0 3.0 %collective-permute-start.1 = (bf16[1,136,768]{2,1,0:T(8,128)(2,1)S(1)}, bf16[1,136,768]{2,1,0:T(8,128)(2,1)S(1)}, u32[]{:S(2)}, u32[]{:S(2)}) collective-permute-start(bf16[1,136,768]{2,1,0:T(8,128)(2,1)S(1)} %get-tuple-element.80), channel_id=1, source_target_pairs={{0,16},{8,24},{16,0},{24,8},{1,17},{9,25},{17,1},{25,9},{2,18},{10... | collective-permute-start | bytes 626696 | tf_op jit(solution)/shard_map/ppermute | solution.py:517
  5.0 0.1 collective-permute-start.3
  5.1 0.0 collective-permute-start
  5.1 4.6 %shard_map.276 = (f32[7,6,256,128]{3,2,1,0:T(8,128)S(1)}, bf16[48,768]{1,0:T(8,128)(2,1)S(1)}, bf16[48,768]{1,0:T(8,128)(2,1)S(1)}, f32[32,96]{1,0:T(8,128)S(1)}...) custom-call(s32[1023]{0:T(1024)} %table_far.1, ...), custom_call_target="tpu_custom_call" | custom-call | flops 22000001024 | tf_op jit(solution)/shard_map/pallas_call | solution.py:72
  9.7 0.0 collective-permute-done.sib
  9.7 1.9 %shard_map.277 = (bf16[6,512,128]{2,1,0:T(8,128)(2,1)S(1)}, bf16[6,512,128]{2,1,0:T(8,128)(2,1)S(1)}, bf16[6,256,128]{2,1,0:T(8,128)(2,1)S(1)}) custom-call(bf16[2,136,768]{2,1,0:T(8,128)(2,1)S(1)} %get-tuple-element.79.own, bf16[2,136,768]{2,1,0:T(8,128)(2,1)S(1)} %collective-permute-done.sib, bf16[768,768]{1,0:T(8,128)(2,1)S(1)} %get-tuple-element.81.wq.rest_1_.rest_0_, ...), custom_call_target="tpu_custom_call" | custom-call | flops 22000001024 | tf_op jit(solution)/shard_map/pallas_call | solution.py:72
  11.6 0.0 collective-permute-done.1.far
  11.6 0.6 collective-permute-start.2
  12.1 1.9 %collective-permute-start.5 = (bf16[1,128,768]{2,1,0:T(8,128)(2,1)S(1)}, bf16[1,128,768]{2,1,0:T(8,128)(2,1)S(1)}, u32[]{:S(2)}, u32[]{:S(2)}) collective-permute-start(bf16[1,128,768]{2,1,0:T(8,128)(2,1)S(1)} %get-tuple-element.108), channel_id=1, source_target_pairs={{0,16},{8,24},{16,0},{24,8},{1,17},{9,25},{17,1},{25,9},{2,18},{10... | collective-permute-start | bytes 589832 | tf_op jit(solution)/shard_map/ppermute | solution.py:517
  14.1 0.6 collective-permute-done.3.far
  14.7 0.0 collective-permute-done.2.far_sib
  14.7 0.0 collective-permute-start.4
  14.7 3.9 %shard_map.279 = (bf16[6,256,128]{2,1,0:T(8,128)(2,1)S(1)}, bf16[6,256,128]{2,1,0:T(8,128)(2,1)S(1)}, bf16[6,128,128]{2,1,0:T(8,128)(2,1)S(1)}, bf16[12,256,512]...) custom-call(bf16[2,136,768]{2,1,0:T(8,128)(2,1)S(1)} %get-tuple-elem, ...), custom_call_target="tpu_custom_call" | custom-call | flops 3300000000 | tf_op jit(solution)/shard_map/pallas_call | solution.py:72
  18.6 0.0 copy-start
  18.6 0.0 collective-permute-done.4.far_sib
  18.6 2.4 %shard_map.278 = (bf16[6,256,128]{2,1,0:T(8,128)(2,1)S(1)}, bf16[6,256,128]{2,1,0:T(8,128)(2,1)S(1)}, bf16[6,256,512]{2,1,0:T(8,128)(2,1)S(1)}, f32[6,128,128]{2...) custom-call(bf16[2,136,768]{2,1,0:T(8,128)(2,1)S(1)} %get-tuple-element.79.own, ...), custom_call_target="tpu_custom_call" | custom-call | flops 3300000000 | tf_op jit(solution)/shard_map/pallas_call | solution.py:72
  21.1 0.0 collective-permute-done.5.cot_far
  21.1 0.0 copy-done
  21.1 10.5 %shard_map.280 = (bf16[3,128,768]{2,1,0:T(8,128)(2,1)S(1)}, bf16[1,128,768]{2,1,0:T(8,128)(2,1)S(1)}, f32[384,768]{1,0:T(8,128)S(1)}, bf16[384,768]{1,0:T(8,128)(2,1)S(1)}, f32[8,768]{1,0:T(8,128)S(1)}) custom-call(f32[256,768]{1,0:T(8,128)S(1)} %get-tuple-element.106.hid_a, f32[128,768]{1,0:T(8,128)S(1)} %get-tuple-element.107.hid_b, ...), custom_call_target="tpu_custom_call" | custom-call | flops 13200000000 | tf_op jit(solution)/shard_map/pallas_call | solution.py:72
  31.6 5.2 %shard_map.281 = (f32[2,128,768]{2,1,0:T(8,128)S(1)}, bf16[2,128,768]{2,1,0:T(8,128)(2,1)S(1)}, f32[8,768]{1,0:T(8,128)S(1)}, bf16[6,128,128]{2,1,0:T(8,128)(2,1)S(1)}) custom-call(bf16[2,136,768]{2,1,0:T(8,128)(2,1)S(1)} %get-tuple-element.79.own, bf16[2,136,768]{2,1,0:T(8,128)(2,1)S(1)} %collective-permute-done.sib, ...), custom_call_target="tpu_custom_call" | custom-call | flops 6600000000 | tf_op jit(solution)/shard_map/pallas_call | solution.py:72
  36.8 0.6 collective-permute-start.6
  37.4 3.5 %shard_map.282 = (f32[1,128,768]{2,1,0:T(8,128)S(1)}, bf16[1,128,768]{2,1,0:T(8,128)(2,1)S(1)}, bf16[2,128,768]{2,1,0:T(8,128)(2,1)S(1)}, f32[8,768]{1,0:T(8,128)S(1)}) custom-call(bf16[2,136,768]{2,1,0:T(8,128)(2,1)S(1)} %get-tuple-element.79.own, bf16[2,136,768]{2,1,0:T(8,128)(2,1)S(1)} %collective-permute-done.sib, ...), custom_call_target="tpu_custom_call" | custom-call | flops 3960000000 | tf_op jit(solution)/shard_map/pallas_call | solution.py:72
  40.9 0.0 collective-permute-done.6.from_sib.sib_a
  40.9 0.1 collective-permute-start.7
  41.0 1.8 %collective-permute-start.10 = (f32[8,768]{1,0:T(8,128)S(1)}, f32[8,768]{1,0:T(8,128)S(1)}, u32[]{:S(2)}, u32[]{:S(2)}) collective-permute-start(f32[8,768]{1,0:T(8,128)S(1)} %get-tuple-element.137.a), channel_id=1, source_target_pairs={{0,16},{8,24},{16,0},{24,8},{1,17},{9,25},{17,1},{25,9},{2,18},{10... | collective-permute-start | bytes 73736 | tf_op jit(solution)/shard_map/ppermute | solution.py:517
  42.8 0.3 collective-permute-start.8
  43.1 0.0 collective-permute-done.7.from_sib_b.sib_b
  43.1 0.3 shard_map.283
  43.4 1.8 %collective-permute-start.9 = (bf16[2,128,768]{2,1,0:T(8,128)(2,1)S(1)}, bf16[2,128,768]{2,1,0:T(8,128)(2,1)S(1)}, u32[]{:S(2)}, u32[]{:S(2)}) collective-permute-start(bf16[2,128,768]{2,1,0:T(8,128)(2,1)S(1)} %shard_map.283), channel_id=1, source_target_pairs={{0,16},{8,24},{16,0},{24,8},{1,17},{9,25},{17,1},{25,9},{2,18},{10... | collective-permute-start | bytes 1179656 | tf_op jit(solution)/shard_map/ppermute | solution.py:517
  45.2 0.0 collective-permute-done.10.b
  45.2 1.6 %collective-permute-start.11 = (f32[8,768]{1,0:T(8,128)S(1)}, f32[8,768]{1,0:T(8,128)S(1)}, u32[]{:S(2)}, u32[]{:S(2)}) collective-permute-start(f32[8,768]{1,0:T(8,128)S(1)} %shard_map.286), channel_id=1, source_target_pairs={{0,1},{1,0},{2,3},{3,2},{4,5},{5,4},{6,7},{7,6},{8,9},{9,8},{10,11... | collective-permute-start | bytes 73736 | tf_op jit(solution)/shard_map/ppermute | solution.py:517
  46.8 2.3 %collective-permute-done.11 = f32[8,768]{1,0:T(8,128)S(1)} collective-permute-done((f32[8,768]{1,0:T(8,128)S(1)}, f32[8,768]{1,0:T(8,128)S(1)}, u32[]{:S(2)}, u32[]{:S(2)}) %collective-permute-start.11) | collective-permute-done | bytes 24608 | tf_op jit(solution)/shard_map/ppermute | solution.py:517
  49.1 1.6 %collective-permute-start.12 = (f32[8,768]{1,0:T(8,128)S(1)}, f32[8,768]{1,0:T(8,128)S(1)}, u32[]{:S(2)}, u32[]{:S(2)}) collective-permute-start(f32[8,768]{1,0:T(8,128)S(1)} %add.9), channel_id=1, source_target_pairs={{0,2},{1,3},{2,0},{3,1},{4,6},{5,7},{6,4},{7,5},{8,10},{9,11},{10,... | collective-permute-start | bytes 73736 | tf_op jit(solution)/shard_map/ppermute | solution.py:517
  50.7 2.3 %collective-permute-done.12 = f32[8,768]{1,0:T(8,128)S(1)} collective-permute-done((f32[8,768]{1,0:T(8,128)S(1)}, f32[8,768]{1,0:T(8,128)S(1)}, u32[]{:S(2)}, u32[]{:S(2)}) %collective-permute-start.12) | collective-permute-done | bytes 24608 | tf_op jit(solution)/shard_map/ppermute | solution.py:517
  52.9 0.0 collective-permute-start.13
  52.9 1.2 %collective-permute-done.13 = f32[8,768]{1,0:T(8,128)S(1)} collective-permute-done((f32[8,768]{1,0:T(8,128)S(1)}, f32[8,768]{1,0:T(8,128)S(1)}, u32[]{:S(2)}, u32[]{:S(2)}) %collective-permute-start.13) | collective-permute-done | bytes 24608 | tf_op jit(solution)/shard_map/ppermute | solution.py:517
  54.1 2.6 %collective-permute-start.14 = (f32[8,768]{1,0:T(8,128)S(1)}, f32[8,768]{1,0:T(8,128)S(1)}, u32[]{:S(2)}, u32[]{:S(2)}) collective-permute-start(f32[8,768]{1,0:T(8,128)S(1)} %add.11.near_pack), channel_id=1, source_target_pairs={{0,4},{1,5},{2,6},{3,7},{4,0},{5,1},{6,2},{7,3},{8,12},{9,13},{10,... | collective-permute-start | bytes 73736 | tf_op jit(solution)/shard_map/ppermute | solution.py:517
  56.7 1.2 %shard_map.284 = (bf16[3,128,768]{2,1,0:T(8,128)(2,1)}, bf16[3,128,768]{2,1,0:T(8,128)(2,1)}) custom-call(bf16[2,136,768]{2,1,0:T(8,128)(2,1)S(1)} %get-tuple-element.79.own, f32[2,128,768]{2,1,0:T(8,128)S(1)} %get-tuple-element.129.own_part.part_a, bf16[2,128,768]{2,1,0:T(8,128)(2,1)S(1)} %collective-permute-done.6.from_sib.sib_a, ...), custom_call_target="tpu_custom_call" | custom-call | flops 1100000000 | tf_op jit(solution)/shard_map/pallas_call | solution.py:72
  57.9 0.0 collective-permute-done.8.out_far
  57.9 0.2 collective-permute-done.9.back
  58.2 1.0 %shard_map.285 = (bf16[3,128,768]{2,1,0:T(8,128)(2,1)}, bf16[3,128,768]{2,1,0:T(8,128)(2,1)}) custom-call(bf16[2,136,768]{2,1,0:T(8,128)(2,1)S(1)} %get-tuple-element.79.own, f32[1,128,768]{2,1,0:T(8,128)S(1)} %get-tuple-element.123.part_b, ...), custom_call_target="tpu_custom_call", output_to_operand_aliasing={{0}: (7, {}), {1}: (8, {})} | custom-call | flops 1100000000 | tf_op jit(solution)/shard_map/pallas_call | solution.py:72
  59.2 0.0 collective-permute-done.14.far_pack
  59.2 0.7 %shard_map.287 = (f32[768]{0:T(1024)}, f32[768]{0:T(1024)}, f32[4,4,4]{2,1,0:T(4,128)}, f32[4,192]{1,0:T(4,128)}, f32[4,12]{1,0:T(4,128)}, /*index=5*/f32[4,12]{...) custom-call(f32[8,768]{1,0:T(8,128)S(1)} %add.11.near_pack, f32[8,768]{1,0:T(8,128)S(1)} %collective-permute-done.14.far_pack, ...), custom_call_target="tpu_custom_call" | custom-call | flops 550000000 | tf_op jit(solution)/shard_map/pallas_call | solution.py:72
  (4 shorter events, 0.0 us)
Async XLA Ops:
  2.0 9.6 %collective-permute-start.1 = (bf16[1,136,768]{2,1,0:T(8,128)(2,1)S(1)}, bf16[1,136,768]{2,1,0:T(8,128)(2,1)S(1)}, u32[]{:S(2)}, u32[]{:S(2)}) collective-permute-start(bf16[1,136,768]{2,1,0:T(8,128)(2,1)S(1)} %get-tuple-element.80), channel_id=1, source_target_pairs={{0,16},{8,24},{16,0},{24,8},{1,17},{9,25},{17,1},{25,9},{2,18},{10... | collective-permute-start | bytes 626696 | tf_op jit(solution)/shard_map/ppermute | solution.py:517
  5.0 9.6 %collective-permute-start.3 = (bf16[1,136,768]{2,1,0:T(8,128)(2,1)S(1)}, bf16[1,136,768]{2,1,0:T(8,128)(2,1)S(1)}, u32[]{:S(2)}, u32[]{:S(2)}) collective-permute-start(bf16[1,136,768]{2,1,0:T(8,128)(2,1)S(1)} %get-tuple-element.87), channel_id=1, source_target_pairs={{0,16},{8,24},{16,0},{24,8},{1,17},{9,25},{17,1},{25,9},{2,18},{10... | collective-permute-start | bytes 626696 | tf_op jit(solution)/shard_map/ppermute | solution.py:517
  5.1 4.6 %collective-permute-start = (bf16[2,136,768]{2,1,0:T(8,128)(2,1)S(1)}, bf16[2,136,768]{2,1,0:T(8,128)(2,1)S(1)}, u32[]{:S(2)}, u32[]{:S(2)}) collective-permute-start(bf16[2,136,768]{2,1,0:T(8,128)(2,1)S(1)} %get-tuple-element.79.own), channel_id=1, source_target_pairs={{0,8},{8,0},{16,24},{24,16},{1,9},{9,1},{17,25},{25,17},{2,10},{10... | collective-permute-start | bytes 1253384 | tf_op jit(solution)/shard_map/ppermute | solution.py:517
  11.6 3.1 %collective-permute-start.2 = (bf16[1,136,768]{2,1,0:T(8,128)(2,1)S(1)}, bf16[1,136,768]{2,1,0:T(8,128)(2,1)S(1)}, u32[]{:S(2)}, u32[]{:S(2)}) collective-permute-start(bf16[1,136,768]{2,1,0:T(8,128)(2,1)S(1)} %collective-permute-done.1.far), channel_id=1, source_target_pairs={{0,8},{8,0},{16,24},{24,16},{1,9},{9,1},{17,25},{25,17},{2,10},{10... | collective-permute-start | bytes 626696 | tf_op jit(solution)/shard_map/ppermute | solution.py:517
  12.1 8.9 %collective-permute-start.5 = (bf16[1,128,768]{2,1,0:T(8,128)(2,1)S(1)}, bf16[1,128,768]{2,1,0:T(8,128)(2,1)S(1)}, u32[]{:S(2)}, u32[]{:S(2)}) collective-permute-start(bf16[1,128,768]{2,1,0:T(8,128)(2,1)S(1)} %get-tuple-element.108), channel_id=1, source_target_pairs={{0,16},{8,24},{16,0},{24,8},{1,17},{9,25},{17,1},{25,9},{2,18},{10... | collective-permute-start | bytes 589832 | tf_op jit(solution)/shard_map/ppermute | solution.py:517
  14.7 3.9 %collective-permute-start.4 = (bf16[1,136,768]{2,1,0:T(8,128)(2,1)S(1)}, bf16[1,136,768]{2,1,0:T(8,128)(2,1)S(1)}, u32[]{:S(2)}, u32[]{:S(2)}) collective-permute-start(bf16[1,136,768]{2,1,0:T(8,128)(2,1)S(1)} %collective-permute-done.3.far), channel_id=1, source_target_pairs={{0,8},{8,0},{16,24},{24,16},{1,9},{9,1},{17,25},{25,17},{2,10},{10... | collective-permute-start | bytes 626696 | tf_op jit(solution)/shard_map/ppermute | solution.py:517
  18.6 2.5 %copy-start = (bf16[3,128,768]{2,1,0:T(8,128)(2,1)S(1)}, bf16[3,128,768]{2,1,0:T(8,128)(2,1)}, u32[]{:S(2)}) copy-start(bf16[3,128,768]{2,1,0:T(8,128)(2,1)} %cot.1) | copy-start | bytes 1769476
  36.8 4.1 %collective-permute-start.6 = (bf16[2,128,768]{2,1,0:T(8,128)(2,1)S(1)}, bf16[2,128,768]{2,1,0:T(8,128)(2,1)S(1)}, u32[]{:S(2)}, u32[]{:S(2)}) collective-permute-start(bf16[2,128,768]{2,1,0:T(8,128)(2,1)S(1)} %get-tuple-element.125), channel_id=1, source_target_pairs={{0,8},{8,0},{16,24},{24,16},{1,9},{9,1},{17,25},{25,17},{2,10},{10... | collective-permute-start | bytes 1179656 | tf_op jit(solution)/shard_map/ppermute | solution.py:517
  40.9 2.2 %collective-permute-start.7 = (bf16[2,128,768]{2,1,0:T(8,128)(2,1)S(1)}, bf16[2,128,768]{2,1,0:T(8,128)(2,1)S(1)}, u32[]{:S(2)}, u32[]{:S(2)}) collective-permute-start(bf16[2,128,768]{2,1,0:T(8,128)(2,1)S(1)} %get-tuple-element.126), channel_id=1, source_target_pairs={{0,8},{8,0},{16,24},{24,16},{1,9},{9,1},{17,25},{25,17},{2,10},{10... | collective-permute-start | bytes 1179656 | tf_op jit(solution)/shard_map/ppermute | solution.py:517
  41.0 4.2 %collective-permute-start.10 = (f32[8,768]{1,0:T(8,128)S(1)}, f32[8,768]{1,0:T(8,128)S(1)}, u32[]{:S(2)}, u32[]{:S(2)}) collective-permute-start(f32[8,768]{1,0:T(8,128)S(1)} %get-tuple-element.137.a), channel_id=1, source_target_pairs={{0,16},{8,24},{16,0},{24,8},{1,17},{9,25},{17,1},{25,9},{2,18},{10... | collective-permute-start | bytes 73736 | tf_op jit(solution)/shard_map/ppermute | solution.py:517
  42.8 15.2 %collective-permute-start.8 = (bf16[1,128,768]{2,1,0:T(8,128)(2,1)S(1)}, bf16[1,128,768]{2,1,0:T(8,128)(2,1)S(1)}, u32[]{:S(2)}, u32[]{:S(2)}) collective-permute-start(bf16[1,128,768]{2,1,0:T(8,128)(2,1)S(1)} %get-tuple-element.128), channel_id=1, source_target_pairs={{0,16},{8,24},{16,0},{24,8},{1,17},{9,25},{17,1},{25,9},{2,18},{10... | collective-permute-start | bytes 589832 | tf_op jit(solution)/shard_map/ppermute | solution.py:517
  43.4 14.8 %collective-permute-start.9 = (bf16[2,128,768]{2,1,0:T(8,128)(2,1)S(1)}, bf16[2,128,768]{2,1,0:T(8,128)(2,1)S(1)}, u32[]{:S(2)}, u32[]{:S(2)}) collective-permute-start(bf16[2,128,768]{2,1,0:T(8,128)(2,1)S(1)} %shard_map.283), channel_id=1, source_target_pairs={{0,16},{8,24},{16,0},{24,8},{1,17},{9,25},{17,1},{25,9},{2,18},{10... | collective-permute-start | bytes 1179656 | tf_op jit(solution)/shard_map/ppermute | solution.py:517
  45.2 3.9 %collective-permute-start.11 = (f32[8,768]{1,0:T(8,128)S(1)}, f32[8,768]{1,0:T(8,128)S(1)}, u32[]{:S(2)}, u32[]{:S(2)}) collective-permute-start(f32[8,768]{1,0:T(8,128)S(1)} %shard_map.286), channel_id=1, source_target_pairs={{0,1},{1,0},{2,3},{3,2},{4,5},{5,4},{6,7},{7,6},{8,9},{9,8},{10,11... | collective-permute-start | bytes 73736 | tf_op jit(solution)/shard_map/ppermute | solution.py:517
  49.1 3.8 %collective-permute-start.12 = (f32[8,768]{1,0:T(8,128)S(1)}, f32[8,768]{1,0:T(8,128)S(1)}, u32[]{:S(2)}, u32[]{:S(2)}) collective-permute-start(f32[8,768]{1,0:T(8,128)S(1)} %add.9), channel_id=1, source_target_pairs={{0,2},{1,3},{2,0},{3,1},{4,6},{5,7},{6,4},{7,5},{8,10},{9,11},{10,... | collective-permute-start | bytes 73736 | tf_op jit(solution)/shard_map/ppermute | solution.py:517
  52.9 1.2 %collective-permute-start.13 = (f32[8,768]{1,0:T(8,128)S(1)}, f32[8,768]{1,0:T(8,128)S(1)}, u32[]{:S(2)}, u32[]{:S(2)}) collective-permute-start(f32[8,768]{1,0:T(8,128)S(1)} %add.10), channel_id=1, source_target_pairs={{0,8},{8,0},{16,24},{24,16},{1,9},{9,1},{17,25},{25,17},{2,10},{10... | collective-permute-start | bytes 73736 | tf_op jit(solution)/shard_map/ppermute | solution.py:517
  54.1 5.0 %collective-permute-start.14 = (f32[8,768]{1,0:T(8,128)S(1)}, f32[8,768]{1,0:T(8,128)S(1)}, u32[]{:S(2)}, u32[]{:S(2)}) collective-permute-start(f32[8,768]{1,0:T(8,128)S(1)} %add.11.near_pack), channel_id=1, source_target_pairs={{0,4},{1,5},{2,6},{3,7},{4,0},{5,1},{6,2},{7,3},{8,12},{9,13},{10,... | collective-permute-start | bytes 73736 | tf_op jit(solution)/shard_map/ppermute | solution.py:517

commit v6 on v5

--- a/solution.py
+++ b/solution.py
@@ -471,7 +471,8 @@
     back[1] = norm_back(far[0, :shard], grad, hidden_grad[shard : 2 * shard, :], gain).astype(BF16)
 
 
-def own_rows_kernel(own, part_a, sib_a, hidden_grad, gain, out, output, grad_input):
+def own_rows_kernel(own, part_a, sib_a, hidden_grad, gain, out, output, grad_input, mark):
+    mark[...] = jnp.zeros(mark.shape, F32)
     rows, shard, width = out.shape
     row = moved_row(rows)
     output[row] = out[0]
@@ -651,15 +652,17 @@
     back = exchange(back, "seq", 2)
     out_far = exchange(out_send, "seq", 2)
     (pack,) = call(add_kernel, [((8, width), F32)], (pack, exchange(pack, "seq", 2)), 4, 10.0)
-    bit = 1
+    first, second, third = (exchange(pack, "batch", k) for k in (1, 2, 3))
+    pack = (pack + first) + (second + third)
+    bit = 4
     while 2 * bit < lax.axis_size("batch"):
         pack = pack + exchange(pack, "batch", bit)
         bit *= 2
     pack = pack + exchange(pack, "seq", 1)
     far_pack = exchange(pack, "batch", bit)
     rowed = ((rows, shard, width), BF16)
-    output, grad_input = call(
-        own_rows_kernel, [rowed, rowed], (own, part_a, sib_a, hidden_grad, gain1, out), 16, 1.0, last=True
+    output, grad_input, mark = call(
+        own_rows_kernel, [rowed, rowed, ((8, 128), F32)], (own, part_a, sib_a, hidden_grad, gain1, out), 16, 0.0, last=True
     )
     output, grad_input = call(
         last_kernel,
@@ -678,7 +681,7 @@
             ((width,), F32), ((width,), F32), ((ranks, ranks, ranks), F32), ((ranks, outer), F32),
             ((ranks, inner), F32), ((ranks, inner), F32), ((ranks, outer), F32), ((mid,), F32), ((width,), F32),
         ],
-        (pack, far_pack, Far(grad_input)),
+        (pack, far_pack, Far(mark)),
         8,
         0.5,
         last=True,

time: 60.1 us -> 60 us (level)
  waiting for transfers between devices: 6.64 us -> 3.97 us
  starting transfers between devices: 15.9 us -> 17.7 us
    ppermute x15 -> x16, waiting for transfers between devices: 6.64 us -> 3.97 us  [exchange(): return lax.ppermute(value, axis, [(k, k ^ bit) for k in range(count)])]
    ppermute x15 -> x16, starting transfers between devices: 15.9 us -> 17.7 us  [exchange(): return lax.ppermute(value, axis, [(k, k ^ bit) for k in range(count)])]
  transfers between devices with their start and end apart: 15 -> 16, of which waited for: 5 -> 6; matrix products, arithmetic and copies ran while one was open for 0% -> 0% of each run, Pallas kernels for 31% -> 31%
where the time goes in v6:
time: 60 us; the launch traced here: 59.8 us
  Pallas kernels  36.5 us (61%)
  starting transfers between devices  17.7 us (30%)
  waiting for transfers between devices  3.97 us (7%)
  between operations  0.98 us (2%)
  local copies, waits for them, and re-layouts  0.6 us (1%)
    pallas_call x13, Pallas kernels, call(): pl.pallas_call(kernel, out_shape=[made(shape, kind) for shape, kind in ou...  36.5 us
    ppermute x16, starting transfers between devices, exchange(): return lax.ppermute(value, axis, [(k, k ^ bit) for k in range(count)])  17.7 us
    ppermute x16, waiting for transfers between devices, exchange(): return lax.ppermute(value, axis, [(k, k ^ bit) for k in range(count)])  3.97 us
  transfers between devices with their start and end apart: 16, of which 6 were waited for; matrix products, arithmetic and copies ran while one was open for 0% of the time, Pallas kernels for 31%

profile of v6, /device:TPU:0, one launch (start us, length us, event | category | flops | bytes accessed | tf_op | source)
XLA Modules:
  0.0 59.8 jit_solution(3702860799818574910)
XLA Ops:
  0.6 1.3 %shard_map.275 = (bf16[2,136,768]{2,1,0:T(8,128)(2,1)S(1)}, bf16[1,136,768]{2,1,0:T(8,128)(2,1)S(1)}, bf16[1,136,768]{2,1,0:T(8,128)(2,1)S(1)}, bf16[1,128,768]{2,1,0:T(8,128)(2,1)S(1)}) custom-call(bf16[3,128,768]{2,1,0:T(8,128)(2,1)} %inputs.1, bf16[3,128,768]{2,1,0:T(8,128)(2,1)} %cot.1, s32[3,128]{1,0:T(4,128)} %segment_ids.1), custom_call_target="tpu_custom_call" | custom-call | flops 1100000000 | tf_op jit(solution)/shard_map/pallas_call | solution.py:72
  2.0 3.0 %collective-permute-start.1 = (bf16[1,136,768]{2,1,0:T(8,128)(2,1)S(1)}, bf16[1,136,768]{2,1,0:T(8,128)(2,1)S(1)}, u32[]{:S(2)}, u32[]{:S(2)}) collective-permute-start(bf16[1,136,768]{2,1,0:T(8,128)(2,1)S(1)} %get-tuple-element.81), channel_id=1, source_target_pairs={{0,16},{8,24},{16,0},{24,8},{1,17},{9,25},{17,1},{25,9},{2,18},{10... | collective-permute-start | bytes 626696 | tf_op jit(solution)/shard_map/ppermute | solution.py:518
  5.0 0.1 collective-permute-start.3
  5.1 0.0 collective-permute-start
  5.1 4.6 %shard_map.276 = (f32[7,6,256,128]{3,2,1,0:T(8,128)S(1)}, bf16[48,768]{1,0:T(8,128)(2,1)S(1)}, bf16[48,768]{1,0:T(8,128)(2,1)S(1)}, f32[32,96]{1,0:T(8,128)S(1)}...) custom-call(s32[1023]{0:T(1024)} %table_far.1, ...), custom_call_target="tpu_custom_call" | custom-call | flops 22000001024 | tf_op jit(solution)/shard_map/pallas_call | solution.py:72
  9.7 0.0 collective-permute-done.sib
  9.7 1.8 %shard_map.277 = (bf16[6,512,128]{2,1,0:T(8,128)(2,1)S(1)}, bf16[6,512,128]{2,1,0:T(8,128)(2,1)S(1)}, bf16[6,256,128]{2,1,0:T(8,128)(2,1)S(1)}) custom-call(bf16[2,136,768]{2,1,0:T(8,128)(2,1)S(1)} %get-tuple-element.80.own, bf16[2,136,768]{2,1,0:T(8,128)(2,1)S(1)} %collective-permute-done.sib, bf16[768,768]{1,0:T(8,128)(2,1)S(1)} %get-tuple-element.82.wq.rest_1_.rest_0_, ...), custom_call_target="tpu_custom_call" | custom-call | flops 22000001024 | tf_op jit(solution)/shard_map/pallas_call | solution.py:72
  11.5 0.0 collective-permute-done.1.far
  11.6 0.6 collective-permute-start.2
  12.1 1.9 %collective-permute-start.5 = (bf16[1,128,768]{2,1,0:T(8,128)(2,1)S(1)}, bf16[1,128,768]{2,1,0:T(8,128)(2,1)S(1)}, u32[]{:S(2)}, u32[]{:S(2)}) collective-permute-start(bf16[1,128,768]{2,1,0:T(8,128)(2,1)S(1)} %get-tuple-element.109), channel_id=1, source_target_pairs={{0,16},{8,24},{16,0},{24,8},{1,17},{9,25},{17,1},{25,9},{2,18},{10... | collective-permute-start | bytes 589832 | tf_op jit(solution)/shard_map/ppermute | solution.py:518
  14.1 0.6 collective-permute-done.3.far
  14.7 0.0 collective-permute-done.2.far_sib
  14.7 0.0 collective-permute-start.4
  14.7 3.9 %shard_map.279 = (bf16[6,256,128]{2,1,0:T(8,128)(2,1)S(1)}, bf16[6,256,128]{2,1,0:T(8,128)(2,1)S(1)}, bf16[6,128,128]{2,1,0:T(8,128)(2,1)S(1)}, bf16[12,256,512]...) custom-call(bf16[2,136,768]{2,1,0:T(8,128)(2,1)S(1)} %get-tuple-elem, ...), custom_call_target="tpu_custom_call" | custom-call | flops 3300000000 | tf_op jit(solution)/shard_map/pallas_call | solution.py:72
  18.6 0.0 copy-start
  18.6 0.0 collective-permute-done.4.far_sib
  18.6 2.4 %shard_map.278 = (bf16[6,256,128]{2,1,0:T(8,128)(2,1)S(1)}, bf16[6,256,128]{2,1,0:T(8,128)(2,1)S(1)}, bf16[6,256,512]{2,1,0:T(8,128)(2,1)S(1)}, f32[6,128,128]{2...) custom-call(bf16[2,136,768]{2,1,0:T(8,128)(2,1)S(1)} %get-tuple-element.80.own, ...), custom_call_target="tpu_custom_call" | custom-call | flops 3300000000 | tf_op jit(solution)/shard_map/pallas_call | solution.py:72
  21.1 0.0 collective-permute-done.5.cot_far
  21.1 0.0 copy-done
  21.1 10.5 %shard_map.280 = (bf16[3,128,768]{2,1,0:T(8,128)(2,1)S(1)}, bf16[1,128,768]{2,1,0:T(8,128)(2,1)S(1)}, f32[384,768]{1,0:T(8,128)S(1)}, bf16[384,768]{1,0:T(8,128)(2,1)S(1)}, f32[8,768]{1,0:T(8,128)S(1)}) custom-call(f32[256,768]{1,0:T(8,128)S(1)} %get-tuple-element.107.hid_a, f32[128,768]{1,0:T(8,128)S(1)} %get-tuple-element.108.hid_b, ...), custom_call_target="tpu_custom_call" | custom-call | flops 13200000000 | tf_op jit(solution)/shard_map/pallas_call | solution.py:72
  31.6 5.2 %shard_map.281 = (f32[2,128,768]{2,1,0:T(8,128)S(1)}, bf16[2,128,768]{2,1,0:T(8,128)(2,1)S(1)}, f32[8,768]{1,0:T(8,128)S(1)}, bf16[6,128,128]{2,1,0:T(8,128)(2,1)S(1)}) custom-call(bf16[2,136,768]{2,1,0:T(8,128)(2,1)S(1)} %get-tuple-element.80.own, bf16[2,136,768]{2,1,0:T(8,128)(2,1)S(1)} %collective-permute-done.sib, ...), custom_call_target="tpu_custom_call" | custom-call | flops 6600000000 | tf_op jit(solution)/shard_map/pallas_call | solution.py:72
  36.8 0.6 collective-permute-start.6
  37.4 3.5 %shard_map.282 = (f32[1,128,768]{2,1,0:T(8,128)S(1)}, bf16[1,128,768]{2,1,0:T(8,128)(2,1)S(1)}, bf16[2,128,768]{2,1,0:T(8,128)(2,1)S(1)}, f32[8,768]{1,0:T(8,128)S(1)}) custom-call(bf16[2,136,768]{2,1,0:T(8,128)(2,1)S(1)} %get-tuple-element.80.own, bf16[2,136,768]{2,1,0:T(8,128)(2,1)S(1)} %collective-permute-done.sib, ...), custom_call_target="tpu_custom_call" | custom-call | flops 3960000000 | tf_op jit(solution)/shard_map/pallas_call | solution.py:72
  40.9 0.0 collective-permute-done.6.from_sib.sib_a
  40.9 0.1 collective-permute-start.7
  41.0 1.8 %collective-permute-start.10 = (f32[8,768]{1,0:T(8,128)S(1)}, f32[8,768]{1,0:T(8,128)S(1)}, u32[]{:S(2)}, u32[]{:S(2)}) collective-permute-start(f32[8,768]{1,0:T(8,128)S(1)} %get-tuple-element.138.a), channel_id=1, source_target_pairs={{0,16},{8,24},{16,0},{24,8},{1,17},{9,25},{17,1},{25,9},{2,18},{10... | collective-permute-start | bytes 73736 | tf_op jit(solution)/shard_map/ppermute | solution.py:518
  42.8 0.0 collective-permute-done.7.from_sib_b.sib_b
  42.8 0.3 shard_map.283
  43.1 1.7 %collective-permute-start.9 = (bf16[2,128,768]{2,1,0:T(8,128)(2,1)S(1)}, bf16[2,128,768]{2,1,0:T(8,128)(2,1)S(1)}, u32[]{:S(2)}, u32[]{:S(2)}) collective-permute-start(bf16[2,128,768]{2,1,0:T(8,128)(2,1)S(1)} %shard_map.283), channel_id=1, source_target_pairs={{0,16},{8,24},{16,0},{24,8},{1,17},{9,25},{17,1},{25,9},{2,18},{10... | collective-permute-start | bytes 1179656 | tf_op jit(solution)/shard_map/ppermute | solution.py:518
  44.8 0.1 collective-permute-done.10.b
  44.9 2.7 %collective-permute-start.13 = (f32[8,768]{1,0:T(8,128)S(1)}, f32[8,768]{1,0:T(8,128)S(1)}, u32[]{:S(2)}, u32[]{:S(2)}) collective-permute-start(f32[8,768]{1,0:T(8,128)S(1)} %shard_map.286), channel_id=1, source_target_pairs={{0,3},{1,2},{2,1},{3,0},{4,7},{5,6},{6,5},{7,4},{8,11},{9,10},{10,... | collective-permute-start | bytes 73736 | tf_op jit(solution)/shard_map/ppermute | solution.py:518
  47.6 0.4 collective-permute-start.12
  48.0 0.3 collective-permute-start.11
  48.4 1.7 %collective-permute-start.8 = (bf16[1,128,768]{2,1,0:T(8,128)(2,1)S(1)}, bf16[1,128,768]{2,1,0:T(8,128)(2,1)S(1)}, u32[]{:S(2)}, u32[]{:S(2)}) collective-permute-start(bf16[1,128,768]{2,1,0:T(8,128)(2,1)S(1)} %get-tuple-element.129), channel_id=1, source_target_pairs={{0,16},{8,24},{16,0},{24,8},{1,17},{9,25},{17,1},{25,9},{2,18},{10... | collective-permute-start | bytes 589832 | tf_op jit(solution)/shard_map/ppermute | solution.py:518
  50.1 0.0 collective-permute-done.13
  50.1 1.3 %collective-permute-done.12 = f32[8,768]{1,0:T(8,128)S(1)} collective-permute-done((f32[8,768]{1,0:T(8,128)S(1)}, f32[8,768]{1,0:T(8,128)S(1)}, u32[]{:S(2)}, u32[]{:S(2)}) %collective-permute-start.12) | collective-permute-done | bytes 24608 | tf_op jit(solution)/shard_map/ppermute | solution.py:518
  51.4 0.4 collective-permute-done.11
  51.9 0.1 collective-permute-start.14
  52.0 1.2 %collective-permute-done.14 = f32[8,768]{1,0:T(8,128)S(1)} collective-permute-done((f32[8,768]{1,0:T(8,128)S(1)}, f32[8,768]{1,0:T(8,128)S(1)}, u32[]{:S(2)}, u32[]{:S(2)}) %collective-permute-start.14) | collective-permute-done | bytes 24608 | tf_op jit(solution)/shard_map/ppermute | solution.py:518
  53.1 2.6 %collective-permute-start.15 = (f32[8,768]{1,0:T(8,128)S(1)}, f32[8,768]{1,0:T(8,128)S(1)}, u32[]{:S(2)}, u32[]{:S(2)}) collective-permute-start(f32[8,768]{1,0:T(8,128)S(1)} %add.15.near_pack), channel_id=1, source_target_pairs={{0,4},{1,5},{2,6},{3,7},{4,0},{5,1},{6,2},{7,3},{8,12},{9,13},{10,... | collective-permute-start | bytes 73736 | tf_op jit(solution)/shard_map/ppermute | solution.py:518
  55.8 1.2 %shard_map.284 = (bf16[3,128,768]{2,1,0:T(8,128)(2,1)}, bf16[3,128,768]{2,1,0:T(8,128)(2,1)}, f32[8,128]{1,0:T(8,128)S(1)}) custom-call(bf16[2,136,768]{2,1,0:T(8,128)(2,1)S(1)} %get-tuple-element.80.own, f32[2,128,768]{2,1,0:T(8,128)S(1)} %get-tuple-element.130.own_part.part_a, bf16[2,128,768]{2,1,0:T(8,128)(2,1)S(1)} %collective-permute-done.6.from_sib.sib_a, ...), custom_call_target="tpu_custom_call" | custom-call | tf_op jit(solution)/shard_map/pallas_call | solution.py:72
  57.0 0.0 copy-start.1
  57.0 0.6 copy-done.1
  57.6 0.3 collective-permute-done.15.far_pack
  57.9 0.7 %shard_map.287 = (f32[768]{0:T(1024)}, f32[768]{0:T(1024)}, f32[4,4,4]{2,1,0:T(4,128)}, f32[4,192]{1,0:T(4,128)}, f32[4,12]{1,0:T(4,128)}, /*index=5*/f32[4,12]{...) custom-call(f32[8,768]{1,0:T(8,128)S(1)} %add.15.near_pack, f32[8,768]{1,0:T(8,128)S(1)} %collective-permute-done.15.far_pack, ...), custom_call_target="tpu_custom_call" | custom-call | flops 550000000 | tf_op jit(solution)/shard_map/pallas_call | solution.py:72
  58.6 0.0 collective-permute-done.8.out_far
  58.6 0.0 collective-permute-done.9.back
  58.6 1.0 %shard_map.285 = (bf16[3,128,768]{2,1,0:T(8,128)(2,1)}, bf16[3,128,768]{2,1,0:T(8,128)(2,1)}) custom-call(bf16[2,136,768]{2,1,0:T(8,128)(2,1)S(1)} %get-tuple-element.80.own, f32[1,128,768]{2,1,0:T(8,128)S(1)} %get-tuple-element.124.part_b, ...), custom_call_target="tpu_custom_call", output_to_operand_aliasing={{0}: (7, {}), {1}: (8, {})} | custom-call | flops 1100000000 | tf_op jit(solution)/shard_map/pallas_call | solution.py:72
  (3 shorter events, 0.0 us)
Async XLA Ops:
  2.0 9.5 %collective-permute-start.1 = (bf16[1,136,768]{2,1,0:T(8,128)(2,1)S(1)}, bf16[1,136,768]{2,1,0:T(8,128)(2,1)S(1)}, u32[]{:S(2)}, u32[]{:S(2)}) collective-permute-start(bf16[1,136,768]{2,1,0:T(8,128)(2,1)S(1)} %get-tuple-element.81), channel_id=1, source_target_pairs={{0,16},{8,24},{16,0},{24,8},{1,17},{9,25},{17,1},{25,9},{2,18},{10... | collective-permute-start | bytes 626696 | tf_op jit(solution)/shard_map/ppermute | solution.py:518
  5.0 9.6 %collective-permute-start.3 = (bf16[1,136,768]{2,1,0:T(8,128)(2,1)S(1)}, bf16[1,136,768]{2,1,0:T(8,128)(2,1)S(1)}, u32[]{:S(2)}, u32[]{:S(2)}) collective-permute-start(bf16[1,136,768]{2,1,0:T(8,128)(2,1)S(1)} %get-tuple-element.88), channel_id=1, source_target_pairs={{0,16},{8,24},{16,0},{24,8},{1,17},{9,25},{17,1},{25,9},{2,18},{10... | collective-permute-start | bytes 626696 | tf_op jit(solution)/shard_map/ppermute | solution.py:518
  5.1 4.6 %collective-permute-start = (bf16[2,136,768]{2,1,0:T(8,128)(2,1)S(1)}, bf16[2,136,768]{2,1,0:T(8,128)(2,1)S(1)}, u32[]{:S(2)}, u32[]{:S(2)}) collective-permute-start(bf16[2,136,768]{2,1,0:T(8,128)(2,1)S(1)} %get-tuple-element.80.own), channel_id=1, source_target_pairs={{0,8},{8,0},{16,24},{24,16},{1,9},{9,1},{17,25},{25,17},{2,10},{10... | collective-permute-start | bytes 1253384 | tf_op jit(solution)/shard_map/ppermute | solution.py:518
  11.6 3.1 %collective-permute-start.2 = (bf16[1,136,768]{2,1,0:T(8,128)(2,1)S(1)}, bf16[1,136,768]{2,1,0:T(8,128)(2,1)S(1)}, u32[]{:S(2)}, u32[]{:S(2)}) collective-permute-start(bf16[1,136,768]{2,1,0:T(8,128)(2,1)S(1)} %collective-permute-done.1.far), channel_id=1, source_target_pairs={{0,8},{8,0},{16,24},{24,16},{1,9},{9,1},{17,25},{25,17},{2,10},{10... | collective-permute-start | bytes 626696 | tf_op jit(solution)/shard_map/ppermute | solution.py:518
  12.1 8.9 %collective-permute-start.5 = (bf16[1,128,768]{2,1,0:T(8,128)(2,1)S(1)}, bf16[1,128,768]{2,1,0:T(8,128)(2,1)S(1)}, u32[]{:S(2)}, u32[]{:S(2)}) collective-permute-start(bf16[1,128,768]{2,1,0:T(8,128)(2,1)S(1)} %get-tuple-element.109), channel_id=1, source_target_pairs={{0,16},{8,24},{16,0},{24,8},{1,17},{9,25},{17,1},{25,9},{2,18},{10... | collective-permute-start | bytes 589832 | tf_op jit(solution)/shard_map/ppermute | solution.py:518
  14.7 4.0 %collective-permute-start.4 = (bf16[1,136,768]{2,1,0:T(8,128)(2,1)S(1)}, bf16[1,136,768]{2,1,0:T(8,128)(2,1)S(1)}, u32[]{:S(2)}, u32[]{:S(2)}) collective-permute-start(bf16[1,136,768]{2,1,0:T(8,128)(2,1)S(1)} %collective-permute-done.3.far), channel_id=1, source_target_pairs={{0,8},{8,0},{16,24},{24,16},{1,9},{9,1},{17,25},{25,17},{2,10},{10... | collective-permute-start | bytes 626696 | tf_op jit(solution)/shard_map/ppermute | solution.py:518
  18.6 2.5 %copy-start = (bf16[3,128,768]{2,1,0:T(8,128)(2,1)S(1)}, bf16[3,128,768]{2,1,0:T(8,128)(2,1)}, u32[]{:S(2)}) copy-start(bf16[3,128,768]{2,1,0:T(8,128)(2,1)} %cot.1) | copy-start | bytes 1769476
  36.8 4.1 %collective-permute-start.6 = (bf16[2,128,768]{2,1,0:T(8,128)(2,1)S(1)}, bf16[2,128,768]{2,1,0:T(8,128)(2,1)S(1)}, u32[]{:S(2)}, u32[]{:S(2)}) collective-permute-start(bf16[2,128,768]{2,1,0:T(8,128)(2,1)S(1)} %get-tuple-element.126), channel_id=1, source_target_pairs={{0,8},{8,0},{16,24},{24,16},{1,9},{9,1},{17,25},{25,17},{2,10},{10... | collective-permute-start | bytes 1179656 | tf_op jit(solution)/shard_map/ppermute | solution.py:518
  40.9 1.9 %collective-permute-start.7 = (bf16[2,128,768]{2,1,0:T(8,128)(2,1)S(1)}, bf16[2,128,768]{2,1,0:T(8,128)(2,1)S(1)}, u32[]{:S(2)}, u32[]{:S(2)}) collective-permute-start(bf16[2,128,768]{2,1,0:T(8,128)(2,1)S(1)} %get-tuple-element.127), channel_id=1, source_target_pairs={{0,8},{8,0},{16,24},{24,16},{1,9},{9,1},{17,25},{25,17},{2,10},{10... | collective-permute-start | bytes 1179656 | tf_op jit(solution)/shard_map/ppermute | solution.py:518
  41.0 3.9 %collective-permute-start.10 = (f32[8,768]{1,0:T(8,128)S(1)}, f32[8,768]{1,0:T(8,128)S(1)}, u32[]{:S(2)}, u32[]{:S(2)}) collective-permute-start(f32[8,768]{1,0:T(8,128)S(1)} %get-tuple-element.138.a), channel_id=1, source_target_pairs={{0,16},{8,24},{16,0},{24,8},{1,17},{9,25},{17,1},{25,9},{2,18},{10... | collective-permute-start | bytes 73736 | tf_op jit(solution)/shard_map/ppermute | solution.py:518
  43.1 15.5 %collective-permute-start.9 = (bf16[2,128,768]{2,1,0:T(8,128)(2,1)S(1)}, bf16[2,128,768]{2,1,0:T(8,128)(2,1)S(1)}, u32[]{:S(2)}, u32[]{:S(2)}) collective-permute-start(bf16[2,128,768]{2,1,0:T(8,128)(2,1)S(1)} %shard_map.283), channel_id=1, source_target_pairs={{0,16},{8,24},{16,0},{24,8},{1,17},{9,25},{17,1},{25,9},{2,18},{10... | collective-permute-start | bytes 1179656 | tf_op jit(solution)/shard_map/ppermute | solution.py:518
  44.9 5.2 %collective-permute-start.13 = (f32[8,768]{1,0:T(8,128)S(1)}, f32[8,768]{1,0:T(8,128)S(1)}, u32[]{:S(2)}, u32[]{:S(2)}) collective-permute-start(f32[8,768]{1,0:T(8,128)S(1)} %shard_map.286), channel_id=1, source_target_pairs={{0,3},{1,2},{2,1},{3,0},{4,7},{5,6},{6,5},{7,4},{8,11},{9,10},{10,... | collective-permute-start | bytes 73736 | tf_op jit(solution)/shard_map/ppermute | solution.py:518
  47.6 3.8 %collective-permute-start.12 = (f32[8,768]{1,0:T(8,128)S(1)}, f32[8,768]{1,0:T(8,128)S(1)}, u32[]{:S(2)}, u32[]{:S(2)}) collective-permute-start(f32[8,768]{1,0:T(8,128)S(1)} %shard_map.286), channel_id=1, source_target_pairs={{0,2},{1,3},{2,0},{3,1},{4,6},{5,7},{6,4},{7,5},{8,10},{9,11},{10,... | collective-permute-start | bytes 73736 | tf_op jit(solution)/shard_map/ppermute | solution.py:518
  48.0 3.8 %collective-permute-start.11 = (f32[8,768]{1,0:T(8,128)S(1)}, f32[8,768]{1,0:T(8,128)S(1)}, u32[]{:S(2)}, u32[]{:S(2)}) collective-permute-start(f32[8,768]{1,0:T(8,128)S(1)} %shard_map.286), channel_id=1, source_target_pairs={{0,1},{1,0},{2,3},{3,2},{4,5},{5,4},{6,7},{7,6},{8,9},{9,8},{10,11... | collective-permute-start | bytes 73736 | tf_op jit(solution)/shard_map/ppermute | solution.py:518
  48.4 10.2 %collective-permute-start.8 = (bf16[1,128,768]{2,1,0:T(8,128)(2,1)S(1)}, bf16[1,128,768]{2,1,0:T(8,128)(2,1)S(1)}, u32[]{:S(2)}, u32[]{:S(2)}) collective-permute-start(bf16[1,128,768]{2,1,0:T(8,128)(2,1)S(1)} %get-tuple-element.129), channel_id=1, source_target_pairs={{0,16},{8,24},{16,0},{24,8},{1,17},{9,25},{17,1},{25,9},{2,18},{10... | collective-permute-start | bytes 589832 | tf_op jit(solution)/shard_map/ppermute | solution.py:518
  51.9 1.3 %collective-permute-start.14 = (f32[8,768]{1,0:T(8,128)S(1)}, f32[8,768]{1,0:T(8,128)S(1)}, u32[]{:S(2)}, u32[]{:S(2)}) collective-permute-start(f32[8,768]{1,0:T(8,128)S(1)} %add_add_fusion), channel_id=1, source_target_pairs={{0,8},{8,0},{16,24},{24,16},{1,9},{9,1},{17,25},{25,17},{2,10},{10... | collective-permute-start | bytes 73736 | tf_op jit(solution)/shard_map/ppermute | solution.py:518
  53.1 4.7 %collective-permute-start.15 = (f32[8,768]{1,0:T(8,128)S(1)}, f32[8,768]{1,0:T(8,128)S(1)}, u32[]{:S(2)}, u32[]{:S(2)}) collective-permute-start(f32[8,768]{1,0:T(8,128)S(1)} %add.15.near_pack), channel_id=1, source_target_pairs={{0,4},{1,5},{2,6},{3,7},{4,0},{5,1},{6,2},{7,3},{8,12},{9,13},{10,... | collective-permute-start | bytes 73736 | tf_op jit(solution)/shard_map/ppermute | solution.py:518
  57.0 0.6 copy-start.1

commit v7 on v6

--- a/solution.py
+++ b/solution.py
@@ -464,33 +464,36 @@
     return hidden_grad + inv * (c - hat * jnp.mean(hat * c, -1, keepdims=True))
 
 
-def return_kernel(far, own_part, from_sib, far_part, from_sib_b, hidden_grad, gain, back):
+def return_kernel(far, own_part, from_sib, out, hidden_grad, gain, back):
     shard = back.shape[1]
-    back[0] = (far_part[0].astype(F32) + from_sib_b[1, :shard].astype(F32)).astype(BF16)
+    back[0] = out[0]
     grad = own_part[1] + from_sib[1].astype(F32)
     back[1] = norm_back(far[0, :shard], grad, hidden_grad[shard : 2 * shard, :], gain).astype(BF16)
 
 
-def own_rows_kernel(own, part_a, sib_a, hidden_grad, gain, out, output, grad_input, mark):
+def far_sum_kernel(far_part, from_sib, total):
+    total[0] = (far_part[0].astype(F32) + from_sib[1].astype(F32)).astype(BF16)
+
+
+def own_rows_kernel(own, part_a, sib_a, hidden_grad, gain, out, back, output, grad_input, mark):
     mark[...] = jnp.zeros(mark.shape, F32)
     rows, shard, width = out.shape
     row = moved_row(rows)
+    other = rows - 1 - row
     output[row] = out[0]
     output[1] = out[2]
+    output[other] = back[0]
+    grad_input[other] = back[1]
     grad = part_a[0] + sib_a[0].astype(F32)
     grad_input[row] = norm_back(own[0, :shard], grad, hidden_grad[0:shard, :], gain).astype(BF16)
 
 
-def last_kernel(own, part_b, sib_b, hidden_grad, gain, out_far, back, _, __, output, grad_input, grad_b, sems):
-    rows, shard, width = output.shape
-    other = rows - 1 - moved_row(rows)
-    started = start_copies([(out_far.at[0], output.at[other]), (back.at[1], grad_input.at[other])], sems)
-    grad = part_b[0] + sib_b[0].astype(F32) + back[0].astype(F32)
+def last_kernel(own, part_b, sib_b, hidden_grad, gain, far_sum, _, grad_input, grad_b, sems):
+    shard = grad_input.shape[1]
+    grad = part_b[0] + sib_b[0].astype(F32) + far_sum[0].astype(F32)
     grad_b[...] = norm_back(own[1, :shard], grad, hidden_grad[2 * shard :, :], gain).astype(BF16)
-    own_copy = pltpu.make_async_copy(grad_b, grad_input.at[1], sems.at[2])
-    own_copy.start()
-    for one in (*started, own_copy):
-        one.wait()
+    (copy,) = start_copies([(grad_b, grad_input.at[1])], sems)
+    copy.wait()
 
 
 def unpack_kernel(ranks, mid, near_pack, far_pack, _, g1, g2, shared, dl, dr, ul, ur, bd, bu):
@@ -642,15 +645,17 @@
     )
     sib_part_b, sib_a = lax.optimization_barrier((sib_part_b, sib_a))
     sib_b = exchange(sib_part_b, "seq", 1)
+    sib_a, pack = lax.optimization_barrier((sib_a, pack))
     (back,) = call(
         return_kernel,
         [((2, shard, width), BF16)],
-        (a_far, part_a, sib_a, far_part, sib_b, hidden_grad, gain1),
+        (a_far, part_a, sib_a, out_send, hidden_grad, gain1),
         16,
         0.5,
     )
     back = exchange(back, "seq", 2)
-    out_far = exchange(out_send, "seq", 2)
+    (far_sum,) = call(far_sum_kernel, [((1, shard, width), BF16)], (far_part, sib_b), 8, 0.2)
+    far_sum = exchange(far_sum, "seq", 2)
     (pack,) = call(add_kernel, [((8, width), F32)], (pack, exchange(pack, "seq", 2)), 4, 10.0)
     first, second, third = (exchange(pack, "batch", k) for k in (1, 2, 3))
     pack = (pack + first) + (second + third)
@@ -662,18 +667,18 @@
     far_pack = exchange(pack, "batch", bit)
     rowed = ((rows, shard, width), BF16)
     output, grad_input, mark = call(
-        own_rows_kernel, [rowed, rowed, ((8, 128), F32)], (own, part_a, sib_a, hidden_grad, gain1, out), 16, 0.0, last=True
-    )
-    output, grad_input = call(
+        own_rows_kernel, [rowed, rowed, ((8, 128), F32)], (own, part_a, sib_a, hidden_grad, gain1, out, back), 16, 0.0, last=True
+    )
+    (grad_input,) = call(
         last_kernel,
-        [rowed, rowed],
-        (own, part_b, sib_b, hidden_grad, gain1, out_far, back, Far(output), Far(grad_input)),
+        [rowed],
+        (own, part_b, sib_b, hidden_grad, gain1, far_sum, Far(grad_input)),
         16,
         1.0,
         [((shard, width), BF16)],
-        copies=3,
+        copies=1,
         last=True,
-        aliases={7: 0, 8: 1},
+        aliases={6: 0},
     )
     grads = call(
         functools.partial(unpack_kernel, ranks, mid),

time: 60 us -> 59.9 us (level)
  starting transfers between devices: 17.7 us -> 16.5 us
  waiting for transfers between devices: 3.97 us -> 5.04 us
    ppermute x16, starting transfers between devices: 17.7 us -> 16.5 us  [exchange(): return lax.ppermute(value, axis, [(k, k ^ bit) for k in range(count)])]
    ppermute x16, waiting for transfers between devices: 3.97 us -> 5.04 us  [exchange(): return lax.ppermute(value, axis, [(k, k ^ bit) for k in range(count)])]
    pallas_call x13 -> x14, Pallas kernels: 36.5 us -> 36.5 us  [call(): pl.pallas_call(kernel, out_shape=[made(shape, kind) for shape, kind in ou...]
where the time goes in v7:
time: 59.9 us; the launch traced here: 59.6 us
  Pallas kernels  36.5 us (61%)
  starting transfers between devices  16.5 us (28%)
  waiting for transfers between devices  5.04 us (8%)
  between operations  0.97 us (2%)
    pallas_call x14, Pallas kernels, call(): pl.pallas_call(kernel, out_shape=[made(shape, kind) for shape, kind in ou...  36.5 us
    ppermute x16, starting transfers between devices, exchange(): return lax.ppermute(value, axis, [(k, k ^ bit) for k in range(count)])  16.5 us
    ppermute x16, waiting for transfers between devices, exchange(): return lax.ppermute(value, axis, [(k, k ^ bit) for k in range(count)])  5.04 us
  transfers between devices with their start and end apart: 16, of which 6 were waited for; matrix products, arithmetic and copies ran while one was open for 0% of the time, Pallas kernels for 31%

profile of v7, /device:TPU:0, one launch (start us, length us, event | category | flops | bytes accessed | tf_op | source)
XLA Modules:
  0.0 59.6 jit_solution(4702197964701327293)
XLA Ops:
  0.6 1.3 %shard_map.275 = (bf16[2,136,768]{2,1,0:T(8,128)(2,1)S(1)}, bf16[1,136,768]{2,1,0:T(8,128)(2,1)S(1)}, bf16[1,136,768]{2,1,0:T(8,128)(2,1)S(1)}, bf16[1,128,768]{2,1,0:T(8,128)(2,1)S(1)}) custom-call(bf16[3,128,768]{2,1,0:T(8,128)(2,1)} %inputs.1, bf16[3,128,768]{2,1,0:T(8,128)(2,1)} %cot.1, s32[3,128]{1,0:T(4,128)} %segment_ids.1), custom_call_target="tpu_custom_call" | custom-call | flops 1100000000 | tf_op jit(solution)/shard_map/pallas_call | solution.py:72
  2.0 3.0 %collective-permute-start.1 = (bf16[1,136,768]{2,1,0:T(8,128)(2,1)S(1)}, bf16[1,136,768]{2,1,0:T(8,128)(2,1)S(1)}, u32[]{:S(2)}, u32[]{:S(2)}) collective-permute-start(bf16[1,136,768]{2,1,0:T(8,128)(2,1)S(1)} %get-tuple-element.81), channel_id=1, source_target_pairs={{0,16},{8,24},{16,0},{24,8},{1,17},{9,25},{17,1},{25,9},{2,18},{10... | collective-permute-start | bytes 626696 | tf_op jit(solution)/shard_map/ppermute | solution.py:521
  5.0 0.1 collective-permute-start.3
  5.1 0.0 collective-permute-start
  5.1 4.6 %shard_map.276 = (f32[7,6,256,128]{3,2,1,0:T(8,128)S(1)}, bf16[48,768]{1,0:T(8,128)(2,1)S(1)}, bf16[48,768]{1,0:T(8,128)(2,1)S(1)}, f32[32,96]{1,0:T(8,128)S(1)}...) custom-call(s32[1023]{0:T(1024)} %table_far.1, ...), custom_call_target="tpu_custom_call" | custom-call | flops 22000001024 | tf_op jit(solution)/shard_map/pallas_call | solution.py:72
  9.7 0.0 collective-permute-done.sib
  9.7 1.9 %shard_map.277 = (bf16[6,512,128]{2,1,0:T(8,128)(2,1)S(1)}, bf16[6,512,128]{2,1,0:T(8,128)(2,1)S(1)}, bf16[6,256,128]{2,1,0:T(8,128)(2,1)S(1)}) custom-call(bf16[2,136,768]{2,1,0:T(8,128)(2,1)S(1)} %get-tuple-element.80.own, bf16[2,136,768]{2,1,0:T(8,128)(2,1)S(1)} %collective-permute-done.sib, bf16[768,768]{1,0:T(8,128)(2,1)S(1)} %get-tuple-element.82.wq.rest_1_.rest_0_, ...), custom_call_target="tpu_custom_call" | custom-call | flops 22000001024 | tf_op jit(solution)/shard_map/pallas_call | solution.py:72
  11.6 0.0 collective-permute-done.1.far
  11.6 0.6 collective-permute-start.2
  12.1 1.9 %collective-permute-start.5 = (bf16[1,128,768]{2,1,0:T(8,128)(2,1)S(1)}, bf16[1,128,768]{2,1,0:T(8,128)(2,1)S(1)}, u32[]{:S(2)}, u32[]{:S(2)}) collective-permute-start(bf16[1,128,768]{2,1,0:T(8,128)(2,1)S(1)} %get-tuple-element.104), channel_id=1, source_target_pairs={{0,16},{8,24},{16,0},{24,8},{1,17},{9,25},{17,1},{25,9},{2,18},{10... | collective-permute-start | bytes 589832 | tf_op jit(solution)/shard_map/ppermute | solution.py:521
  14.1 0.6 collective-permute-done.3.far
  14.7 0.0 collective-permute-done.2.far_sib
  14.7 0.0 collective-permute-start.4
  14.7 3.9 %shard_map.278 = (bf16[6,256,128]{2,1,0:T(8,128)(2,1)S(1)}, bf16[6,256,128]{2,1,0:T(8,128)(2,1)S(1)}, bf16[6,128,128]{2,1,0:T(8,128)(2,1)S(1)}, bf16[12,256,512]...) custom-call(bf16[2,136,768]{2,1,0:T(8,128)(2,1)S(1)} %get-tuple-elem, ...), custom_call_target="tpu_custom_call" | custom-call | flops 3300000000 | tf_op jit(solution)/shard_map/pallas_call | solution.py:72
  18.6 0.0 copy-start
  18.6 0.0 collective-permute-done.4.far_sib
  18.6 2.4 %shard_map.279 = (bf16[6,256,128]{2,1,0:T(8,128)(2,1)S(1)}, bf16[6,256,128]{2,1,0:T(8,128)(2,1)S(1)}, bf16[6,256,512]{2,1,0:T(8,128)(2,1)S(1)}, f32[6,128,128]{2...) custom-call(bf16[2,136,768]{2,1,0:T(8,128)(2,1)S(1)} %get-tuple-element.80.own, ...), custom_call_target="tpu_custom_call" | custom-call | flops 3300000000 | tf_op jit(solution)/shard_map/pallas_call | solution.py:72
  21.1 0.0 collective-permute-done.5.cot_far
  21.1 0.0 copy-done
  21.1 10.5 %shard_map.280 = (bf16[3,128,768]{2,1,0:T(8,128)(2,1)S(1)}, bf16[1,128,768]{2,1,0:T(8,128)(2,1)S(1)}, f32[384,768]{1,0:T(8,128)S(1)}, bf16[384,768]{1,0:T(8,128)(2,1)S(1)}, f32[8,768]{1,0:T(8,128)S(1)}) custom-call(f32[256,768]{1,0:T(8,128)S(1)} %get-tuple-element.101.hid_a, f32[128,768]{1,0:T(8,128)S(1)} %get-tuple-element.103.hid_b, ...), custom_call_target="tpu_custom_call" | custom-call | flops 13200000000 | tf_op jit(solution)/shard_map/pallas_call | solution.py:72
  31.6 5.2 %shard_map.281 = (f32[2,128,768]{2,1,0:T(8,128)S(1)}, bf16[2,128,768]{2,1,0:T(8,128)(2,1)S(1)}, f32[8,768]{1,0:T(8,128)S(1)}, bf16[6,128,128]{2,1,0:T(8,128)(2,1)S(1)}) custom-call(bf16[2,136,768]{2,1,0:T(8,128)(2,1)S(1)} %get-tuple-element.80.own, bf16[2,136,768]{2,1,0:T(8,128)(2,1)S(1)} %collective-permute-done.sib, ...), custom_call_target="tpu_custom_call" | custom-call | flops 6600000000 | tf_op jit(solution)/shard_map/pallas_call | solution.py:72
  36.8 0.6 collective-permute-start.6
  37.4 3.5 %shard_map.282 = (f32[1,128,768]{2,1,0:T(8,128)S(1)}, bf16[1,128,768]{2,1,0:T(8,128)(2,1)S(1)}, bf16[2,128,768]{2,1,0:T(8,128)(2,1)S(1)}, f32[8,768]{1,0:T(8,128)S(1)}) custom-call(bf16[2,136,768]{2,1,0:T(8,128)(2,1)S(1)} %get-tuple-element.80.own, bf16[2,136,768]{2,1,0:T(8,128)(2,1)S(1)} %collective-permute-done.sib, ...), custom_call_target="tpu_custom_call" | custom-call | flops 3960000000 | tf_op jit(solution)/shard_map/pallas_call | solution.py:72
  40.9 0.0 collective-permute-done.6.from_sib.sib_a
  40.9 1.8 %collective-permute-start.10 = (f32[8,768]{1,0:T(8,128)S(1)}, f32[8,768]{1,0:T(8,128)S(1)}, u32[]{:S(2)}, u32[]{:S(2)}) collective-permute-start(f32[8,768]{1,0:T(8,128)S(1)} %get-tuple-element.138.a), channel_id=1, source_target_pairs={{0,16},{8,24},{16,0},{24,8},{1,17},{9,25},{17,1},{25,9},{2,18},{10... | collective-permute-start | bytes 73736 | tf_op jit(solution)/shard_map/ppermute | solution.py:521
  42.7 0.3 shard_map.283
  43.0 0.3 collective-permute-start.7
  43.3 0.0 collective-permute-start.8
  43.3 1.5 %collective-permute-done.10.b = f32[8,768]{1,0:T(8,128)S(1)} collective-permute-done((f32[8,768]{1,0:T(8,128)S(1)}, f32[8,768]{1,0:T(8,128)S(1)}, u32[]{:S(2)}, u32[]{:S(2)}) %collective-permute-start.10) | collective-permute-done | bytes 24608 | tf_op jit(solution)/shard_map/ppermute | solution.py:521
  44.8 2.7 %collective-permute-start.13 = (f32[8,768]{1,0:T(8,128)S(1)}, f32[8,768]{1,0:T(8,128)S(1)}, u32[]{:S(2)}, u32[]{:S(2)}) collective-permute-start(f32[8,768]{1,0:T(8,128)S(1)} %shard_map.287), channel_id=1, source_target_pairs={{0,3},{1,2},{2,1},{3,0},{4,7},{5,6},{6,5},{7,4},{8,11},{9,10},{10,... | collective-permute-start | bytes 73736 | tf_op jit(solution)/shard_map/ppermute | solution.py:521
  47.5 0.4 collective-permute-start.12
  48.0 0.3 collective-permute-start.11
  48.3 0.0 collective-permute-done.8.from_sib.sib_b
  48.3 2.0 %collective-permute-start.9 = (bf16[1,128,768]{2,1,0:T(8,128)(2,1)S(1)}, bf16[1,128,768]{2,1,0:T(8,128)(2,1)S(1)}, u32[]{:S(2)}, u32[]{:S(2)}) collective-permute-start(bf16[1,128,768]{2,1,0:T(8,128)(2,1)S(1)} %shard_map.285), channel_id=1, source_target_pairs={{0,16},{8,24},{16,0},{24,8},{1,17},{9,25},{17,1},{25,9},{2,18},{10... | collective-permute-start | bytes 589832 | tf_op jit(solution)/shard_map/ppermute | solution.py:521
  50.4 0.0 collective-permute-done.13
  50.4 1.0 %collective-permute-done.12 = f32[8,768]{1,0:T(8,128)S(1)} collective-permute-done((f32[8,768]{1,0:T(8,128)S(1)}, f32[8,768]{1,0:T(8,128)S(1)}, u32[]{:S(2)}, u32[]{:S(2)}) %collective-permute-start.12) | collective-permute-done | bytes 24608 | tf_op jit(solution)/shard_map/ppermute | solution.py:521
  51.3 0.4 collective-permute-done.11
  51.8 0.1 collective-permute-start.14
  51.9 1.2 %collective-permute-done.14 = f32[8,768]{1,0:T(8,128)S(1)} collective-permute-done((f32[8,768]{1,0:T(8,128)S(1)}, f32[8,768]{1,0:T(8,128)S(1)}, u32[]{:S(2)}, u32[]{:S(2)}) %collective-permute-start.14) | collective-permute-done | bytes 24608 | tf_op jit(solution)/shard_map/ppermute | solution.py:521
  53.1 2.6 %collective-permute-start.15 = (f32[8,768]{1,0:T(8,128)S(1)}, f32[8,768]{1,0:T(8,128)S(1)}, u32[]{:S(2)}, u32[]{:S(2)}) collective-permute-start(f32[8,768]{1,0:T(8,128)S(1)} %add.15.near_pack), channel_id=1, source_target_pairs={{0,4},{1,5},{2,6},{3,7},{4,0},{5,1},{6,2},{7,3},{8,12},{9,13},{10,... | collective-permute-start | bytes 73736 | tf_op jit(solution)/shard_map/ppermute | solution.py:521
  55.6 0.0 collective-permute-done.7.back
  55.6 1.2 %shard_map.284 = (bf16[3,128,768]{2,1,0:T(8,128)(2,1)}, bf16[3,128,768]{2,1,0:T(8,128)(2,1)}, f32[8,128]{1,0:T(8,128)S(1)}) custom-call(bf16[2,136,768]{2,1,0:T(8,128)(2,1)S(1)} %get-tuple-element.80.own, f32[2,128,768]{2,1,0:T(8,128)S(1)} %get-tuple-element.117.own_part.part_a, bf16[2,128,768]{2,1,0:T(8,128)(2,1)S(1)} %collective-permute-done.6.from_sib.sib_a, ...), custom_call_target="tpu_custom_call" | custom-call | tf_op jit(solution)/shard_map/pallas_call | solution.py:72
  56.9 0.0 copy-start.1
  56.9 0.6 copy-done.1
  57.5 0.3 collective-permute-done.15.far_pack
  57.8 0.7 %shard_map.288 = (f32[768]{0:T(1024)}, f32[768]{0:T(1024)}, f32[4,4,4]{2,1,0:T(4,128)}, f32[4,192]{1,0:T(4,128)}, f32[4,12]{1,0:T(4,128)}, /*index=5*/f32[4,12]{...) custom-call(f32[8,768]{1,0:T(8,128)S(1)} %add.15.near_pack, f32[8,768]{1,0:T(8,128)S(1)} %collective-permute-done.15.far_pack, ...), custom_call_target="tpu_custom_call" | custom-call | flops 550000000 | tf_op jit(solution)/shard_map/pallas_call | solution.py:72
  58.5 0.0 collective-permute-done.9.far_sum
  58.5 1.0 %shard_map.286 = bf16[3,128,768]{2,1,0:T(8,128)(2,1)} custom-call(bf16[2,136,768]{2,1,0:T(8,128)(2,1)S(1)} %get-tuple-element.80.own, f32[1,128,768]{2,1,0:T(8,128)S(1)} %get-tuple-element.134.part_b, bf16[2,128,768]{2,1,0:T(8,128)(2,1)S(1)} %collective-permute-done.8.from_sib.sib_b, ...), custom_call_target="tpu_custom_call", output_to_operand_aliasing={{}: (6, {})} | custom-call | flops 1100000000 | tf_op jit(solution)/shard_map/pallas_call | solution.py:72
  (4 shorter events, 0.1 us)
Async XLA Ops:
  2.0 9.6 %collective-permute-start.1 = (bf16[1,136,768]{2,1,0:T(8,128)(2,1)S(1)}, bf16[1,136,768]{2,1,0:T(8,128)(2,1)S(1)}, u32[]{:S(2)}, u32[]{:S(2)}) collective-permute-start(bf16[1,136,768]{2,1,0:T(8,128)(2,1)S(1)} %get-tuple-element.81), channel_id=1, source_target_pairs={{0,16},{8,24},{16,0},{24,8},{1,17},{9,25},{17,1},{25,9},{2,18},{10... | collective-permute-start | bytes 626696 | tf_op jit(solution)/shard_map/ppermute | solution.py:521
  5.0 9.6 %collective-permute-start.3 = (bf16[1,136,768]{2,1,0:T(8,128)(2,1)S(1)}, bf16[1,136,768]{2,1,0:T(8,128)(2,1)S(1)}, u32[]{:S(2)}, u32[]{:S(2)}) collective-permute-start(bf16[1,136,768]{2,1,0:T(8,128)(2,1)S(1)} %get-tuple-element.88), channel_id=1, source_target_pairs={{0,16},{8,24},{16,0},{24,8},{1,17},{9,25},{17,1},{25,9},{2,18},{10... | collective-permute-start | bytes 626696 | tf_op jit(solution)/shard_map/ppermute | solution.py:521
  5.1 4.6 %collective-permute-start = (bf16[2,136,768]{2,1,0:T(8,128)(2,1)S(1)}, bf16[2,136,768]{2,1,0:T(8,128)(2,1)S(1)}, u32[]{:S(2)}, u32[]{:S(2)}) collective-permute-start(bf16[2,136,768]{2,1,0:T(8,128)(2,1)S(1)} %get-tuple-element.80.own), channel_id=1, source_target_pairs={{0,8},{8,0},{16,24},{24,16},{1,9},{9,1},{17,25},{25,17},{2,10},{10... | collective-permute-start | bytes 1253384 | tf_op jit(solution)/shard_map/ppermute | solution.py:521
  11.6 3.1 %collective-permute-start.2 = (bf16[1,136,768]{2,1,0:T(8,128)(2,1)S(1)}, bf16[1,136,768]{2,1,0:T(8,128)(2,1)S(1)}, u32[]{:S(2)}, u32[]{:S(2)}) collective-permute-start(bf16[1,136,768]{2,1,0:T(8,128)(2,1)S(1)} %collective-permute-done.1.far), channel_id=1, source_target_pairs={{0,8},{8,0},{16,24},{24,16},{1,9},{9,1},{17,25},{25,17},{2,10},{10... | collective-permute-start | bytes 626696 | tf_op jit(solution)/shard_map/ppermute | solution.py:521
  12.1 8.9 %collective-permute-start.5 = (bf16[1,128,768]{2,1,0:T(8,128)(2,1)S(1)}, bf16[1,128,768]{2,1,0:T(8,128)(2,1)S(1)}, u32[]{:S(2)}, u32[]{:S(2)}) collective-permute-start(bf16[1,128,768]{2,1,0:T(8,128)(2,1)S(1)} %get-tuple-element.104), channel_id=1, source_target_pairs={{0,16},{8,24},{16,0},{24,8},{1,17},{9,25},{17,1},{25,9},{2,18},{10... | collective-permute-start | bytes 589832 | tf_op jit(solution)/shard_map/ppermute | solution.py:521
  14.7 3.9 %collective-permute-start.4 = (bf16[1,136,768]{2,1,0:T(8,128)(2,1)S(1)}, bf16[1,136,768]{2,1,0:T(8,128)(2,1)S(1)}, u32[]{:S(2)}, u32[]{:S(2)}) collective-permute-start(bf16[1,136,768]{2,1,0:T(8,128)(2,1)S(1)} %collective-permute-done.3.far), channel_id=1, source_target_pairs={{0,8},{8,0},{16,24},{24,16},{1,9},{9,1},{17,25},{25,17},{2,10},{10... | collective-permute-start | bytes 626696 | tf_op jit(solution)/shard_map/ppermute | solution.py:521
  18.6 2.5 %copy-start = (bf16[3,128,768]{2,1,0:T(8,128)(2,1)S(1)}, bf16[3,128,768]{2,1,0:T(8,128)(2,1)}, u32[]{:S(2)}) copy-start(bf16[3,128,768]{2,1,0:T(8,128)(2,1)} %cot.1) | copy-start | bytes 1769476
  36.8 4.1 %collective-permute-start.6 = (bf16[2,128,768]{2,1,0:T(8,128)(2,1)S(1)}, bf16[2,128,768]{2,1,0:T(8,128)(2,1)S(1)}, u32[]{:S(2)}, u32[]{:S(2)}) collective-permute-start(bf16[2,128,768]{2,1,0:T(8,128)(2,1)S(1)} %get-tuple-element.126), channel_id=1, source_target_pairs={{0,8},{8,0},{16,24},{24,16},{1,9},{9,1},{17,25},{25,17},{2,10},{10... | collective-permute-start | bytes 1179656 | tf_op jit(solution)/shard_map/ppermute | solution.py:521
  40.9 3.9 %collective-permute-start.10 = (f32[8,768]{1,0:T(8,128)S(1)}, f32[8,768]{1,0:T(8,128)S(1)}, u32[]{:S(2)}, u32[]{:S(2)}) collective-permute-start(f32[8,768]{1,0:T(8,128)S(1)} %get-tuple-element.138.a), channel_id=1, source_target_pairs={{0,16},{8,24},{16,0},{24,8},{1,17},{9,25},{17,1},{25,9},{2,18},{10... | collective-permute-start | bytes 73736 | tf_op jit(solution)/shard_map/ppermute | solution.py:521
  43.0 12.7 %collective-permute-start.7 = (bf16[2,128,768]{2,1,0:T(8,128)(2,1)S(1)}, bf16[2,128,768]{2,1,0:T(8,128)(2,1)S(1)}, u32[]{:S(2)}, u32[]{:S(2)}) collective-permute-start(bf16[2,128,768]{2,1,0:T(8,128)(2,1)S(1)} %shard_map.283), channel_id=1, source_target_pairs={{0,16},{8,24},{16,0},{24,8},{1,17},{9,25},{17,1},{25,9},{2,18},{10... | collective-permute-start | bytes 1179656 | tf_op jit(solution)/shard_map/ppermute | solution.py:521
  43.3 5.0 %collective-permute-start.8 = (bf16[2,128,768]{2,1,0:T(8,128)(2,1)S(1)}, bf16[2,128,768]{2,1,0:T(8,128)(2,1)S(1)}, u32[]{:S(2)}, u32[]{:S(2)}) collective-permute-start(bf16[2,128,768]{2,1,0:T(8,128)(2,1)S(1)} %get-tuple-element.135), channel_id=1, source_target_pairs={{0,8},{8,0},{16,24},{24,16},{1,9},{9,1},{17,25},{25,17},{2,10},{10... | collective-permute-start | bytes 1179656 | tf_op jit(solution)/shard_map/ppermute | solution.py:521
  44.8 5.6 %collective-permute-start.13 = (f32[8,768]{1,0:T(8,128)S(1)}, f32[8,768]{1,0:T(8,128)S(1)}, u32[]{:S(2)}, u32[]{:S(2)}) collective-permute-start(f32[8,768]{1,0:T(8,128)S(1)} %shard_map.287), channel_id=1, source_target_pairs={{0,3},{1,2},{2,1},{3,0},{4,7},{5,6},{6,5},{7,4},{8,11},{9,10},{10,... | collective-permute-start | bytes 73736 | tf_op jit(solution)/shard_map/ppermute | solution.py:521
  47.5 3.8 %collective-permute-start.12 = (f32[8,768]{1,0:T(8,128)S(1)}, f32[8,768]{1,0:T(8,128)S(1)}, u32[]{:S(2)}, u32[]{:S(2)}) collective-permute-start(f32[8,768]{1,0:T(8,128)S(1)} %shard_map.287), channel_id=1, source_target_pairs={{0,2},{1,3},{2,0},{3,1},{4,6},{5,7},{6,4},{7,5},{8,10},{9,11},{10,... | collective-permute-start | bytes 73736 | tf_op jit(solution)/shard_map/ppermute | solution.py:521
  48.0 3.8 %collective-permute-start.11 = (f32[8,768]{1,0:T(8,128)S(1)}, f32[8,768]{1,0:T(8,128)S(1)}, u32[]{:S(2)}, u32[]{:S(2)}) collective-permute-start(f32[8,768]{1,0:T(8,128)S(1)} %shard_map.287), channel_id=1, source_target_pairs={{0,1},{1,0},{2,3},{3,2},{4,5},{5,4},{6,7},{7,6},{8,9},{9,8},{10,11... | collective-permute-start | bytes 73736 | tf_op jit(solution)/shard_map/ppermute | solution.py:521
  48.3 10.2 %collective-permute-start.9 = (bf16[1,128,768]{2,1,0:T(8,128)(2,1)S(1)}, bf16[1,128,768]{2,1,0:T(8,128)(2,1)S(1)}, u32[]{:S(2)}, u32[]{:S(2)}) collective-permute-start(bf16[1,128,768]{2,1,0:T(8,128)(2,1)S(1)} %shard_map.285), channel_id=1, source_target_pairs={{0,16},{8,24},{16,0},{24,8},{1,17},{9,25},{17,1},{25,9},{2,18},{10... | collective-permute-start | bytes 589832 | tf_op jit(solution)/shard_map/ppermute | solution.py:521
  51.8 1.3 %collective-permute-start.14 = (f32[8,768]{1,0:T(8,128)S(1)}, f32[8,768]{1,0:T(8,128)S(1)}, u32[]{:S(2)}, u32[]{:S(2)}) collective-permute-start(f32[8,768]{1,0:T(8,128)S(1)} %add_add_fusion), channel_id=1, source_target_pairs={{0,8},{8,0},{16,24},{24,16},{1,9},{9,1},{17,25},{25,17},{2,10},{10... | collective-permute-start | bytes 73736 | tf_op jit(solution)/shard_map/ppermute | solution.py:521
  53.1 4.7 %collective-permute-start.15 = (f32[8,768]{1,0:T(8,128)S(1)}, f32[8,768]{1,0:T(8,128)S(1)}, u32[]{:S(2)}, u32[]{:S(2)}) collective-permute-start(f32[8,768]{1,0:T(8,128)S(1)} %add.15.near_pack), channel_id=1, source_target_pairs={{0,4},{1,5},{2,6},{3,7},{4,0},{5,1},{6,2},{7,3},{8,12},{9,13},{10,... | collective-permute-start | bytes 73736 | tf_op jit(solution)/shard_map/ppermute | solution.py:521
  56.9 0.6 copy-start.1

commit v8 on v6

--- a/solution.py
+++ b/solution.py
@@ -681,7 +681,7 @@
             ((width,), F32), ((width,), F32), ((ranks, ranks, ranks), F32), ((ranks, outer), F32),
             ((ranks, inner), F32), ((ranks, inner), F32), ((ranks, outer), F32), ((mid,), F32), ((width,), F32),
         ],
-        (pack, far_pack, Far(mark)),
+        (pack, far_pack, mark),
         8,
         0.5,
         last=True,

time: 60 us -> 60 us (level)
  no operation moved by 1% of the time
where the time goes in v8:
time: 60 us; the launch traced here: 59.8 us
  Pallas kernels  36.5 us (61%)
  starting transfers between devices  17.7 us (30%)
  waiting for transfers between devices  4.56 us (8%)
  between operations  0.98 us (2%)
    pallas_call x13, Pallas kernels, call(): pl.pallas_call(kernel, out_shape=[made(shape, kind) for shape, kind in ou...  36.5 us
    ppermute x16, starting transfers between devices, exchange(): return lax.ppermute(value, axis, [(k, k ^ bit) for k in range(count)])  17.7 us
    ppermute x16, waiting for transfers between devices, exchange(): return lax.ppermute(value, axis, [(k, k ^ bit) for k in range(count)])  4.56 us
  transfers between devices with their start and end apart: 16, of which 6 were waited for; matrix products, arithmetic and copies ran while one was open for 0% of the time, Pallas kernels for 31%

profile of v8, /device:TPU:0, one launch (start us, length us, event | category | flops | bytes accessed | tf_op | source)
XLA Modules:
  0.0 59.8 jit_solution(13252553563724670741)
XLA Ops:
  0.6 1.3 %shard_map.275 = (bf16[2,136,768]{2,1,0:T(8,128)(2,1)S(1)}, bf16[1,136,768]{2,1,0:T(8,128)(2,1)S(1)}, bf16[1,136,768]{2,1,0:T(8,128)(2,1)S(1)}, bf16[1,128,768]{2,1,0:T(8,128)(2,1)S(1)}) custom-call(bf16[3,128,768]{2,1,0:T(8,128)(2,1)} %inputs.1, bf16[3,128,768]{2,1,0:T(8,128)(2,1)} %cot.1, s32[3,128]{1,0:T(4,128)} %segment_ids.1), custom_call_target="tpu_custom_call" | custom-call | flops 1100000000 | tf_op jit(solution)/shard_map/pallas_call | solution.py:72
  2.0 3.0 %collective-permute-start.1 = (bf16[1,136,768]{2,1,0:T(8,128)(2,1)S(1)}, bf16[1,136,768]{2,1,0:T(8,128)(2,1)S(1)}, u32[]{:S(2)}, u32[]{:S(2)}) collective-permute-start(bf16[1,136,768]{2,1,0:T(8,128)(2,1)S(1)} %get-tuple-element.81), channel_id=1, source_target_pairs={{0,16},{8,24},{16,0},{24,8},{1,17},{9,25},{17,1},{25,9},{2,18},{10... | collective-permute-start | bytes 626696 | tf_op jit(solution)/shard_map/ppermute | solution.py:518
  5.0 0.1 collective-permute-start.3
  5.1 0.0 collective-permute-start
  5.1 4.6 %shard_map.276 = (f32[7,6,256,128]{3,2,1,0:T(8,128)S(1)}, bf16[48,768]{1,0:T(8,128)(2,1)S(1)}, bf16[48,768]{1,0:T(8,128)(2,1)S(1)}, f32[32,96]{1,0:T(8,128)S(1)}...) custom-call(s32[1023]{0:T(1024)} %table_far.1, ...), custom_call_target="tpu_custom_call" | custom-call | flops 22000001024 | tf_op jit(solution)/shard_map/pallas_call | solution.py:72
  9.7 0.0 collective-permute-done.sib
  9.7 1.8 %shard_map.277 = (bf16[6,512,128]{2,1,0:T(8,128)(2,1)S(1)}, bf16[6,512,128]{2,1,0:T(8,128)(2,1)S(1)}, bf16[6,256,128]{2,1,0:T(8,128)(2,1)S(1)}) custom-call(bf16[2,136,768]{2,1,0:T(8,128)(2,1)S(1)} %get-tuple-element.80.own, bf16[2,136,768]{2,1,0:T(8,128)(2,1)S(1)} %collective-permute-done.sib, bf16[768,768]{1,0:T(8,128)(2,1)S(1)} %get-tuple-element.82.wq.rest_1_.rest_0_, ...), custom_call_target="tpu_custom_call" | custom-call | flops 22000001024 | tf_op jit(solution)/shard_map/pallas_call | solution.py:72
  11.5 0.0 collective-permute-done.1.far
  11.6 0.6 collective-permute-start.2
  12.1 1.9 %collective-permute-start.5 = (bf16[1,128,768]{2,1,0:T(8,128)(2,1)S(1)}, bf16[1,128,768]{2,1,0:T(8,128)(2,1)S(1)}, u32[]{:S(2)}, u32[]{:S(2)}) collective-permute-start(bf16[1,128,768]{2,1,0:T(8,128)(2,1)S(1)} %get-tuple-element.109), channel_id=1, source_target_pairs={{0,16},{8,24},{16,0},{24,8},{1,17},{9,25},{17,1},{25,9},{2,18},{10... | collective-permute-start | bytes 589832 | tf_op jit(solution)/shard_map/ppermute | solution.py:518
  14.1 0.6 collective-permute-done.3.far
  14.7 0.0 collective-permute-done.2.far_sib
  14.7 0.0 collective-permute-start.4
  14.7 3.9 %shard_map.279 = (bf16[6,256,128]{2,1,0:T(8,128)(2,1)S(1)}, bf16[6,256,128]{2,1,0:T(8,128)(2,1)S(1)}, bf16[6,128,128]{2,1,0:T(8,128)(2,1)S(1)}, bf16[12,256,512]...) custom-call(bf16[2,136,768]{2,1,0:T(8,128)(2,1)S(1)} %get-tuple-elem, ...), custom_call_target="tpu_custom_call" | custom-call | flops 3300000000 | tf_op jit(solution)/shard_map/pallas_call | solution.py:72
  18.6 0.0 copy-start
  18.6 0.0 collective-permute-done.4.far_sib
  18.6 2.4 %shard_map.278 = (bf16[6,256,128]{2,1,0:T(8,128)(2,1)S(1)}, bf16[6,256,128]{2,1,0:T(8,128)(2,1)S(1)}, bf16[6,256,512]{2,1,0:T(8,128)(2,1)S(1)}, f32[6,128,128]{2...) custom-call(bf16[2,136,768]{2,1,0:T(8,128)(2,1)S(1)} %get-tuple-element.80.own, ...), custom_call_target="tpu_custom_call" | custom-call | flops 3300000000 | tf_op jit(solution)/shard_map/pallas_call | solution.py:72
  21.1 0.0 collective-permute-done.5.cot_far
  21.1 0.0 copy-done
  21.1 10.5 %shard_map.280 = (bf16[3,128,768]{2,1,0:T(8,128)(2,1)S(1)}, bf16[1,128,768]{2,1,0:T(8,128)(2,1)S(1)}, f32[384,768]{1,0:T(8,128)S(1)}, bf16[384,768]{1,0:T(8,128)(2,1)S(1)}, f32[8,768]{1,0:T(8,128)S(1)}) custom-call(f32[256,768]{1,0:T(8,128)S(1)} %get-tuple-element.107.hid_a, f32[128,768]{1,0:T(8,128)S(1)} %get-tuple-element.108.hid_b, ...), custom_call_target="tpu_custom_call" | custom-call | flops 13200000000 | tf_op jit(solution)/shard_map/pallas_call | solution.py:72
  31.6 5.2 %shard_map.281 = (f32[2,128,768]{2,1,0:T(8,128)S(1)}, bf16[2,128,768]{2,1,0:T(8,128)(2,1)S(1)}, f32[8,768]{1,0:T(8,128)S(1)}, bf16[6,128,128]{2,1,0:T(8,128)(2,1)S(1)}) custom-call(bf16[2,136,768]{2,1,0:T(8,128)(2,1)S(1)} %get-tuple-element.80.own, bf16[2,136,768]{2,1,0:T(8,128)(2,1)S(1)} %collective-permute-done.sib, ...), custom_call_target="tpu_custom_call" | custom-call | flops 6600000000 | tf_op jit(solution)/shard_map/pallas_call | solution.py:72
  36.8 0.6 collective-permute-start.6
  37.4 3.5 %shard_map.282 = (f32[1,128,768]{2,1,0:T(8,128)S(1)}, bf16[1,128,768]{2,1,0:T(8,128)(2,1)S(1)}, bf16[2,128,768]{2,1,0:T(8,128)(2,1)S(1)}, f32[8,768]{1,0:T(8,128)S(1)}) custom-call(bf16[2,136,768]{2,1,0:T(8,128)(2,1)S(1)} %get-tuple-element.80.own, bf16[2,136,768]{2,1,0:T(8,128)(2,1)S(1)} %collective-permute-done.sib, ...), custom_call_target="tpu_custom_call" | custom-call | flops 3960000000 | tf_op jit(solution)/shard_map/pallas_call | solution.py:72
  40.9 0.0 collective-permute-done.6.from_sib.sib_a
  40.9 0.1 collective-permute-start.7
  41.0 1.8 %collective-permute-start.10 = (f32[8,768]{1,0:T(8,128)S(1)}, f32[8,768]{1,0:T(8,128)S(1)}, u32[]{:S(2)}, u32[]{:S(2)}) collective-permute-start(f32[8,768]{1,0:T(8,128)S(1)} %get-tuple-element.138.a), channel_id=1, source_target_pairs={{0,16},{8,24},{16,0},{24,8},{1,17},{9,25},{17,1},{25,9},{2,18},{10... | collective-permute-start | bytes 73736 | tf_op jit(solution)/shard_map/ppermute | solution.py:518
  42.8 0.0 collective-permute-done.7.from_sib_b.sib_b
  42.8 0.3 shard_map.283
  43.1 1.7 %collective-permute-start.9 = (bf16[2,128,768]{2,1,0:T(8,128)(2,1)S(1)}, bf16[2,128,768]{2,1,0:T(8,128)(2,1)S(1)}, u32[]{:S(2)}, u32[]{:S(2)}) collective-permute-start(bf16[2,128,768]{2,1,0:T(8,128)(2,1)S(1)} %shard_map.283), channel_id=1, source_target_pairs={{0,16},{8,24},{16,0},{24,8},{1,17},{9,25},{17,1},{25,9},{2,18},{10... | collective-permute-start | bytes 1179656 | tf_op jit(solution)/shard_map/ppermute | solution.py:518
  44.8 0.1 collective-permute-done.10.b
  44.9 2.7 %collective-permute-start.13 = (f32[8,768]{1,0:T(8,128)S(1)}, f32[8,768]{1,0:T(8,128)S(1)}, u32[]{:S(2)}, u32[]{:S(2)}) collective-permute-start(f32[8,768]{1,0:T(8,128)S(1)} %shard_map.286), channel_id=1, source_target_pairs={{0,3},{1,2},{2,1},{3,0},{4,7},{5,6},{6,5},{7,4},{8,11},{9,10},{10,... | collective-permute-start | bytes 73736 | tf_op jit(solution)/shard_map/ppermute | solution.py:518
  47.6 0.4 collective-permute-start.12
  48.0 0.3 collective-permute-start.11
  48.4 1.7 %collective-permute-start.8 = (bf16[1,128,768]{2,1,0:T(8,128)(2,1)S(1)}, bf16[1,128,768]{2,1,0:T(8,128)(2,1)S(1)}, u32[]{:S(2)}, u32[]{:S(2)}) collective-permute-start(bf16[1,128,768]{2,1,0:T(8,128)(2,1)S(1)} %get-tuple-element.129), channel_id=1, source_target_pairs={{0,16},{8,24},{16,0},{24,8},{1,17},{9,25},{17,1},{25,9},{2,18},{10... | collective-permute-start | bytes 589832 | tf_op jit(solution)/shard_map/ppermute | solution.py:518
  50.1 0.0 collective-permute-done.13
  50.1 1.3 %collective-permute-done.12 = f32[8,768]{1,0:T(8,128)S(1)} collective-permute-done((f32[8,768]{1,0:T(8,128)S(1)}, f32[8,768]{1,0:T(8,128)S(1)}, u32[]{:S(2)}, u32[]{:S(2)}) %collective-permute-start.12) | collective-permute-done | bytes 24608 | tf_op jit(solution)/shard_map/ppermute | solution.py:518
  51.4 0.4 collective-permute-done.11
  51.9 0.1 collective-permute-start.14
  52.0 1.2 %collective-permute-done.14 = f32[8,768]{1,0:T(8,128)S(1)} collective-permute-done((f32[8,768]{1,0:T(8,128)S(1)}, f32[8,768]{1,0:T(8,128)S(1)}, u32[]{:S(2)}, u32[]{:S(2)}) %collective-permute-start.14) | collective-permute-done | bytes 24608 | tf_op jit(solution)/shard_map/ppermute | solution.py:518
  53.1 2.6 %collective-permute-start.15 = (f32[8,768]{1,0:T(8,128)S(1)}, f32[8,768]{1,0:T(8,128)S(1)}, u32[]{:S(2)}, u32[]{:S(2)}) collective-permute-start(f32[8,768]{1,0:T(8,128)S(1)} %add.15.near_pack), channel_id=1, source_target_pairs={{0,4},{1,5},{2,6},{3,7},{4,0},{5,1},{6,2},{7,3},{8,12},{9,13},{10,... | collective-permute-start | bytes 73736 | tf_op jit(solution)/shard_map/ppermute | solution.py:518
  55.8 1.2 %shard_map.284 = (bf16[3,128,768]{2,1,0:T(8,128)(2,1)}, bf16[3,128,768]{2,1,0:T(8,128)(2,1)}, f32[8,128]{1,0:T(8,128)S(1)}) custom-call(bf16[2,136,768]{2,1,0:T(8,128)(2,1)S(1)} %get-tuple-element.80.own, f32[2,128,768]{2,1,0:T(8,128)S(1)} %get-tuple-element.130.own_part.part_a, bf16[2,128,768]{2,1,0:T(8,128)(2,1)S(1)} %collective-permute-done.6.from_sib.sib_a, ...), custom_call_target="tpu_custom_call" | custom-call | tf_op jit(solution)/shard_map/pallas_call | solution.py:72
  57.0 0.9 %collective-permute-done.15.far_pack = f32[8,768]{1,0:T(8,128)S(1)} collective-permute-done((f32[8,768]{1,0:T(8,128)S(1)}, f32[8,768]{1,0:T(8,128)S(1)}, u32[]{:S(2)}, u32[]{:S(2)}) %collective-permute-start.15) | collective-permute-done | bytes 24608 | tf_op jit(solution)/shard_map/ppermute | solution.py:518
  57.9 0.7 %shard_map.287 = (f32[768]{0:T(1024)}, f32[768]{0:T(1024)}, f32[4,4,4]{2,1,0:T(4,128)}, f32[4,192]{1,0:T(4,128)}, f32[4,12]{1,0:T(4,128)}, /*index=5*/f32[4,12]{...) custom-call(f32[8,768]{1,0:T(8,128)S(1)} %add.15.near_pack, f32[8,768]{1,0:T(8,128)S(1)} %collective-permute-done.15.far_pack, ...), custom_call_target="tpu_custom_call" | custom-call | flops 550000000 | tf_op jit(solution)/shard_map/pallas_call | solution.py:72
  58.6 0.0 collective-permute-done.8.out_far
  58.6 0.0 collective-permute-done.9.back
  58.6 1.0 %shard_map.285 = (bf16[3,128,768]{2,1,0:T(8,128)(2,1)}, bf16[3,128,768]{2,1,0:T(8,128)(2,1)}) custom-call(bf16[2,136,768]{2,1,0:T(8,128)(2,1)S(1)} %get-tuple-element.80.own, f32[1,128,768]{2,1,0:T(8,128)S(1)} %get-tuple-element.124.part_b, ...), custom_call_target="tpu_custom_call", output_to_operand_aliasing={{0}: (7, {}), {1}: (8, {})} | custom-call | flops 1100000000 | tf_op jit(solution)/shard_map/pallas_call | solution.py:72
  (3 shorter events, 0.0 us)
Async XLA Ops:
  2.0 9.5 %collective-permute-start.1 = (bf16[1,136,768]{2,1,0:T(8,128)(2,1)S(1)}, bf16[1,136,768]{2,1,0:T(8,128)(2,1)S(1)}, u32[]{:S(2)}, u32[]{:S(2)}) collective-permute-start(bf16[1,136,768]{2,1,0:T(8,128)(2,1)S(1)} %get-tuple-element.81), channel_id=1, source_target_pairs={{0,16},{8,24},{16,0},{24,8},{1,17},{9,25},{17,1},{25,9},{2,18},{10... | collective-permute-start | bytes 626696 | tf_op jit(solution)/shard_map/ppermute | solution.py:518
  5.0 9.6 %collective-permute-start.3 = (bf16[1,136,768]{2,1,0:T(8,128)(2,1)S(1)}, bf16[1,136,768]{2,1,0:T(8,128)(2,1)S(1)}, u32[]{:S(2)}, u32[]{:S(2)}) collective-permute-start(bf16[1,136,768]{2,1,0:T(8,128)(2,1)S(1)} %get-tuple-element.88), channel_id=1, source_target_pairs={{0,16},{8,24},{16,0},{24,8},{1,17},{9,25},{17,1},{25,9},{2,18},{10... | collective-permute-start | bytes 626696 | tf_op jit(solution)/shard_map/ppermute | solution.py:518
  5.1 4.6 %collective-permute-start = (bf16[2,136,768]{2,1,0:T(8,128)(2,1)S(1)}, bf16[2,136,768]{2,1,0:T(8,128)(2,1)S(1)}, u32[]{:S(2)}, u32[]{:S(2)}) collective-permute-start(bf16[2,136,768]{2,1,0:T(8,128)(2,1)S(1)} %get-tuple-element.80.own), channel_id=1, source_target_pairs={{0,8},{8,0},{16,24},{24,16},{1,9},{9,1},{17,25},{25,17},{2,10},{10... | collective-permute-start | bytes 1253384 | tf_op jit(solution)/shard_map/ppermute | solution.py:518
  11.6 3.1 %collective-permute-start.2 = (bf16[1,136,768]{2,1,0:T(8,128)(2,1)S(1)}, bf16[1,136,768]{2,1,0:T(8,128)(2,1)S(1)}, u32[]{:S(2)}, u32[]{:S(2)}) collective-permute-start(bf16[1,136,768]{2,1,0:T(8,128)(2,1)S(1)} %collective-permute-done.1.far), channel_id=1, source_target_pairs={{0,8},{8,0},{16,24},{24,16},{1,9},{9,1},{17,25},{25,17},{2,10},{10... | collective-permute-start | bytes 626696 | tf_op jit(solution)/shard_map/ppermute | solution.py:518
  12.1 8.9 %collective-permute-start.5 = (bf16[1,128,768]{2,1,0:T(8,128)(2,1)S(1)}, bf16[1,128,768]{2,1,0:T(8,128)(2,1)S(1)}, u32[]{:S(2)}, u32[]{:S(2)}) collective-permute-start(bf16[1,128,768]{2,1,0:T(8,128)(2,1)S(1)} %get-tuple-element.109), channel_id=1, source_target_pairs={{0,16},{8,24},{16,0},{24,8},{1,17},{9,25},{17,1},{25,9},{2,18},{10... | collective-permute-start | bytes 589832 | tf_op jit(solution)/shard_map/ppermute | solution.py:518
  14.7 4.0 %collective-permute-start.4 = (bf16[1,136,768]{2,1,0:T(8,128)(2,1)S(1)}, bf16[1,136,768]{2,1,0:T(8,128)(2,1)S(1)}, u32[]{:S(2)}, u32[]{:S(2)}) collective-permute-start(bf16[1,136,768]{2,1,0:T(8,128)(2,1)S(1)} %collective-permute-done.3.far), channel_id=1, source_target_pairs={{0,8},{8,0},{16,24},{24,16},{1,9},{9,1},{17,25},{25,17},{2,10},{10... | collective-permute-start | bytes 626696 | tf_op jit(solution)/shard_map/ppermute | solution.py:518
  18.6 2.5 %copy-start = (bf16[3,128,768]{2,1,0:T(8,128)(2,1)S(1)}, bf16[3,128,768]{2,1,0:T(8,128)(2,1)}, u32[]{:S(2)}) copy-start(bf16[3,128,768]{2,1,0:T(8,128)(2,1)} %cot.1) | copy-start | bytes 1769476
  36.8 4.1 %collective-permute-start.6 = (bf16[2,128,768]{2,1,0:T(8,128)(2,1)S(1)}, bf16[2,128,768]{2,1,0:T(8,128)(2,1)S(1)}, u32[]{:S(2)}, u32[]{:S(2)}) collective-permute-start(bf16[2,128,768]{2,1,0:T(8,128)(2,1)S(1)} %get-tuple-element.126), channel_id=1, source_target_pairs={{0,8},{8,0},{16,24},{24,16},{1,9},{9,1},{17,25},{25,17},{2,10},{10... | collective-permute-start | bytes 1179656 | tf_op jit(solution)/shard_map/ppermute | solution.py:518
  40.9 1.9 %collective-permute-start.7 = (bf16[2,128,768]{2,1,0:T(8,128)(2,1)S(1)}, bf16[2,128,768]{2,1,0:T(8,128)(2,1)S(1)}, u32[]{:S(2)}, u32[]{:S(2)}) collective-permute-start(bf16[2,128,768]{2,1,0:T(8,128)(2,1)S(1)} %get-tuple-element.127), channel_id=1, source_target_pairs={{0,8},{8,0},{16,24},{24,16},{1,9},{9,1},{17,25},{25,17},{2,10},{10... | collective-permute-start | bytes 1179656 | tf_op jit(solution)/shard_map/ppermute | solution.py:518
  41.0 3.9 %collective-permute-start.10 = (f32[8,768]{1,0:T(8,128)S(1)}, f32[8,768]{1,0:T(8,128)S(1)}, u32[]{:S(2)}, u32[]{:S(2)}) collective-permute-start(f32[8,768]{1,0:T(8,128)S(1)} %get-tuple-element.138.a), channel_id=1, source_target_pairs={{0,16},{8,24},{16,0},{24,8},{1,17},{9,25},{17,1},{25,9},{2,18},{10... | collective-permute-start | bytes 73736 | tf_op jit(solution)/shard_map/ppermute | solution.py:518
  43.1 15.5 %collective-permute-start.9 = (bf16[2,128,768]{2,1,0:T(8,128)(2,1)S(1)}, bf16[2,128,768]{2,1,0:T(8,128)(2,1)S(1)}, u32[]{:S(2)}, u32[]{:S(2)}) collective-permute-start(bf16[2,128,768]{2,1,0:T(8,128)(2,1)S(1)} %shard_map.283), channel_id=1, source_target_pairs={{0,16},{8,24},{16,0},{24,8},{1,17},{9,25},{17,1},{25,9},{2,18},{10... | collective-permute-start | bytes 1179656 | tf_op jit(solution)/shard_map/ppermute | solution.py:518
  44.9 5.2 %collective-permute-start.13 = (f32[8,768]{1,0:T(8,128)S(1)}, f32[8,768]{1,0:T(8,128)S(1)}, u32[]{:S(2)}, u32[]{:S(2)}) collective-permute-start(f32[8,768]{1,0:T(8,128)S(1)} %shard_map.286), channel_id=1, source_target_pairs={{0,3},{1,2},{2,1},{3,0},{4,7},{5,6},{6,5},{7,4},{8,11},{9,10},{10,... | collective-permute-start | bytes 73736 | tf_op jit(solution)/shard_map/ppermute | solution.py:518
  47.6 3.8 %collective-permute-start.12 = (f32[8,768]{1,0:T(8,128)S(1)}, f32[8,768]{1,0:T(8,128)S(1)}, u32[]{:S(2)}, u32[]{:S(2)}) collective-permute-start(f32[8,768]{1,0:T(8,128)S(1)} %shard_map.286), channel_id=1, source_target_pairs={{0,2},{1,3},{2,0},{3,1},{4,6},{5,7},{6,4},{7,5},{8,10},{9,11},{10,... | collective-permute-start | bytes 73736 | tf_op jit(solution)/shard_map/ppermute | solution.py:518
  48.0 3.8 %collective-permute-start.11 = (f32[8,768]{1,0:T(8,128)S(1)}, f32[8,768]{1,0:T(8,128)S(1)}, u32[]{:S(2)}, u32[]{:S(2)}) collective-permute-start(f32[8,768]{1,0:T(8,128)S(1)} %shard_map.286), channel_id=1, source_target_pairs={{0,1},{1,0},{2,3},{3,2},{4,5},{5,4},{6,7},{7,6},{8,9},{9,8},{10,11... | collective-permute-start | bytes 73736 | tf_op jit(solution)/shard_map/ppermute | solution.py:518
  48.4 10.2 %collective-permute-start.8 = (bf16[1,128,768]{2,1,0:T(8,128)(2,1)S(1)}, bf16[1,128,768]{2,1,0:T(8,128)(2,1)S(1)}, u32[]{:S(2)}, u32[]{:S(2)}) collective-permute-start(bf16[1,128,768]{2,1,0:T(8,128)(2,1)S(1)} %get-tuple-element.129), channel_id=1, source_target_pairs={{0,16},{8,24},{16,0},{24,8},{1,17},{9,25},{17,1},{25,9},{2,18},{10... | collective-permute-start | bytes 589832 | tf_op jit(solution)/shard_map/ppermute | solution.py:518
  51.9 1.3 %collective-permute-start.14 = (f32[8,768]{1,0:T(8,128)S(1)}, f32[8,768]{1,0:T(8,128)S(1)}, u32[]{:S(2)}, u32[]{:S(2)}) collective-permute-start(f32[8,768]{1,0:T(8,128)S(1)} %add_add_fusion), channel_id=1, source_target_pairs={{0,8},{8,0},{16,24},{24,16},{1,9},{9,1},{17,25},{25,17},{2,10},{10... | collective-permute-start | bytes 73736 | tf_op jit(solution)/shard_map/ppermute | solution.py:518
  53.1 4.7 %collective-permute-start.15 = (f32[8,768]{1,0:T(8,128)S(1)}, f32[8,768]{1,0:T(8,128)S(1)}, u32[]{:S(2)}, u32[]{:S(2)}) collective-permute-start(f32[8,768]{1,0:T(8,128)S(1)} %add.15.near_pack), channel_id=1, source_target_pairs={{0,4},{1,5},{2,6},{3,7},{4,0},{5,1},{6,2},{7,3},{8,12},{9,13},{10,... | collective-permute-start | bytes 73736 | tf_op jit(solution)/shard_map/ppermute | solution.py:518
